TPU v7x, 32 devices: a whole 2x2x4 slice. The times are simulated.
32 devices in a mesh: narrow: 4 (over x, core), wide: 8 (over z, y).
Axes of the slice: x: 2, y: 2, z: 4, core: 2. Of those that a mesh axis runs over, the one named last changes fastest.
Arguments:
- series: bfloat16 [4096, 1024], P('wide', 'narrow'), may hold values from -6 to 6
- reduction: bfloat16 [1024, 512], P('narrow'), may hold values from -0.1875 to 0.1875
- unmixing: float32 [512, 512], P('wide'), may hold values from -0.25 to 0.25
Outputs:
- sources: bfloat16 [4096, 512], P(('wide', 'narrow'))
- unmixed: float32 [512, 512], P('wide')
All inputs are finite; a program needn't handle non-finite values.
Results may differ from a plain program's by a relative error of at most 0.0063.
Values may be sent and summed in bfloat16 or wider, within the bound.
No kernel may reach another device: no remote copies, remote signals or barrier semaphores. Data moves between devices by JAX's collectives and lax.ppermute only.
A program may use at most 64 MiB of HBM per device.

v0:
```python
import jax
import jax.numpy as jnp
from jax import lax
from jax.sharding import PartitionSpec as P

ITERS = 2


def transposed(left, right):
    return lax.dot_general(
        left, right, (((1,), (1,)), ((), ())), preferred_element_type=jnp.float32
    )


def moment_of(reduced, weights):
    activity = transposed(reduced, weights.astype(jnp.bfloat16))
    squashed = jnp.tanh(activity).astype(jnp.bfloat16)
    flat = activity.astype(jnp.bfloat16)
    return lax.dot_general(
        squashed, flat, (((0,), (0,)), ((), ())), preferred_element_type=jnp.float32
    )


def shards(series, reduction, unmixing):
    narrow_count = lax.axis_size("narrow")
    partial_sum = jnp.dot(series, reduction, preferred_element_type=jnp.float32)
    scores = lax.psum_scatter(partial_sum, "narrow", scatter_dimension=0, tiled=True)
    reduced = scores.astype(jnp.bfloat16)
    gray_total = reduced.shape[0] * narrow_count * lax.axis_size("wide")
    own_rows = unmixing.shape[0]
    comps = unmixing.shape[1]
    first_row = lax.axis_index("wide") * own_rows
    scale_top = 0.25 * jnp.sqrt(jnp.float32(comps))
    eye_full = jnp.eye(comps, dtype=jnp.float32)
    weights = lax.all_gather(unmixing, "wide", axis=0, tiled=True)
    for step in range(ITERS):
        moment = lax.psum(moment_of(reduced, weights), ("narrow", "wide"))
        gradient = eye_full - moment / gray_total
        size_now = jnp.sqrt(jnp.sum(gradient * gradient))
        rate = scale_top / jnp.maximum(size_now, 1.0)
        weights = weights + rate * jnp.dot(gradient, weights, precision=lax.Precision.HIGHEST)
    rows_now = lax.dynamic_slice_in_dim(weights, first_row, own_rows, 0)
    final_weights = weights.astype(jnp.bfloat16)
    sources = transposed(reduced, final_weights).astype(jnp.bfloat16)
    return (sources, rows_now)


def solution(mesh):
    return jax.shard_map(
        shards,
        mesh=mesh,
        in_specs=(P("wide", "narrow"), P("narrow", None), P("wide", None)),
        out_specs=(P(("wide", "narrow"), None), P("wide", None)),
        check_vma=False,
    )
```

profile of v0, /device:TPU:0, one launch (start us, length us, event | category | flops | bytes accessed | tf_op | source)
XLA Modules:
  0.0 337.9 jit_solution(11952598159011840324)
XLA Ops:
  8.0 0.0 copy-start
  8.0 0.0 all-gather.2.cloned.1.call-start
  8.1 0.7 all-gather.2.cloned.1.call-update
  8.7 0.0 reduce-scatter.2.cloned.1.call-start
  8.8 0.2 copy-done
  9.0 2.3 fusion.18
  11.2 0.0 reduce-scatter.2.cloned.1.call-update
  11.2 0.0 all-reduce.3.cloned.1.call-start
  11.3 42.6 %all-gather.2.cloned.1.call-done = f32[512,512]{1,0:T(8,128)} async-done(((f32[64,512]{1,0:T(8,128)}), f32[512,512]{1,0:T(8,128)}) %all-gather.2.cloned.1.call-update) | async-done | bytes 1048592 | tf_op jit(solution)/shard_map/all_gather | solution.py:35
  53.9 0.0 reduce-scatter.2.cloned.1.call-done
  53.9 1.6 fusion.7
  55.5 1.3 fusion.9
  56.8 0.0 copy-start.1
  56.8 0.0 all-reduce.3.cloned.1.call-update
  56.8 0.0 all-reduce.5.cloned.1.call-start
  56.9 131.6 %all-reduce.3.cloned.1.call-done = f32[512,512]{1,0:T(8,128)} async-done(((f32[512,512]{1,0:T(8,128)}), f32[512,512]{1,0:T(8,128)}) %all-reduce.3.cloned.1.call-update) | async-done | bytes 1048592 | tf_op jit(solution)/shard_map/psum | solution.py:37
  188.5 0.0 copy-start.3
  188.5 2.2 multiply_reduce_fusion.1
  191.4 0.0 copy-done.1
  191.4 0.0 copy-done.3
  191.4 0.0 copy-start.4
  191.4 1.9 fusion.1
  193.4 0.0 copy-done.4
  193.4 0.3 fusion.3
  193.7 1.3 fusion.10
  195.0 0.0 all-reduce.5.cloned.1.call-update
  195.1 128.9 %all-reduce.5.cloned.1.call-done = f32[512,512]{1,0:T(8,128)} async-done(((f32[512,512]{1,0:T(8,128)}), f32[512,512]{1,0:T(8,128)}) %all-reduce.5.cloned.1.call-update) | async-done | bytes 1048592 | tf_op jit(solution)/shard_map/psum | solution.py:37
  324.0 0.0 copy-start.2
  324.0 2.2 multiply_reduce_fusion
  326.9 0.0 copy-done.2
  326.9 1.9 fusion
  328.8 0.0 copy-start.5
  328.8 0.7 constant_dynamic-slice_fusion
  329.5 0.3 copy-done.5
  329.8 1.0 convolution_convert_fusion
Async XLA Ops:
  8.0 1.0 copy-start
  8.0 45.8 %all-gather.2.cloned.1.call-start = ((), (), s32[]{:S(2)}) async-start(), calls=%async_computation.2 | async-start | bytes 1179648 | tf_op jit(solution)/shard_map/all_gather | solution.py:35
  8.7 45.1 %reduce-scatter.2.cloned.1.call-start = ((), (), s32[]{:S(2)}) async-start(), calls=%async_computation.1 | async-start | bytes 1310720 | tf_op jit(solution)/shard_map/reduce_scatter | solution.py:27
  11.2 177.2 %all-reduce.3.cloned.1.call-start = ((), (), s32[]{:S(2)}) async-start(), calls=%async_computation.3 | async-start | bytes 2097152 | tf_op jit(solution)/shard_map/psum | solution.py:37
  56.8 134.6 %copy-start.1 = (f32[512,512]{1,0:T(8,128)S(1)}, f32[512,512]{1,0:T(8,128)}, u32[]{:S(2)}) copy-start(f32[512,512]{1,0:T(8,128)} %all-gather.2.cloned.1.call-done) | copy-start | bytes 3145732
  56.8 267.1 %all-reduce.5.cloned.1.call-start = ((), (), s32[]{:S(2)}) async-start(), calls=%async_computation.4 | async-start | bytes 2097152 | tf_op jit(solution)/shard_map/psum | solution.py:37
  188.5 2.9 copy-start.3
  191.4 1.9 copy-start.4
  324.0 2.9 copy-start.2
  328.8 1.0 copy-start.5
Sparse Core Ops, SparseCore 0:
  11.0 42.8 all-gather.1
  59.9 128.5 all-reduce.2
  195.2 128.7 all-reduce.4
Sparse Core Ops, SparseCore 1:
  11.7 27.5 reduce-scatter.1
where the time goes:
time: 338 us
  waiting for transfers between devices  304 us (90%)
  between operations  16.8 us (5%)
  matrix products  11.7 us (3%)
  other arithmetic  4.38 us (1%)
    psum x2, waiting for transfers between devices, shards(): moment = lax.psum(moment_of(reduced, weights), ('narrow', 'wide'))  260 us
    all_gather x1, waiting for transfers between devices, shards(): weights = lax.all_gather(unmixing, 'wide', axis=0, tiled=True)  42.6 us
  transfers between devices with their start and end apart: 4, of which 3 were waited for; matrix products, arithmetic and copies ran while one was open for 1% of the time, Pallas kernels for 0%

commit v1 on v0

v1 whole, which is shorter than its diff:
```python
import functools

import jax
import jax.numpy as jnp
from jax import lax
from jax.experimental import pallas as pl
from jax.experimental.pallas import tpu as pltpu
from jax.sharding import PartitionSpec as P

ITERS = 2
CHUNK_BYTES = 4 * 1024 * 1024
AXES = ("narrow", "wide")
VMEM = pl.BlockSpec(memory_space=pltpu.VMEM)
SMEM = pl.BlockSpec(memory_space=pltpu.SMEM)
PARAMS = pltpu.CompilerParams(vmem_limit_bytes=48 * 1024 * 1024)


def by_rows(left, right):
    return lax.dot_general(
        left, right, (((1,), (1,)), ((), ())), preferred_element_type=jnp.float32
    )


def call(body, shapes, operands, scratch=()):
    return pl.pallas_call(
        body,
        out_shape=shapes,
        in_specs=[SMEM if item.dtype == jnp.int32 else VMEM for item in operands],
        out_specs=jax.tree.map(lambda _: VMEM, shapes),
        scratch_shapes=scratch,
        compiler_params=PARAMS,
    )(*operands)


def partial_body(order_ref, series_ref, reduction_ref, *out_refs):
    rows = out_refs[0].shape[0]
    for place, out_ref in enumerate(out_refs):
        picked = pl.ds(pl.multiple_of(order_ref[place] * rows, rows), rows)
        out_ref[...] = jnp.dot(
            series_ref[picked, :], reduction_ref[...], preferred_element_type=jnp.float32
        )


def partial_sums(order, series, reduction, rows):
    shape = jax.ShapeDtypeStruct((rows, reduction.shape[1]), jnp.float32)
    return call(partial_body, (shape,) * order.shape[0], (order, series, reduction))


def eye_of(shape):
    return (
        lax.broadcasted_iota(jnp.int32, shape, 0) == lax.broadcasted_iota(jnp.int32, shape, 1)
    ).astype(jnp.float32)


def moment_of(groups, weights):
    parts = []
    for rows in groups:
        activity = by_rows(weights, rows)
        parts.append(by_rows(jnp.tanh(activity).astype(jnp.bfloat16), activity.astype(jnp.bfloat16)))
    return (parts[0] + parts[3]) + (parts[1] + parts[2])


def groups_of(refs, places):
    rows = refs[0].shape[0]
    found = [[], [], [], []]
    for k in range(places):
        own, first, second = refs[3 * k : 3 * k + 3]
        found[0].append(own[...])
        found[1].append(first[...])
        found[2].append(second[0])
        found[3].append(second[1])
    return [jnp.concatenate(group, axis=0) if places > 1 else group[0] for group in found]


def share_of(moment, gray_total):
    return 0.5 * eye_of(moment.shape) - moment / gray_total


def stepped(own_ref, other_ref, weights_ref):
    gradient = own_ref[...].astype(jnp.float32) + other_ref[...].astype(jnp.float32)
    comps = gradient.shape[0]
    size = jnp.sqrt(jnp.sum(gradient * gradient))
    rate = 0.25 * jnp.sqrt(jnp.float32(comps)) / jnp.maximum(size, 1.0)
    weights = weights_ref[...].astype(jnp.float32)
    product = jnp.dot(
        gradient.astype(jnp.bfloat16), weights.astype(jnp.bfloat16), preferred_element_type=jnp.float32
    )
    return weights + rate * product


def round_body(places, gray_total, update, carried, last, *refs):
    refs = list(refs)
    if update:
        own_ref, other_ref = refs.pop(0), refs.pop(0)
    weights_ref = refs.pop(0)
    total_ref = refs.pop(0) if carried else None
    if update:
        weights = stepped(own_ref, other_ref, weights_ref)
        refs[-2][...] = weights
    else:
        weights = weights_ref[...]
    moment = moment_of(groups_of(refs, places), weights.astype(jnp.bfloat16))
    if carried:
        moment = moment + total_ref[...]
    refs[-1][...] = share_of(moment, gray_total).astype(jnp.bfloat16) if last else moment


def last_body(place_ref, own_ref, other_ref, weights_ref, reduced_ref, unmixing_ref, sources_ref, rows_ref, held_ref):
    weights = stepped(own_ref, other_ref, weights_ref)
    held_ref[...] = weights
    sources_ref[...] = by_rows(reduced_ref[...], weights.astype(jnp.bfloat16)).astype(jnp.bfloat16)
    rows = rows_ref.shape[0]
    start = unmixing_ref[...]
    rows_ref[...] = held_ref[pl.ds(pl.multiple_of(place_ref[0] * rows, rows), rows), :] + (
        start - start.astype(jnp.bfloat16).astype(jnp.float32)
    )


def shards(narrow_count, wide_count, series, reduction, unmixing):
    narrow, wide = lax.axis_index("narrow"), lax.axis_index("wide")
    core = narrow % 2
    comps = reduction.shape[1]
    rows = series.shape[0] // narrow_count
    gray_total = series.shape[0] * wide_count

    def over(value, partner):
        pairs = []
        for n in range(narrow_count):
            for w in range(wide_count):
                to = partner(n, w)
                pairs.append((n * wide_count + w, to[0] * wide_count + to[1]))
        return lax.ppermute(value, AXES, pairs)

    def core_swap(value):
        return over(value, lambda n, w: (n ^ 1, w))

    def x_swap(value):
        return over(value, lambda n, w: (n ^ 2, w))

    def line_swap(value, k):
        return over(value, lambda n, w: (n, w ^ (2 * k)))

    def plane_one(value):
        return over(value, lambda n, w: (n, w ^ 1) if n % 2 else (n ^ 2, w))

    def plane_two(value):
        return over(value, lambda n, w: (n ^ 2, w) if n % 2 else (n, w ^ 1))

    own_rows = unmixing.shape[0]
    half = own_rows // 2
    mine = lax.dynamic_slice_in_dim(unmixing, core * half, half, 0).astype(jnp.bfloat16)
    gathered = lax.all_to_all(
        jnp.broadcast_to(mine[None], (wide_count, half, comps)), "wide", 0, 0
    )
    others = core_swap(gathered)
    low, high = jnp.where(core == 0, gathered, others), jnp.where(core == 0, others, gathered)
    weights = jnp.stack([low, high], axis=1).reshape(comps, comps)

    order = jnp.stack([narrow ^ 3, narrow ^ 1, narrow ^ 2, narrow]).astype(jnp.int32)
    send_far, send_near, keep_far, keep_near = partial_sums(order, series, reduction, rows)
    far = (keep_far + core_swap(send_far)).astype(jnp.bfloat16)
    near = keep_near + core_swap(send_near)
    own = (near + x_swap(far).astype(jnp.float32)).astype(jnp.bfloat16)

    line = wide_count // 2
    blocks = [own] + [line_swap(own, k) for k in sorted(range(1, line), key=lambda k: (k ^ (k >> 1)) & 1 or 2)]
    gathered_rows = []
    for block in blocks:
        first = plane_one(block)
        second = plane_two(jnp.stack([block, first]))
        gathered_rows += [block, first, second]

    square16 = jax.ShapeDtypeStruct((comps, comps), jnp.bfloat16)
    square32 = jax.ShapeDtypeStruct((comps, comps), jnp.float32)
    at_once = max(1, CHUNK_BYTES // (3 * blocks[0].size * blocks[0].dtype.itemsize))
    starts = range(0, len(blocks), at_once)
    shared = None
    for _ in range(ITERS):
        total = None
        for begin in starts:
            chunk = gathered_rows[3 * begin : 3 * (begin + at_once)]
            update, last = shared is not None and begin == 0, begin == starts[-1]
            operands = [shared, core_swap(shared)] if update else []
            operands += [weights] if total is None else [weights, total]
            result = square16 if last else square32
            out = call(
                functools.partial(round_body, len(chunk) // 3, gray_total, update, total is not None, last),
                (square32, result) if update else (result,),
                (*operands, *chunk),
            )
            total = out[-1]
            weights = out[0] if update else weights
        shared = total
    return call(
        last_body,
        (
            jax.ShapeDtypeStruct((rows, comps), jnp.bfloat16),
            jax.ShapeDtypeStruct((own_rows, comps), jnp.float32),
        ),
        (wide[None].astype(jnp.int32), shared, core_swap(shared), weights, own, unmixing),
        (pltpu.VMEM((comps, comps), jnp.float32),),
    )


def solution(mesh):
    return jax.shard_map(
        functools.partial(shards, mesh.shape["narrow"], mesh.shape["wide"]),
        mesh=mesh,
        in_specs=(P("wide", "narrow"), P("narrow", None), P("wide", None)),
        out_specs=(P(("wide", "narrow"), None), P("wide", None)),
        check_vma=False,
    )
```

time: 338 us -> 63.1 us (0.19)
  waiting for transfers between devices: 304 us -> 27 us
  starting transfers between devices: 0.16 us -> 23.6 us
  between operations: 16.8 us -> 0.74 us
  matrix products: 11.7 us -> 0 us
  Pallas kernels: 0 us -> 8.42 us
  other arithmetic: 4.38 us -> 0.36 us
    psum x2 -> x0, waiting for transfers between devices: 260 us -> none  [shards(): moment = lax.psum(moment_of(reduced, weights), ('narrow', 'wide'))]
    all_gather x1 -> x0, waiting for transfers between devices: 42.6 us -> none  [shards(): weights = lax.all_gather(unmixing, 'wide', axis=0, tiled=True)]
    ppermute x0 -> x17, waiting for transfers between devices: none -> 24.5 us  [over(): return lax.ppermute(value, AXES, pairs)]
    ppermute x0 -> x17, starting transfers between devices: none -> 17.8 us  [over(): return lax.ppermute(value, AXES, pairs)]
    dot_general x8 -> x0, matrix products: 11.7 us -> none  [the longest x2 3.82 us: shards(): jnp.dot(gradient, weights, precision=lax.Precision.HIGHEST)]
    pallas_call x0 -> x4, Pallas kernels: none -> 8.42 us  [call(): pl.pallas_call(body, out_shape=shapes, in_specs=[SMEM if item.dtype == jn...]
    all_to_all x0 -> x1, starting transfers between devices: none -> 5.83 us  [shards(): lax.all_to_all(jnp.broadcast_to(mine[None], (wide_count, half, comps)), '...]
    reduce_sum x2 -> x0, other arithmetic: 4.38 us -> none  [shards(): size_now = jnp.sqrt(jnp.sum(gradient * gradient))]
  transfers between devices with their start and end apart: 4 -> 18, of which waited for: 3 -> 10; matrix products, arithmetic and copies ran while one was open for 1% -> 2% of each run, Pallas kernels for 0% -> 0%
where the time goes in v1:
time: 63.1 us; the launch traced here: 62.8 us
  waiting for transfers between devices  27 us (43%)
  starting transfers between devices  23.6 us (37%)
  Pallas kernels  8.42 us (13%)
  local copies, waits for them, and re-layouts  2.65 us (4%)
  between operations  0.74 us (1%)
    ppermute x17, waiting for transfers between devices, over(): return lax.ppermute(value, AXES, pairs)  24.5 us
    ppermute x17, starting transfers between devices, over(): return lax.ppermute(value, AXES, pairs)  17.8 us
    pallas_call x4, Pallas kernels, call(): pl.pallas_call(body, out_shape=shapes, in_specs=[SMEM if item.dtype == jn...  8.42 us
    all_to_all x1, starting transfers between devices, shards(): lax.all_to_all(jnp.broadcast_to(mine[None], (wide_count, half, comps)), '...  5.83 us
    all_to_all x1, waiting for transfers between devices, shards(): lax.all_to_all(jnp.broadcast_to(mine[None], (wide_count, half, comps)), '...  2.51 us
    unnamed x6, local copies, waits for them, and re-layouts  1.9 us
  transfers between devices with their start and end apart: 18, of which 10 were waited for; matrix products, arithmetic and copies ran while one was open for 2% of the time, Pallas kernels for 0%

profile of v1, /device:TPU:0, one launch (start us, length us, event | category | flops | bytes accessed | tf_op | source)
XLA Modules:
  0.0 62.8 jit_solution(2349095735433406749)
XLA Ops:
  0.6 0.1 pad_add_fusion.order_ref
  0.7 0.0 copy-start
  0.7 0.9 %copy-done = bf16[512,256]{1,0:T(8,128)(2,1)S(1)} copy-done((bf16[512,256]{1,0:T(8,128)(2,1)S(1)}, bf16[512,256]{1,0:T(8,128)(2,1)}, u32[]{:S(2)}) %copy-start) | copy-done | bytes 262168
  1.7 0.0 copy-start.1
  1.7 0.9 %copy-done.1 = bf16[256,512]{1,0:T(8,128)(2,1)S(1)} copy-done((bf16[256,512]{1,0:T(8,128)(2,1)S(1)}, bf16[256,512]{1,0:T(8,128)(2,1)}, u32[]{:S(2)}) %copy-start.1) | copy-done | bytes 262168
  2.6 0.8 %shard_map.50 = (f32[128,512]{1,0:T(8,128)S(1)}, f32[128,512]{1,0:T(8,128)S(1)}, f32[128,512]{1,0:T(8,128)S(1)}, f32[128,512]{1,0:T(8,128)S(1)}) custom-call(s32[4]{0:T(128)S(1)} %pad_add_fusion.order_ref, bf16[512,256]{1,0:T(8,128)(2,1)S(1)} %copy-done, bf16[256,512]{1,0:T(8,128)(2,1)S(1)} %copy-done.1), custom_call_target="tpu_custom_call" | custom-call | tf_op jit(solution)/shard_map/pallas_call | solution.py:25
  3.5 0.5 collective-permute-start.2
  4.0 0.1 collective-permute-start.1
  4.1 1.1 %collective-permute-done.2 = f32[128,512]{1,0:T(8,128)S(1)} collective-permute-done((f32[128,512]{1,0:T(8,128)S(1)}, f32[128,512]{1,0:T(8,128)S(1)}, u32[]{:S(2)}, u32[]{:S(2)}) %collective-permute-start.2) | collective-permute-done | bytes 262176 | tf_op jit(solution)/shard_map/ppermute | solution.py:132
  5.2 0.0 copy-start.2
  5.2 2.9 %collective-permute-start.3 = (bf16[128,512]{1,0:T(8,128)(2,1)S(1)}, bf16[128,512]{1,0:T(8,128)(2,1)S(1)}, u32[]{:S(2)}, u32[]{:S(2)}) collective-permute-start(bf16[128,512]{1,0:T(8,128)(2,1)S(1)} %add_convert_fusion.1), channel_id=1, source_target_pairs={{0,16},{1,17},{2,18},{3,19},{4,20},{5,21},{6,22},{7,23},{8,24},{9,... | collective-permute-start | bytes 393224 | tf_op jit(solution)/shard_map/ppermute | solution.py:132
  8.1 0.0 copy-done.2
  8.1 0.7 %broadcast_in_dim.10 = bf16[8,32,512]{2,1,0:T(8,128)(2,1)} broadcast(bf16[32,512]{1,0:T(8,128)(2,1)S(1)} %dynamic-slice_convert_fusion), dimensions={1,2} | broadcast | bytes 294912 | tf_op jit(solution)/shard_map/broadcast_in_dim | solution.py:153
  8.9 5.8 %all-to-all-start = ((bf16[8,32,512]{2,1,0:T(8,128)(2,1)}), bf16[8,32,512]{2,1,0:T(8,128)(2,1)S(1)}, u32[]{:S(2)}, u32[]{:S(2)}) async-start(bf16[8,32,512]{2,1,0:T(8,128)(2,1)} %broadcast_in_dim.10), calls=%async_computation | async-start | bytes 524288 | tf_op jit(solution)/shard_map/all_to_all | solution.py:152
  14.7 0.0 collective-permute-done.1
  14.7 0.0 collective-permute-done.3
  14.7 0.1 add_convert_fusion.refs_1_.refs_3_.reduced_ref
  14.8 3.9 %collective-permute-start.12 = (bf16[128,512]{1,0:T(8,128)(2,1)S(1)}, bf16[128,512]{1,0:T(8,128)(2,1)S(1)}, u32[]{:S(2)}, u32[]{:S(2)}) collective-permute-start(bf16[128,512]{1,0:T(8,128)(2,1)S(1)} %add_convert_fusion.refs_1_.refs_3_.reduced_ref), channel_id=1, source_target_pairs={{0,6},{1,7},{2,4},{3,5},{4,2},{5,3},{6,0},{7,1},{8,14},{9,15},{10,... | collective-permute-start | bytes 393224 | tf_op jit(solution)/shard_map/ppermute | solution.py:132
  18.6 0.0 collective-permute-start.9
  18.7 0.8 %collective-permute-start.4 = (bf16[128,512]{1,0:T(8,128)(2,1)S(1)}, bf16[128,512]{1,0:T(8,128)(2,1)S(1)}, u32[]{:S(2)}, u32[]{:S(2)}) collective-permute-start(bf16[128,512]{1,0:T(8,128)(2,1)S(1)} %add_convert_fusion.refs_1_.refs_3_.reduced_ref), channel_id=1, source_target_pairs={{0,16},{1,17},{2,18},{3,19},{4,20},{5,21},{6,22},{7,23},{8,9},{9,8... | collective-permute-start | bytes 393224 | tf_op jit(solution)/shard_map/ppermute | solution.py:132
  19.4 0.6 %collective-permute-start.6 = (bf16[128,512]{1,0:T(8,128)(2,1)S(1)}, bf16[128,512]{1,0:T(8,128)(2,1)S(1)}, u32[]{:S(2)}, u32[]{:S(2)}) collective-permute-start(bf16[128,512]{1,0:T(8,128)(2,1)S(1)} %add_convert_fusion.refs_1_.refs_3_.reduced_ref), channel_id=1, source_target_pairs={{0,2},{1,3},{2,0},{3,1},{4,6},{5,7},{6,4},{7,5},{8,10},{9,11},{10,... | collective-permute-start | bytes 393224 | tf_op jit(solution)/shard_map/ppermute | solution.py:132
  20.1 7.3 %collective-permute-done.12.refs_10_.refs_12_ = bf16[128,512]{1,0:T(8,128)(2,1)S(1)} collective-permute-done((bf16[128,512]{1,0:T(8,128)(2,1)S(1)}, bf16[128,512]{1,0:T(8,128)(2,1)S(1)}, u32[]{:S(2)}, u32[]{:S(2)}) %collective-permute-start.12) | collective-permute-done | bytes 131104 | tf_op jit(solution)/shard_map/ppermute | solution.py:132
  27.4 0.8 %collective-permute-start.13 = (bf16[128,512]{1,0:T(8,128)(2,1)S(1)}, bf16[128,512]{1,0:T(8,128)(2,1)S(1)}, u32[]{:S(2)}, u32[]{:S(2)}) collective-permute-start(bf16[128,512]{1,0:T(8,128)(2,1)S(1)} %collective-permute-done.12.refs_10_.refs_12_), channel_id=1, source_target_pairs={{0,16},{1,17},{2,18},{3,19},{4,20},{5,21},{6,22},{7,23},{8,9},{9,8... | collective-permute-start | bytes 393224 | tf_op jit(solution)/shard_map/ppermute | solution.py:132
  28.1 2.5 %all-to-all-done = bf16[8,32,512]{2,1,0:T(8,128)(2,1)S(1)} async-done(((bf16[8,32,512]{2,1,0:T(8,128)(2,1)}), bf16[8,32,512]{2,1,0:T(8,128)(2,1)S(1)}, u32[]{:S(2)}, u32[]{:S(2)}) %all-to-all-start) | async-done | bytes 262176 | tf_op jit(solution)/shard_map/all_to_all | solution.py:152
  30.7 0.0 collective-permute-start
  30.7 4.2 %collective-permute-done.9.refs_7_.refs_9_ = bf16[128,512]{1,0:T(8,128)(2,1)S(1)} collective-permute-done((bf16[128,512]{1,0:T(8,128)(2,1)S(1)}, bf16[128,512]{1,0:T(8,128)(2,1)S(1)}, u32[]{:S(2)}, u32[]{:S(2)}) %collective-permute-start.9) | collective-permute-done | bytes 131104 | tf_op jit(solution)/shard_map/ppermute | solution.py:132
  34.9 1.0 %collective-permute-start.10 = (bf16[128,512]{1,0:T(8,128)(2,1)S(1)}, bf16[128,512]{1,0:T(8,128)(2,1)S(1)}, u32[]{:S(2)}, u32[]{:S(2)}) collective-permute-start(bf16[128,512]{1,0:T(8,128)(2,1)S(1)} %collective-permute-done.9.refs_7_.refs_9_), channel_id=1, source_target_pairs={{0,16},{1,17},{2,18},{3,19},{4,20},{5,21},{6,22},{7,23},{8,9},{9,8... | collective-permute-start | bytes 393224 | tf_op jit(solution)/shard_map/ppermute | solution.py:132
  35.9 0.0 collective-permute-done.4.refs_2_.refs_4_
  35.9 1.5 %collective-permute-start.5 = (bf16[2,128,512]{2,1,0:T(8,128)(2,1)S(1)}, bf16[2,128,512]{2,1,0:T(8,128)(2,1)S(1)}, u32[]{:S(2)}, u32[]{:S(2)}) collective-permute-start(bf16[2,128,512]{2,1,0:T(8,128)(2,1)S(1)} %pad_maximum_fusion.1), channel_id=1, source_target_pairs={{0,1},{1,0},{2,3},{3,2},{4,5},{5,4},{6,7},{7,6},{8,24},{9,25},{10,... | collective-permute-start | bytes 786440 | tf_op jit(solution)/shard_map/ppermute | solution.py:132
  37.5 0.0 collective-permute-done.6.refs_4_.refs_6_
  37.5 1.0 %collective-permute-start.7 = (bf16[128,512]{1,0:T(8,128)(2,1)S(1)}, bf16[128,512]{1,0:T(8,128)(2,1)S(1)}, u32[]{:S(2)}, u32[]{:S(2)}) collective-permute-start(bf16[128,512]{1,0:T(8,128)(2,1)S(1)} %collective-permute-done.6.refs_4_.refs_6_), channel_id=1, source_target_pairs={{0,16},{1,17},{2,18},{3,19},{4,20},{5,21},{6,22},{7,23},{8,9},{9,8... | collective-permute-start | bytes 393224 | tf_op jit(solution)/shard_map/ppermute | solution.py:132
  38.4 0.0 collective-permute-done.13.refs_11_.refs_13_
  38.5 0.7 %collective-permute-start.14 = (bf16[2,128,512]{2,1,0:T(8,128)(2,1)S(1)}, bf16[2,128,512]{2,1,0:T(8,128)(2,1)S(1)}, u32[]{:S(2)}, u32[]{:S(2)}) collective-permute-start(bf16[2,128,512]{2,1,0:T(8,128)(2,1)S(1)} %pad_maximum_fusion.4), channel_id=1, source_target_pairs={{0,1},{1,0},{2,3},{3,2},{4,5},{5,4},{6,7},{7,6},{8,24},{9,25},{10,... | collective-permute-start | bytes 786440 | tf_op jit(solution)/shard_map/ppermute | solution.py:132
  39.1 2.1 %collective-permute-done.10.refs_8_.refs_10_ = bf16[128,512]{1,0:T(8,128)(2,1)S(1)} collective-permute-done((bf16[128,512]{1,0:T(8,128)(2,1)S(1)}, bf16[128,512]{1,0:T(8,128)(2,1)S(1)}, u32[]{:S(2)}, u32[]{:S(2)}) %collective-permute-start.10) | collective-permute-done | bytes 131104 | tf_op jit(solution)/shard_map/ppermute | solution.py:132
  41.2 1.6 %collective-permute-start.11 = (bf16[2,128,512]{2,1,0:T(8,128)(2,1)S(1)}, bf16[2,128,512]{2,1,0:T(8,128)(2,1)S(1)}, u32[]{:S(2)}, u32[]{:S(2)}) collective-permute-start(bf16[2,128,512]{2,1,0:T(8,128)(2,1)S(1)} %pad_maximum_fusion.3), channel_id=1, source_target_pairs={{0,1},{1,0},{2,3},{3,2},{4,5},{5,4},{6,7},{7,6},{8,24},{9,25},{10,... | collective-permute-start | bytes 786440 | tf_op jit(solution)/shard_map/ppermute | solution.py:132
  42.8 1.2 %collective-permute-done.7.refs_5_.refs_7_ = bf16[128,512]{1,0:T(8,128)(2,1)S(1)} collective-permute-done((bf16[128,512]{1,0:T(8,128)(2,1)S(1)}, bf16[128,512]{1,0:T(8,128)(2,1)S(1)}, u32[]{:S(2)}, u32[]{:S(2)}) %collective-permute-start.7) | collective-permute-done | bytes 131104 | tf_op jit(solution)/shard_map/ppermute | solution.py:132
  44.0 1.6 %collective-permute-start.8 = (bf16[2,128,512]{2,1,0:T(8,128)(2,1)S(1)}, bf16[2,128,512]{2,1,0:T(8,128)(2,1)S(1)}, u32[]{:S(2)}, u32[]{:S(2)}) collective-permute-start(bf16[2,128,512]{2,1,0:T(8,128)(2,1)S(1)} %pad_maximum_fusion.2), channel_id=1, source_target_pairs={{0,1},{1,0},{2,3},{3,2},{4,5},{5,4},{6,7},{7,6},{8,24},{9,25},{10,... | collective-permute-start | bytes 786440 | tf_op jit(solution)/shard_map/ppermute | solution.py:132
  45.6 0.0 collective-permute-done
  45.7 0.1 pad_maximum_fusion
  45.7 0.0 collective-permute-done.5.refs_3_.refs_5_
  45.7 0.0 collective-permute-done.14.refs_12_.refs_14_
  45.8 2.7 %collective-permute-done.11.refs_9_.refs_11_ = bf16[2,128,512]{2,1,0:T(8,128)(2,1)S(1)} collective-permute-done((bf16[2,128,512]{2,1,0:T(8,128)(2,1)S(1)}, bf16[2,128,512]{2,1,0:T(8,128)(2,1)S(1)}, u32[]{:S(2)}, u32[]{:S(2)}) %collective-permute-start.11) | collective-permute-done | bytes 262176 | tf_op jit(solution)/shard_map/ppermute | solution.py:132
  48.4 2.8 %collective-permute-done.8.refs_6_.refs_8_ = bf16[2,128,512]{2,1,0:T(8,128)(2,1)S(1)} collective-permute-done((bf16[2,128,512]{2,1,0:T(8,128)(2,1)S(1)}, bf16[2,128,512]{2,1,0:T(8,128)(2,1)S(1)}, u32[]{:S(2)}, u32[]{:S(2)}) %collective-permute-start.8) | collective-permute-done | bytes 262176 | tf_op jit(solution)/shard_map/ppermute | solution.py:132
  51.2 2.5 %shard_map.51.refs_0_ = bf16[512,512]{1,0:T(8,128)(2,1)S(1)} custom-call(bf16[512,512]{1,0:T(8,128)(2,1)S(1)} %bitcast.20, bf16[128,512]{1,0:T(8,128)(2,1)S(1)} %add_convert_fusion.refs_1_.refs_3_.reduced_ref, bf16[128,512]{1,0:T(8,128)(2,1)S(1)} %collective-permute-done.4.refs_2_.refs_4_, bf16[2,128,512]{2,1,0:T(8,128)(2,1)S(1)} %collective-permute-done.5.refs_3_.refs_5_, ...), custom_call_target="tpu_custom_call" | custom-call | tf_op jit(solution)/shard_map/pallas_call | solution.py:25
  53.8 0.4 collective-permute-start.15
  54.2 1.6 %collective-permute-done.15.refs_1_ = bf16[512,512]{1,0:T(8,128)(2,1)S(1)} collective-permute-done((bf16[512,512]{1,0:T(8,128)(2,1)S(1)}, bf16[512,512]{1,0:T(8,128)(2,1)S(1)}, u32[]{:S(2)}, u32[]{:S(2)}) %collective-permute-start.15) | collective-permute-done | bytes 524320 | tf_op jit(solution)/shard_map/ppermute | solution.py:132
  55.8 3.3 %shard_map.52 = (f32[512,512]{1,0:T(8,128)S(1)}, bf16[512,512]{1,0:T(8,128)(2,1)S(1)}) custom-call(bf16[512,512]{1,0:T(8,128)(2,1)S(1)} %shard_map.51.refs_0_, bf16[512,512]{1,0:T(8,128)(2,1)S(1)} %collective-permute-done.15.refs_1_, bf16[512,512]{1,0:T(8,128)(2,1)S(1)} %bitcast.21, bf16[128,512]{1,0:T(8,128)(2,1)S(1)} %add_convert_fusion.refs_1_.refs_3_.reduced_ref, ...), custom_call_target="tpu_custom_call" | custom-call | tf_op jit(solution)/shard_map/pallas_call | solution.py:25
  59.1 0.4 collective-permute-start.16
  59.4 1.6 %collective-permute-done.16.other_ref = bf16[512,512]{1,0:T(8,128)(2,1)S(1)} collective-permute-done((bf16[512,512]{1,0:T(8,128)(2,1)S(1)}, bf16[512,512]{1,0:T(8,128)(2,1)S(1)}, u32[]{:S(2)}, u32[]{:S(2)}) %collective-permute-start.16) | collective-permute-done | bytes 524320 | tf_op jit(solution)/shard_map/ppermute | solution.py:132
  61.0 1.7 %shard_map.53 = (bf16[128,512]{1,0:T(8,128)(2,1)}, f32[64,512]{1,0:T(8,128)}) custom-call(s32[1]{0:T(128)} %bitcast.place_ref, bf16[512,512]{1,0:T(8,128)(2,1)S(1)} %get-tuple-element.12.own_ref, bf16[512,512]{1,0:T(8,128)(2,1)S(1)} %collective-permute-done.16.other_ref, f32[512,512]{1,0:T(8,128)S(1)} %get-tuple-element.13.weights_ref, ...), custom_call_target="tpu_custom_call" | custom-call | tf_op jit(solution)/shard_map/pallas_call | solution.py:25
  (7 shorter events, 0.2 us)
Async XLA Ops:
  0.7 1.0 %copy-start = (bf16[512,256]{1,0:T(8,128)(2,1)S(1)}, bf16[512,256]{1,0:T(8,128)(2,1)}, u32[]{:S(2)}) copy-start(bf16[512,256]{1,0:T(8,128)(2,1)} %series_ref.1) | copy-start | bytes 786436
  1.7 0.9 %copy-start.1 = (bf16[256,512]{1,0:T(8,128)(2,1)S(1)}, bf16[256,512]{1,0:T(8,128)(2,1)}, u32[]{:S(2)}) copy-start(bf16[256,512]{1,0:T(8,128)(2,1)} %reduction_ref.1) | copy-start | bytes 786436
  3.5 1.7 %collective-permute-start.2 = (f32[128,512]{1,0:T(8,128)S(1)}, f32[128,512]{1,0:T(8,128)S(1)}, u32[]{:S(2)}, u32[]{:S(2)}) collective-permute-start(f32[128,512]{1,0:T(8,128)S(1)} %get-tuple-element.11), channel_id=1, source_target_pairs={{0,8},{1,9},{2,10},{3,11},{4,12},{5,13},{6,14},{7,15},{8,0},{9,1},... | collective-permute-start | bytes 786440 | tf_op jit(solution)/shard_map/ppermute | solution.py:132
  4.0 10.7 %collective-permute-start.1 = (f32[128,512]{1,0:T(8,128)S(1)}, f32[128,512]{1,0:T(8,128)S(1)}, u32[]{:S(2)}, u32[]{:S(2)}) collective-permute-start(f32[128,512]{1,0:T(8,128)S(1)} %get-tuple-element.9), channel_id=1, source_target_pairs={{0,8},{1,9},{2,10},{3,11},{4,12},{5,13},{6,14},{7,15},{8,0},{9,1},... | collective-permute-start | bytes 786440 | tf_op jit(solution)/shard_map/ppermute | solution.py:132
  5.2 3.0 %copy-start.2 = (f32[64,512]{1,0:T(8,128)S(1)}, f32[64,512]{1,0:T(8,128)}, u32[]{:S(2)}) copy-start(f32[64,512]{1,0:T(8,128)} %unmixing_ref.1) | copy-start | bytes 393220
  5.2 9.5 %collective-permute-start.3 = (bf16[128,512]{1,0:T(8,128)(2,1)S(1)}, bf16[128,512]{1,0:T(8,128)(2,1)S(1)}, u32[]{:S(2)}, u32[]{:S(2)}) collective-permute-start(bf16[128,512]{1,0:T(8,128)(2,1)S(1)} %add_convert_fusion.1), channel_id=1, source_target_pairs={{0,16},{1,17},{2,18},{3,19},{4,20},{5,21},{6,22},{7,23},{8,24},{9,... | collective-permute-start | bytes 393224 | tf_op jit(solution)/shard_map/ppermute | solution.py:132
  8.9 21.8 %all-to-all-start = ((bf16[8,32,512]{2,1,0:T(8,128)(2,1)}), bf16[8,32,512]{2,1,0:T(8,128)(2,1)S(1)}, u32[]{:S(2)}, u32[]{:S(2)}) async-start(bf16[8,32,512]{2,1,0:T(8,128)(2,1)} %broadcast_in_dim.10), calls=%async_computation | async-start | bytes 524288 | tf_op jit(solution)/shard_map/all_to_all | solution.py:152
  14.8 12.6 %collective-permute-start.12 = (bf16[128,512]{1,0:T(8,128)(2,1)S(1)}, bf16[128,512]{1,0:T(8,128)(2,1)S(1)}, u32[]{:S(2)}, u32[]{:S(2)}) collective-permute-start(bf16[128,512]{1,0:T(8,128)(2,1)S(1)} %add_convert_fusion.refs_1_.refs_3_.reduced_ref), channel_id=1, source_target_pairs={{0,6},{1,7},{2,4},{3,5},{4,2},{5,3},{6,0},{7,1},{8,14},{9,15},{10,... | collective-permute-start | bytes 393224 | tf_op jit(solution)/shard_map/ppermute | solution.py:132
  18.6 16.2 %collective-permute-start.9 = (bf16[128,512]{1,0:T(8,128)(2,1)S(1)}, bf16[128,512]{1,0:T(8,128)(2,1)S(1)}, u32[]{:S(2)}, u32[]{:S(2)}) collective-permute-start(bf16[128,512]{1,0:T(8,128)(2,1)S(1)} %add_convert_fusion.refs_1_.refs_3_.reduced_ref), channel_id=1, source_target_pairs={{0,4},{1,5},{2,6},{3,7},{4,0},{5,1},{6,2},{7,3},{8,12},{9,13},{10,... | collective-permute-start | bytes 393224 | tf_op jit(solution)/shard_map/ppermute | solution.py:132
  18.7 17.3 %collective-permute-start.4 = (bf16[128,512]{1,0:T(8,128)(2,1)S(1)}, bf16[128,512]{1,0:T(8,128)(2,1)S(1)}, u32[]{:S(2)}, u32[]{:S(2)}) collective-permute-start(bf16[128,512]{1,0:T(8,128)(2,1)S(1)} %add_convert_fusion.refs_1_.refs_3_.reduced_ref), channel_id=1, source_target_pairs={{0,16},{1,17},{2,18},{3,19},{4,20},{5,21},{6,22},{7,23},{8,9},{9,8... | collective-permute-start | bytes 393224 | tf_op jit(solution)/shard_map/ppermute | solution.py:132
  19.4 18.0 %collective-permute-start.6 = (bf16[128,512]{1,0:T(8,128)(2,1)S(1)}, bf16[128,512]{1,0:T(8,128)(2,1)S(1)}, u32[]{:S(2)}, u32[]{:S(2)}) collective-permute-start(bf16[128,512]{1,0:T(8,128)(2,1)S(1)} %add_convert_fusion.refs_1_.refs_3_.reduced_ref), channel_id=1, source_target_pairs={{0,2},{1,3},{2,0},{3,1},{4,6},{5,7},{6,4},{7,5},{8,10},{9,11},{10,... | collective-permute-start | bytes 393224 | tf_op jit(solution)/shard_map/ppermute | solution.py:132
  27.4 11.1 %collective-permute-start.13 = (bf16[128,512]{1,0:T(8,128)(2,1)S(1)}, bf16[128,512]{1,0:T(8,128)(2,1)S(1)}, u32[]{:S(2)}, u32[]{:S(2)}) collective-permute-start(bf16[128,512]{1,0:T(8,128)(2,1)S(1)} %collective-permute-done.12.refs_10_.refs_12_), channel_id=1, source_target_pairs={{0,16},{1,17},{2,18},{3,19},{4,20},{5,21},{6,22},{7,23},{8,9},{9,8... | collective-permute-start | bytes 393224 | tf_op jit(solution)/shard_map/ppermute | solution.py:132
  30.7 15.0 %collective-permute-start = (bf16[8,32,512]{2,1,0:T(8,128)(2,1)S(1)}, bf16[8,32,512]{2,1,0:T(8,128)(2,1)S(1)}, u32[]{:S(2)}, u32[]{:S(2)}) collective-permute-start(bf16[8,32,512]{2,1,0:T(8,128)(2,1)S(1)} %all-to-all-done), channel_id=1, source_target_pairs={{0,8},{1,9},{2,10},{3,11},{4,12},{5,13},{6,14},{7,15},{8,0},{9,1},... | collective-permute-start | bytes 786440 | tf_op jit(solution)/shard_map/ppermute | solution.py:132
  34.9 6.3 %collective-permute-start.10 = (bf16[128,512]{1,0:T(8,128)(2,1)S(1)}, bf16[128,512]{1,0:T(8,128)(2,1)S(1)}, u32[]{:S(2)}, u32[]{:S(2)}) collective-permute-start(bf16[128,512]{1,0:T(8,128)(2,1)S(1)} %collective-permute-done.9.refs_7_.refs_9_), channel_id=1, source_target_pairs={{0,16},{1,17},{2,18},{3,19},{4,20},{5,21},{6,22},{7,23},{8,9},{9,8... | collective-permute-start | bytes 393224 | tf_op jit(solution)/shard_map/ppermute | solution.py:132
  35.9 9.8 %collective-permute-start.5 = (bf16[2,128,512]{2,1,0:T(8,128)(2,1)S(1)}, bf16[2,128,512]{2,1,0:T(8,128)(2,1)S(1)}, u32[]{:S(2)}, u32[]{:S(2)}) collective-permute-start(bf16[2,128,512]{2,1,0:T(8,128)(2,1)S(1)} %pad_maximum_fusion.1), channel_id=1, source_target_pairs={{0,1},{1,0},{2,3},{3,2},{4,5},{5,4},{6,7},{7,6},{8,24},{9,25},{10,... | collective-permute-start | bytes 786440 | tf_op jit(solution)/shard_map/ppermute | solution.py:132
  37.5 6.5 %collective-permute-start.7 = (bf16[128,512]{1,0:T(8,128)(2,1)S(1)}, bf16[128,512]{1,0:T(8,128)(2,1)S(1)}, u32[]{:S(2)}, u32[]{:S(2)}) collective-permute-start(bf16[128,512]{1,0:T(8,128)(2,1)S(1)} %collective-permute-done.6.refs_4_.refs_6_), channel_id=1, source_target_pairs={{0,16},{1,17},{2,18},{3,19},{4,20},{5,21},{6,22},{7,23},{8,9},{9,8... | collective-permute-start | bytes 393224 | tf_op jit(solution)/shard_map/ppermute | solution.py:132
  38.5 7.3 %collective-permute-start.14 = (bf16[2,128,512]{2,1,0:T(8,128)(2,1)S(1)}, bf16[2,128,512]{2,1,0:T(8,128)(2,1)S(1)}, u32[]{:S(2)}, u32[]{:S(2)}) collective-permute-start(bf16[2,128,512]{2,1,0:T(8,128)(2,1)S(1)} %pad_maximum_fusion.4), channel_id=1, source_target_pairs={{0,1},{1,0},{2,3},{3,2},{4,5},{5,4},{6,7},{7,6},{8,24},{9,25},{10,... | collective-permute-start | bytes 786440 | tf_op jit(solution)/shard_map/ppermute | solution.py:132
  41.2 7.2 %collective-permute-start.11 = (bf16[2,128,512]{2,1,0:T(8,128)(2,1)S(1)}, bf16[2,128,512]{2,1,0:T(8,128)(2,1)S(1)}, u32[]{:S(2)}, u32[]{:S(2)}) collective-permute-start(bf16[2,128,512]{2,1,0:T(8,128)(2,1)S(1)} %pad_maximum_fusion.3), channel_id=1, source_target_pairs={{0,1},{1,0},{2,3},{3,2},{4,5},{5,4},{6,7},{7,6},{8,24},{9,25},{10,... | collective-permute-start | bytes 786440 | tf_op jit(solution)/shard_map/ppermute | solution.py:132
  44.0 7.2 %collective-permute-start.8 = (bf16[2,128,512]{2,1,0:T(8,128)(2,1)S(1)}, bf16[2,128,512]{2,1,0:T(8,128)(2,1)S(1)}, u32[]{:S(2)}, u32[]{:S(2)}) collective-permute-start(bf16[2,128,512]{2,1,0:T(8,128)(2,1)S(1)} %pad_maximum_fusion.2), channel_id=1, source_target_pairs={{0,1},{1,0},{2,3},{3,2},{4,5},{5,4},{6,7},{7,6},{8,24},{9,25},{10,... | collective-permute-start | bytes 786440 | tf_op jit(solution)/shard_map/ppermute | solution.py:132
  53.8 2.0 %collective-permute-start.15 = (bf16[512,512]{1,0:T(8,128)(2,1)S(1)}, bf16[512,512]{1,0:T(8,128)(2,1)S(1)}, u32[]{:S(2)}, u32[]{:S(2)}) collective-permute-start(bf16[512,512]{1,0:T(8,128)(2,1)S(1)} %shard_map.51.refs_0_), channel_id=1, source_target_pairs={{0,8},{1,9},{2,10},{3,11},{4,12},{5,13},{6,14},{7,15},{8,0},{9,1},... | collective-permute-start | bytes 1572872 | tf_op jit(solution)/shard_map/ppermute | solution.py:132
  59.1 2.0 %collective-permute-start.16 = (bf16[512,512]{1,0:T(8,128)(2,1)S(1)}, bf16[512,512]{1,0:T(8,128)(2,1)S(1)}, u32[]{:S(2)}, u32[]{:S(2)}) collective-permute-start(bf16[512,512]{1,0:T(8,128)(2,1)S(1)} %get-tuple-element.12.own_ref), channel_id=1, source_target_pairs={{0,8},{1,9},{2,10},{3,11},{4,12},{5,13},{6,14},{7,15},{8,0},{9,1},... | collective-permute-start | bytes 1572872 | tf_op jit(solution)/shard_map/ppermute | solution.py:132

commit v2 on v0

v2 whole, which is shorter than its diff:
```python
import functools

import jax
import jax.numpy as jnp
from jax import lax
from jax.experimental import pallas as pl
from jax.experimental.pallas import tpu as pltpu
from jax.sharding import PartitionSpec as P

ITERS = 2
AXES = ("narrow", "wide")
MIB = 1024 * 1024
CHUNK_BYTES = 4 * MIB
VMEM = pl.BlockSpec(memory_space=pltpu.VMEM)
SMEM = pl.BlockSpec(memory_space=pltpu.SMEM)
ANY = pl.BlockSpec(memory_space=pl.ANY)

AFTER = {
    "z3": ("wz1",),
    "z2": ("wz3",),
    "p3": ("p0",),
    "p2": ("p1",),
    "wy": ("p0",),
    "wc": ("p1",),
}


def after(value, *earlier):
    return lax.optimization_barrier((value, *earlier))[0] if earlier else value


def by_rows(left, right):
    return lax.dot_general(
        left, right, (((1,), (1,)), ((), ())), preferred_element_type=jnp.float32
    )


def call(body, shapes, operands, specs=None, scratch=(), limit=24 * MIB):
    return pl.pallas_call(
        body,
        out_shape=shapes,
        in_specs=specs or [SMEM if item.dtype == jnp.int32 else VMEM for item in operands],
        out_specs=jax.tree.map(lambda _: VMEM, shapes),
        scratch_shapes=scratch,
        compiler_params=pltpu.CompilerParams(vmem_limit_bytes=limit),
    )(*operands)


def partial_body(order_ref, series_ref, reduction_ref, *refs):
    out_refs, (left_ref, right_ref, sem_ref) = refs[:-3], refs[-3:]
    copies = [
        pltpu.make_async_copy(reduction_ref, right_ref, sem_ref.at[0]),
        pltpu.make_async_copy(series_ref, left_ref, sem_ref.at[1]),
    ]
    for copy in copies:
        copy.start()
    for copy in copies:
        copy.wait()
    rows = out_refs[0].shape[0]
    for place, out_ref in enumerate(out_refs):
        picked = pl.ds(pl.multiple_of(order_ref[place] * rows, rows), rows)
        out_ref[...] = jnp.dot(left_ref[picked, :], right_ref[...], preferred_element_type=jnp.float32)


def partial_sums(order, series, reduction, rows):
    shape = jax.ShapeDtypeStruct((rows, reduction.shape[1]), jnp.float32)
    return call(
        partial_body,
        (shape,) * order.shape[0],
        (order, series, reduction),
        specs=[SMEM, ANY, ANY],
        scratch=(
            pltpu.VMEM(series.shape, series.dtype),
            pltpu.VMEM(reduction.shape, reduction.dtype),
            pltpu.SemaphoreType.DMA((2,)),
        ),
        limit=52 * MIB + 7 * MIB // 10,
    )


def place_body(places_ref, mine_ref, other_ref, out_ref):
    rows = mine_ref.shape[-2]
    pieces = [ref[j, k] for ref in (mine_ref, other_ref) for j in range(ref.shape[0]) for k in range(ref.shape[1])]
    for n, piece in enumerate(pieces):
        out_ref[pl.ds(pl.multiple_of(places_ref[n] * rows, rows), rows), :] = piece


def joined(parts):
    return jnp.concatenate(parts, axis=0) if len(parts) > 1 else parts[0]


def moment_of(flag, refs, weights):
    owns, firsts = [ref[...] for ref in refs[0::3]], [ref[...] for ref in refs[1::3]]
    sides, across = [ref[0] for ref in refs[2::3]], [ref[1] for ref in refs[2::3]]
    lower = [jnp.where(flag, first, side) for first, side in zip(firsts, sides)]
    upper = [jnp.where(flag, side, first) for first, side in zip(firsts, sides)]
    moments = []
    for rows in (joined(owns + across), joined(lower + upper)):
        activity = by_rows(weights, rows)
        moments.append(by_rows(jnp.tanh(activity).astype(jnp.bfloat16), activity.astype(jnp.bfloat16)))
    return moments[0] + moments[1]


def stepped(own_ref, other_ref, weights_ref):
    gradient = own_ref[...].astype(jnp.float32) + other_ref[...].astype(jnp.float32)
    size = jnp.sqrt(jnp.sum(gradient * gradient))
    rate = 0.25 * jnp.sqrt(jnp.float32(gradient.shape[0])) / jnp.maximum(size, 1.0)
    weights = weights_ref[...].astype(jnp.float32)
    product = jnp.dot(
        gradient.astype(jnp.bfloat16), weights.astype(jnp.bfloat16), preferred_element_type=jnp.float32
    )
    return weights + rate * product


def round_body(gray_total, update, carried, last, core_ref, *refs):
    refs = list(refs)
    step_refs = [refs.pop(0) for _ in range(2)] if update else []
    weights_ref = refs.pop(0)
    total_ref = refs.pop(0) if carried else None
    out_ref = refs.pop()
    if update:
        weights = stepped(*step_refs, weights_ref)
        refs.pop()[...] = weights
    else:
        weights = weights_ref[...]
    total = moment_of(core_ref[0] == 0, refs, weights.astype(jnp.bfloat16))
    if carried:
        total = total + total_ref[...]
    if last:
        places = [lax.broadcasted_iota(jnp.int32, total.shape, axis) for axis in (0, 1)]
        total = (0.5 * (places[0] == places[1]).astype(jnp.float32) - total / gray_total).astype(jnp.bfloat16)
    out_ref[...] = total


def last_body(rounded, place_ref, own_ref, other_ref, weights_ref, reduced_ref, start_ref, sources_ref, rows_ref, held_ref):
    weights = stepped(own_ref, other_ref, weights_ref)
    held_ref[...] = weights
    sources_ref[...] = by_rows(reduced_ref[...], weights.astype(jnp.bfloat16)).astype(jnp.bfloat16)
    rows = rows_ref.shape[0]
    found = held_ref[pl.ds(pl.multiple_of(place_ref[0] * rows, rows), rows), :]
    if rounded:
        start = start_ref[...]
        found = found + (start - start.astype(jnp.bfloat16).astype(jnp.float32))
    rows_ref[...] = found


def shards(narrow_count, wide_count, series, reduction, unmixing):
    narrow, wide = lax.axis_index("narrow"), lax.axis_index("wide")
    core = narrow % 2
    comps, own_rows = reduction.shape[1], unmixing.shape[0]
    rows, half = series.shape[0] // narrow_count, own_rows // 2
    gray_total = series.shape[0] * wide_count
    offsets = sorted(range(1, wide_count // 2), key=lambda k: (k < 2, -k))
    riding = half % 16 == 0
    done = {}

    def permute(name, value, partner):
        pairs = []
        for n in range(narrow_count):
            for w in range(wide_count):
                there = partner(n, w)
                pairs.append((n * wide_count + w, there[0] * wide_count + there[1]))
        value = after(value, *(done[earlier] for earlier in AFTER.get(name, ()) if earlier in done))
        done[name] = lax.ppermute(value, AXES, pairs)
        return done[name]

    def core_swap(name, value):
        return permute(name, value, lambda n, w: (n ^ 1, w))

    def line_swap(name, value, k):
        return permute(name, value, lambda n, w: (n, w ^ (2 * k)))

    def plane_one(name, value):
        return permute(name, value, lambda n, w: (n, w ^ 1) if n % 2 else (n ^ 2, w))

    def plane_two(name, value):
        return permute(name, value, lambda n, w: (n ^ 2, w) if n % 2 else (n, w ^ 1))

    order = jnp.stack([narrow ^ 3, narrow ^ 1, narrow ^ 2, narrow]).astype(jnp.int32)
    send_far, send_near, keep_far, keep_near = partial_sums(order, series, reduction, rows)
    far = (keep_far + core_swap("cf", send_far)).astype(jnp.bfloat16)
    near = keep_near + core_swap("cn", send_near)
    arrived = permute("x", far, lambda n, w: (n ^ 2, w))
    own = (near + arrived.astype(jnp.float32)).astype(jnp.bfloat16)

    blocks = {0: own}

    def over_line(k):
        blocks[k] = line_swap(f"z{k}", own, k)

    def over_plane(k):
        first = plane_one(f"p{k}", blocks[k])
        return lambda: (blocks[k], first, plane_two(f"q{k}", jnp.stack([blocks[k], first])))

    mine = lax.dynamic_slice_in_dim(unmixing, core * half, half, 0).astype(jnp.bfloat16)
    if riding:
        along = jnp.stack([mine] + [line_swap(f"wz{k}", mine, k) for k in offsets])
    finish = {0: over_plane(0)}
    for k in offsets:
        over_line(k)
    gathered = {0: finish[0]()}
    if riding:
        paired = jnp.stack([along, permute("wy", along, lambda n, w: (n, w ^ 1))])
    early, late = [k for k in offsets if k != 2], [k for k in offsets if k == 2]
    for k in early:
        finish[k] = over_plane(k)
    if riding:
        swapped = core_swap("wc", paired)
        places = [
            (wide ^ (2 * k + j)) * 2 + by for by in (core, 1 - core) for j in range(2) for k in [0] + offsets
        ]
        weights = call(
            place_body,
            jax.ShapeDtypeStruct((comps, comps), jnp.bfloat16),
            (jnp.stack(places).astype(jnp.int32), paired, swapped),
        )
    else:
        weights = lax.all_gather(unmixing, "wide", axis=0, tiled=True)
    for k in early:
        gathered[k] = finish[k]()
    for k in late:
        gathered[k] = over_plane(k)()

    at_once = max(1, CHUNK_BYTES // (4 * own.size * own.dtype.itemsize))

    def cut(names):
        return [names[begin : begin + at_once] for begin in range(0, len(names), at_once)]

    shared = None
    core = core[None].astype(jnp.int32)
    for _ in range(ITERS):
        total = None
        chunks = cut([0] + offsets) if shared is not None else cut([0] + early) + cut(late)
        for number, chunk in enumerate(chunks):
            update, last = shared is not None and number == 0, number == len(chunks) - 1
            operands = [shared, core_swap("m", shared)] if update else []
            operands += [weights] if total is None else [weights, total]
            square = jax.ShapeDtypeStruct((comps, comps), jnp.float32)
            result = jax.ShapeDtypeStruct((comps, comps), jnp.bfloat16) if last else square
            out = call(
                functools.partial(round_body, gray_total, update, total is not None, last),
                (square, result) if update else (result,),
                (core, *operands, *(part for k in chunk for part in gathered[k])),
            )
            total = out[-1]
            weights = out[0] if update else weights
        shared = total
    return call(
        functools.partial(last_body, riding),
        (
            jax.ShapeDtypeStruct((rows, comps), jnp.bfloat16),
            jax.ShapeDtypeStruct((own_rows, comps), jnp.float32),
        ),
        (wide[None].astype(jnp.int32), shared, core_swap("m", shared), weights, own, unmixing),
        scratch=(pltpu.VMEM((comps, comps), jnp.float32),),
    )


def solution(mesh):
    return jax.shard_map(
        functools.partial(shards, mesh.shape["narrow"], mesh.shape["wide"]),
        mesh=mesh,
        in_specs=(P("wide", "narrow"), P("narrow", None), P("wide", None)),
        out_specs=(P(("wide", "narrow"), None), P("wide", None)),
        check_vma=False,
    )
```

time: 338 us -> 51.8 us (0.15)
  waiting for transfers between devices: 304 us -> 16.6 us
  starting transfers between devices: 0.16 us -> 22.9 us
  between operations: 16.8 us -> 0.79 us
  matrix products: 11.7 us -> 0 us
  Pallas kernels: 0 us -> 10.1 us
    psum x2 -> x0, waiting for transfers between devices: 260 us -> none  [shards(): moment = lax.psum(moment_of(reduced, weights), ('narrow', 'wide'))]
    all_gather x1 -> x0, waiting for transfers between devices: 42.6 us -> none  [shards(): weights = lax.all_gather(unmixing, 'wide', axis=0, tiled=True)]
    ppermute x0 -> x21, starting transfers between devices: none -> 22.9 us  [permute(): done[name] = lax.ppermute(value, AXES, pairs)]
    ppermute x0 -> x21, waiting for transfers between devices: none -> 16.6 us  [permute(): done[name] = lax.ppermute(value, AXES, pairs)]
    dot_general x8 -> x0, matrix products: 11.7 us -> none  [the longest x2 3.82 us: shards(): jnp.dot(gradient, weights, precision=lax.Precision.HIGHEST)]
    pallas_call x0 -> x6, Pallas kernels: none -> 10.1 us  [call(): pl.pallas_call(body, out_shape=shapes, in_specs=specs or [SMEM if item.dt...]
    reduce_sum x2 -> x0, other arithmetic: 4.38 us -> none  [shards(): size_now = jnp.sqrt(jnp.sum(gradient * gradient))]
  transfers between devices with their start and end apart: 4 -> 21, of which waited for: 3 -> 9; matrix products, arithmetic and copies ran while one was open for 1% -> 2% of each run, Pallas kernels for 0% -> 5%
where the time goes in v2:
time: 51.8 us; the launch traced here: 51.6 us
  starting transfers between devices  22.9 us (44%)
  waiting for transfers between devices  16.6 us (32%)
  Pallas kernels  10.1 us (19%)
  other arithmetic  1.04 us (2%)
  between operations  0.79 us (2%)
    ppermute x21, starting transfers between devices, permute(): done[name] = lax.ppermute(value, AXES, pairs)  22.9 us
    ppermute x21, waiting for transfers between devices, permute(): done[name] = lax.ppermute(value, AXES, pairs)  16.6 us
    pallas_call x6, Pallas kernels, call(): pl.pallas_call(body, out_shape=shapes, in_specs=specs or [SMEM if item.dt...  10.1 us
  transfers between devices with their start and end apart: 21, of which 9 were waited for; matrix products, arithmetic and copies ran while one was open for 2% of the time, Pallas kernels for 5%

profile of v2, /device:TPU:0, one launch (start us, length us, event | category | flops | bytes accessed | tf_op | source)
XLA Modules:
  0.0 51.6 jit_solution(2605695292441228508)
XLA Ops:
  0.6 0.1 pad_add_fusion.order_ref
  0.7 1.9 %shard_map.50 = (f32[128,512]{1,0:T(8,128)S(1)}, f32[128,512]{1,0:T(8,128)S(1)}, f32[128,512]{1,0:T(8,128)S(1)}, f32[128,512]{1,0:T(8,128)S(1)}) custom-call(s32[4]{0:T(128)S(1)} %pad_add_fusion.order_ref, bf16[512,256]{1,0:T(8,128)(2,1)} %series_ref.1, bf16[256,512]{1,0:T(8,128)(2,1)} %reduction_ref.1), custom_call_target="tpu_custom_call" | custom-call | tf_op jit(solution)/shard_map/pallas_call | solution.py:39
  2.6 0.5 %collective-permute-start.4 = (f32[128,512]{1,0:T(8,128)S(1)}, f32[128,512]{1,0:T(8,128)S(1)}, u32[]{:S(2)}, u32[]{:S(2)}) collective-permute-start(f32[128,512]{1,0:T(8,128)S(1)} %get-tuple-element.17), channel_id=1, source_target_pairs={{0,8},{1,9},{2,10},{3,11},{4,12},{5,13},{6,14},{7,15},{8,0},{9,1},... | collective-permute-start | bytes 786440 | tf_op jit(solution)/shard_map/ppermute | solution.py:164
  3.1 0.1 collective-permute-start.3
  3.2 1.1 %collective-permute-done.4 = f32[128,512]{1,0:T(8,128)S(1)} collective-permute-done((f32[128,512]{1,0:T(8,128)S(1)}, f32[128,512]{1,0:T(8,128)S(1)}, u32[]{:S(2)}, u32[]{:S(2)}) %collective-permute-start.4) | collective-permute-done | bytes 262176 | tf_op jit(solution)/shard_map/ppermute | solution.py:164
  4.3 0.0 copy-start
  4.3 2.9 %collective-permute-start.5 = (bf16[128,512]{1,0:T(8,128)(2,1)S(1)}, bf16[128,512]{1,0:T(8,128)(2,1)S(1)}, u32[]{:S(2)}, u32[]{:S(2)}) collective-permute-start(bf16[128,512]{1,0:T(8,128)(2,1)S(1)} %add_convert_fusion.1), channel_id=1, source_target_pairs={{0,16},{1,17},{2,18},{3,19},{4,20},{5,21},{6,22},{7,23},{8,24},{9,... | collective-permute-start | bytes 393224 | tf_op jit(solution)/shard_map/ppermute | solution.py:164
  7.3 0.0 copy-done
  7.3 2.7 %collective-permute-start.1 = (bf16[32,512]{1,0:T(8,128)(2,1)S(1)}, bf16[32,512]{1,0:T(8,128)(2,1)S(1)}, u32[]{:S(2)}, u32[]{:S(2)}) collective-permute-start(bf16[32,512]{1,0:T(8,128)(2,1)S(1)} %dynamic-slice_convert_fusion), channel_id=1, source_target_pairs={{0,4},{1,5},{2,6},{3,7},{4,0},{5,1},{6,2},{7,3},{8,12},{9,13},{10,... | collective-permute-start | bytes 98312 | tf_op jit(solution)/shard_map/ppermute | solution.py:164
  9.9 1.3 %collective-permute-start = (bf16[32,512]{1,0:T(8,128)(2,1)S(1)}, bf16[32,512]{1,0:T(8,128)(2,1)S(1)}, u32[]{:S(2)}, u32[]{:S(2)}) collective-permute-start(bf16[32,512]{1,0:T(8,128)(2,1)S(1)} %dynamic-slice_convert_fusion), channel_id=1, source_target_pairs={{0,6},{1,7},{2,4},{3,5},{4,2},{5,3},{6,0},{7,1},{8,14},{9,15},{10,... | collective-permute-start | bytes 98312 | tf_op jit(solution)/shard_map/ppermute | solution.py:164
  11.3 0.2 collective-permute-start.2
  11.5 0.0 collective-permute-done.3
  11.5 0.0 collective-permute-done.5
  11.5 0.1 add_convert_fusion.refs_1_.refs_3_.reduced_ref
  11.6 1.9 %collective-permute-start.8 = (bf16[128,512]{1,0:T(8,128)(2,1)S(1)}, bf16[128,512]{1,0:T(8,128)(2,1)S(1)}, u32[]{:S(2)}, u32[]{:S(2)}) collective-permute-start(bf16[128,512]{1,0:T(8,128)(2,1)S(1)} %add_convert_fusion.refs_1_.refs_3_.reduced_ref), channel_id=1, source_target_pairs={{0,2},{1,3},{2,0},{3,1},{4,6},{5,7},{6,4},{7,5},{8,10},{9,11},{10,... | collective-permute-start | bytes 393224 | tf_op jit(solution)/shard_map/ppermute | solution.py:164
  13.4 1.1 %collective-permute-start.6 = (bf16[128,512]{1,0:T(8,128)(2,1)S(1)}, bf16[128,512]{1,0:T(8,128)(2,1)S(1)}, u32[]{:S(2)}, u32[]{:S(2)}) collective-permute-start(bf16[128,512]{1,0:T(8,128)(2,1)S(1)} %add_convert_fusion.refs_1_.refs_3_.reduced_ref), channel_id=1, source_target_pairs={{0,16},{1,17},{2,18},{3,19},{4,20},{5,21},{6,22},{7,23},{8,9},{9,8... | collective-permute-start | bytes 393224 | tf_op jit(solution)/shard_map/ppermute | solution.py:164
  14.5 1.5 %collective-permute-done.2 = bf16[32,512]{1,0:T(8,128)(2,1)S(1)} collective-permute-done((bf16[32,512]{1,0:T(8,128)(2,1)S(1)}, bf16[32,512]{1,0:T(8,128)(2,1)S(1)}, u32[]{:S(2)}, u32[]{:S(2)}) %collective-permute-start.2) | collective-permute-done | bytes 32800 | tf_op jit(solution)/shard_map/ppermute | solution.py:164
  16.0 2.1 %collective-permute-start.12 = (bf16[128,512]{1,0:T(8,128)(2,1)S(1)}, bf16[128,512]{1,0:T(8,128)(2,1)S(1)}, u32[]{:S(2)}, u32[]{:S(2)}) collective-permute-start(bf16[128,512]{1,0:T(8,128)(2,1)S(1)} %add_convert_fusion.refs_1_.refs_3_.reduced_ref), channel_id=1, source_target_pairs={{0,6},{1,7},{2,4},{3,5},{4,2},{5,3},{6,0},{7,1},{8,14},{9,15},{10,... | collective-permute-start | bytes 393224 | tf_op jit(solution)/shard_map/ppermute | solution.py:164
  18.0 0.0 collective-permute-done.1
  18.0 0.0 collective-permute-done
  18.1 0.1 collective-permute-start.16
  18.2 0.0 collective-permute-done.8.refs_7_.refs_12_
  18.2 0.5 %collective-permute-start.9 = (bf16[128,512]{1,0:T(8,128)(2,1)S(1)}, bf16[128,512]{1,0:T(8,128)(2,1)S(1)}, u32[]{:S(2)}, u32[]{:S(2)}) collective-permute-start(bf16[128,512]{1,0:T(8,128)(2,1)S(1)} %collective-permute-done.8.refs_7_.refs_12_), channel_id=1, source_target_pairs={{0,16},{1,17},{2,18},{3,19},{4,20},{5,21},{6,22},{7,23},{8,9},{9,8... | collective-permute-start | bytes 393224 | tf_op jit(solution)/shard_map/ppermute | solution.py:164
  18.7 0.0 collective-permute-done.6.refs_2_.refs_4_
  18.7 1.5 %collective-permute-start.7 = (bf16[4,32,512]{2,1,0:T(8,128)(2,1)S(1)}, bf16[4,32,512]{2,1,0:T(8,128)(2,1)S(1)}, u32[]{:S(2)}, u32[]{:S(2)}) collective-permute-start(bf16[4,32,512]{2,1,0:T(8,128)(2,1)S(1)} %get-tuple-element.18), channel_id=1, source_target_pairs={{0,1},{1,0},{2,3},{3,2},{4,5},{5,4},{6,7},{7,6},{8,9},{9,8},{10,11... | collective-permute-start | bytes 393224 | tf_op jit(solution)/shard_map/ppermute | solution.py:164
  20.2 2.9 %collective-permute-done.12.refs_4_.refs_6_ = bf16[128,512]{1,0:T(8,128)(2,1)S(1)} collective-permute-done((bf16[128,512]{1,0:T(8,128)(2,1)S(1)}, bf16[128,512]{1,0:T(8,128)(2,1)S(1)}, u32[]{:S(2)}, u32[]{:S(2)}) %collective-permute-start.12) | collective-permute-done | bytes 131104 | tf_op jit(solution)/shard_map/ppermute | solution.py:164
  23.1 1.1 %collective-permute-start.13 = (bf16[128,512]{1,0:T(8,128)(2,1)S(1)}, bf16[128,512]{1,0:T(8,128)(2,1)S(1)}, u32[]{:S(2)}, u32[]{:S(2)}) collective-permute-start(bf16[128,512]{1,0:T(8,128)(2,1)S(1)} %collective-permute-done.12.refs_4_.refs_6_), channel_id=1, source_target_pairs={{0,16},{1,17},{2,18},{3,19},{4,20},{5,21},{6,22},{7,23},{8,9},{9,8... | collective-permute-start | bytes 393224 | tf_op jit(solution)/shard_map/ppermute | solution.py:164
  24.2 1.6 %collective-permute-start.11 = (bf16[2,128,512]{2,1,0:T(8,128)(2,1)S(1)}, bf16[2,128,512]{2,1,0:T(8,128)(2,1)S(1)}, u32[]{:S(2)}, u32[]{:S(2)}) collective-permute-start(bf16[2,128,512]{2,1,0:T(8,128)(2,1)S(1)} %pad_maximum_fusion.1), channel_id=1, source_target_pairs={{0,1},{1,0},{2,3},{3,2},{4,5},{5,4},{6,7},{7,6},{8,24},{9,25},{10,... | collective-permute-start | bytes 786440 | tf_op jit(solution)/shard_map/ppermute | solution.py:164
  25.8 2.4 %collective-permute-done.16.refs_2_.refs_9_ = bf16[128,512]{1,0:T(8,128)(2,1)S(1)} collective-permute-done((bf16[128,512]{1,0:T(8,128)(2,1)S(1)}, bf16[128,512]{1,0:T(8,128)(2,1)S(1)}, u32[]{:S(2)}, u32[]{:S(2)}) %collective-permute-start.16) | collective-permute-done | bytes 131104 | tf_op jit(solution)/shard_map/ppermute | solution.py:164
  28.2 0.0 collective-permute-done.9.refs_8_.refs_13_
  28.2 1.2 %collective-permute-start.17 = (bf16[128,512]{1,0:T(8,128)(2,1)S(1)}, bf16[128,512]{1,0:T(8,128)(2,1)S(1)}, u32[]{:S(2)}, u32[]{:S(2)}) collective-permute-start(bf16[128,512]{1,0:T(8,128)(2,1)S(1)} %collective-permute-done.16.refs_2_.refs_9_), channel_id=1, source_target_pairs={{0,16},{1,17},{2,18},{3,19},{4,20},{5,21},{6,22},{7,23},{8,9},{9,8... | collective-permute-start | bytes 393224 | tf_op jit(solution)/shard_map/ppermute | solution.py:164
  29.5 0.0 collective-permute-done.7
  29.5 1.0 %collective-permute-start.15 = (bf16[2,128,512]{2,1,0:T(8,128)(2,1)S(1)}, bf16[2,128,512]{2,1,0:T(8,128)(2,1)S(1)}, u32[]{:S(2)}, u32[]{:S(2)}) collective-permute-start(bf16[2,128,512]{2,1,0:T(8,128)(2,1)S(1)} %pad_maximum_fusion.3), channel_id=1, source_target_pairs={{0,1},{1,0},{2,3},{3,2},{4,5},{5,4},{6,7},{7,6},{8,24},{9,25},{10,... | collective-permute-start | bytes 786440 | tf_op jit(solution)/shard_map/ppermute | solution.py:164
  30.5 0.0 collective-permute-done.13.refs_5_.refs_7_
  30.6 1.1 %collective-permute-start.14 = (bf16[2,128,512]{2,1,0:T(8,128)(2,1)S(1)}, bf16[2,128,512]{2,1,0:T(8,128)(2,1)S(1)}, u32[]{:S(2)}, u32[]{:S(2)}) collective-permute-start(bf16[2,128,512]{2,1,0:T(8,128)(2,1)S(1)} %pad_maximum_fusion.2), channel_id=1, source_target_pairs={{0,1},{1,0},{2,3},{3,2},{4,5},{5,4},{6,7},{7,6},{8,24},{9,25},{10,... | collective-permute-start | bytes 786440 | tf_op jit(solution)/shard_map/ppermute | solution.py:164
  31.7 0.0 collective-permute-start.10
  31.7 2.8 %collective-permute-done.17.refs_3_.refs_10_ = bf16[128,512]{1,0:T(8,128)(2,1)S(1)} collective-permute-done((bf16[128,512]{1,0:T(8,128)(2,1)S(1)}, bf16[128,512]{1,0:T(8,128)(2,1)S(1)}, u32[]{:S(2)}, u32[]{:S(2)}) %collective-permute-start.17) | collective-permute-done | bytes 131104 | tf_op jit(solution)/shard_map/ppermute | solution.py:164
  34.5 0.7 %pad_maximum_fusion.4 = bf16[2,128,512]{2,1,0:T(8,128)(2,1)} fusion(bf16[1,128,512]{2,1,0:T(8,128)(2,1)S(1)} %bitcast.40, bf16[1,128,512]{2,1,0:T(8,128)(2,1)S(1)} %bitcast.39), kind=kLoop, calls=%fused_computation.4 | loop fusion | flops 131072 | bytes 524288 | tf_op jit(solution)/shard_map/stack | solution.py:193
  35.2 1.7 %collective-permute-start.18 = (bf16[2,128,512]{2,1,0:T(8,128)(2,1)}, bf16[2,128,512]{2,1,0:T(8,128)(2,1)S(1)}, u32[]{:S(2)}, u32[]{:S(2)}) collective-permute-start(bf16[2,128,512]{2,1,0:T(8,128)(2,1)} %pad_maximum_fusion.4), channel_id=1, source_target_pairs={{0,1},{1,0},{2,3},{3,2},{4,5},{5,4},{6,7},{7,6},{8,24},{9,25},{10,... | collective-permute-start | bytes 786440 | tf_op jit(solution)/shard_map/ppermute | solution.py:164
  36.9 0.1 stack.142.places_ref
  37.0 0.0 collective-permute-done.10.other_ref
  37.0 0.6 %shard_map.51.refs_0_.refs_2_ = bf16[512,512]{1,0:T(8,128)(2,1)S(1)} custom-call(s32[16]{0:T(128)S(1)} %stack.142.places_ref, bf16[2,4,32,512]{3,2,1,0:T(8,128)(2,1)S(1)} %pad_maximum_fusion.mine_ref, bf16[2,4,32,512]{3,2,1,0:T(8,128)(2,1)S(1)} %collective-permute-done.10.other_ref), custom_call_target="tpu_custom_call" | custom-call | tf_op jit(solution)/shard_map/pallas_call | solution.py:39
  37.6 0.0 collective-permute-done.11.refs_3_.refs_5_
  37.6 0.0 collective-permute-done.15.refs_9_.refs_14_
  37.6 1.1 %collective-permute-done.14.refs_6_.refs_8_ = bf16[2,128,512]{2,1,0:T(8,128)(2,1)S(1)} collective-permute-done((bf16[2,128,512]{2,1,0:T(8,128)(2,1)S(1)}, bf16[2,128,512]{2,1,0:T(8,128)(2,1)S(1)}, u32[]{:S(2)}, u32[]{:S(2)}) %collective-permute-start.14) | collective-permute-done | bytes 262176 | tf_op jit(solution)/shard_map/ppermute | solution.py:164
  38.8 1.8 %shard_map.52.refs_1_ = f32[512,512]{1,0:T(8,128)S(1)} custom-call(s32[1]{0:T(128)} %bitcast.1.core_ref, bf16[512,512]{1,0:T(8,128)(2,1)S(1)} %shard_map.51.refs_0_.refs_2_, bf16[128,512]{1,0:T(8,128)(2,1)S(1)} %add_convert_fusion.refs_1_.refs_3_.reduced_ref, bf16[128,512]{1,0:T(8,128)(2,1)S(1)} %collective-permute-done.6.refs_2_.refs_4_, ...), custom_call_target="tpu_custom_call" | custom-call | tf_op jit(solution)/shard_map/pallas_call | solution.py:39
  40.6 1.2 %collective-permute-done.18.refs_4_.refs_11_ = bf16[2,128,512]{2,1,0:T(8,128)(2,1)S(1)} collective-permute-done((bf16[2,128,512]{2,1,0:T(8,128)(2,1)}, bf16[2,128,512]{2,1,0:T(8,128)(2,1)S(1)}, u32[]{:S(2)}, u32[]{:S(2)}) %collective-permute-start.18) | collective-permute-done | bytes 262176 | tf_op jit(solution)/shard_map/ppermute | solution.py:164
  41.8 0.9 %shard_map.53.refs_0_ = bf16[512,512]{1,0:T(8,128)(2,1)S(1)} custom-call(s32[1]{0:T(128)} %bitcast.1.core_ref, bf16[512,512]{1,0:T(8,128)(2,1)S(1)} %shard_map.51.refs_0_.refs_2_, f32[512,512]{1,0:T(8,128)S(1)} %shard_map.52.refs_1_, bf16[128,512]{1,0:T(8,128)(2,1)S(1)} %collective-permute-done.16.refs_2_.refs_9_, ...), custom_call_target="tpu_custom_call" | custom-call | tf_op jit(solution)/shard_map/pallas_call | solution.py:39
  42.7 0.1 collective-permute-start.19
  42.8 1.9 %collective-permute-done.19.refs_1_ = bf16[512,512]{1,0:T(8,128)(2,1)S(1)} collective-permute-done((bf16[512,512]{1,0:T(8,128)(2,1)S(1)}, bf16[512,512]{1,0:T(8,128)(2,1)S(1)}, u32[]{:S(2)}, u32[]{:S(2)}) %collective-permute-start.19) | collective-permute-done | bytes 524320 | tf_op jit(solution)/shard_map/ppermute | solution.py:164
  44.7 3.2 %shard_map.54 = (f32[512,512]{1,0:T(8,128)S(1)}, bf16[512,512]{1,0:T(8,128)(2,1)S(1)}) custom-call(s32[1]{0:T(128)} %bitcast.1.core_ref, bf16[512,512]{1,0:T(8,128)(2,1)S(1)} %shard_map.53.refs_0_, bf16[512,512]{1,0:T(8,128)(2,1)S(1)} %collective-permute-done.19.refs_1_, bf16[512,512]{1,0:T(8,128)(2,1)S(1)} %shard_map.51.refs_0_.refs_2_, ...), custom_call_target="tpu_custom_call" | custom-call | tf_op jit(solution)/shard_map/pallas_call | solution.py:39
  47.8 0.2 collective-permute-start.20
  48.0 1.8 %collective-permute-done.20.other_ref = bf16[512,512]{1,0:T(8,128)(2,1)S(1)} collective-permute-done((bf16[512,512]{1,0:T(8,128)(2,1)S(1)}, bf16[512,512]{1,0:T(8,128)(2,1)S(1)}, u32[]{:S(2)}, u32[]{:S(2)}) %collective-permute-start.20) | collective-permute-done | bytes 524320 | tf_op jit(solution)/shard_map/ppermute | solution.py:164
  49.8 1.8 %shard_map.55 = (bf16[128,512]{1,0:T(8,128)(2,1)}, f32[64,512]{1,0:T(8,128)}) custom-call(s32[1]{0:T(128)} %bitcast.place_ref, bf16[512,512]{1,0:T(8,128)(2,1)S(1)} %get-tuple-element.24.own_ref, bf16[512,512]{1,0:T(8,128)(2,1)S(1)} %collective-permute-done.20.other_ref, f32[512,512]{1,0:T(8,128)S(1)} %get-tuple-element.25.weights_ref, ...), custom_call_target="tpu_custom_call" | custom-call | tf_op jit(solution)/shard_map/pallas_call | solution.py:39
  (8 shorter events, 0.2 us)
Async XLA Ops:
  2.6 1.7 %collective-permute-start.4 = (f32[128,512]{1,0:T(8,128)S(1)}, f32[128,512]{1,0:T(8,128)S(1)}, u32[]{:S(2)}, u32[]{:S(2)}) collective-permute-start(f32[128,512]{1,0:T(8,128)S(1)} %get-tuple-element.17), channel_id=1, source_target_pairs={{0,8},{1,9},{2,10},{3,11},{4,12},{5,13},{6,14},{7,15},{8,0},{9,1},... | collective-permute-start | bytes 786440 | tf_op jit(solution)/shard_map/ppermute | solution.py:164
  3.1 8.4 %collective-permute-start.3 = (f32[128,512]{1,0:T(8,128)S(1)}, f32[128,512]{1,0:T(8,128)S(1)}, u32[]{:S(2)}, u32[]{:S(2)}) collective-permute-start(f32[128,512]{1,0:T(8,128)S(1)} %get-tuple-element.15), channel_id=1, source_target_pairs={{0,8},{1,9},{2,10},{3,11},{4,12},{5,13},{6,14},{7,15},{8,0},{9,1},... | collective-permute-start | bytes 786440 | tf_op jit(solution)/shard_map/ppermute | solution.py:164
  4.3 3.0 %copy-start = (f32[64,512]{1,0:T(8,128)S(1)}, f32[64,512]{1,0:T(8,128)}, u32[]{:S(2)}) copy-start(f32[64,512]{1,0:T(8,128)} %start_ref.1) | copy-start | bytes 393220
  4.3 7.2 %collective-permute-start.5 = (bf16[128,512]{1,0:T(8,128)(2,1)S(1)}, bf16[128,512]{1,0:T(8,128)(2,1)S(1)}, u32[]{:S(2)}, u32[]{:S(2)}) collective-permute-start(bf16[128,512]{1,0:T(8,128)(2,1)S(1)} %add_convert_fusion.1), channel_id=1, source_target_pairs={{0,16},{1,17},{2,18},{3,19},{4,20},{5,21},{6,22},{7,23},{8,24},{9,... | collective-permute-start | bytes 393224 | tf_op jit(solution)/shard_map/ppermute | solution.py:164
  7.3 10.8 %collective-permute-start.1 = (bf16[32,512]{1,0:T(8,128)(2,1)S(1)}, bf16[32,512]{1,0:T(8,128)(2,1)S(1)}, u32[]{:S(2)}, u32[]{:S(2)}) collective-permute-start(bf16[32,512]{1,0:T(8,128)(2,1)S(1)} %dynamic-slice_convert_fusion), channel_id=1, source_target_pairs={{0,4},{1,5},{2,6},{3,7},{4,0},{5,1},{6,2},{7,3},{8,12},{9,13},{10,... | collective-permute-start | bytes 98312 | tf_op jit(solution)/shard_map/ppermute | solution.py:164
  9.9 8.1 %collective-permute-start = (bf16[32,512]{1,0:T(8,128)(2,1)S(1)}, bf16[32,512]{1,0:T(8,128)(2,1)S(1)}, u32[]{:S(2)}, u32[]{:S(2)}) collective-permute-start(bf16[32,512]{1,0:T(8,128)(2,1)S(1)} %dynamic-slice_convert_fusion), channel_id=1, source_target_pairs={{0,6},{1,7},{2,4},{3,5},{4,2},{5,3},{6,0},{7,1},{8,14},{9,15},{10,... | collective-permute-start | bytes 98312 | tf_op jit(solution)/shard_map/ppermute | solution.py:164
  11.3 4.7 %collective-permute-start.2 = (bf16[32,512]{1,0:T(8,128)(2,1)S(1)}, bf16[32,512]{1,0:T(8,128)(2,1)S(1)}, u32[]{:S(2)}, u32[]{:S(2)}) collective-permute-start(bf16[32,512]{1,0:T(8,128)(2,1)S(1)} %dynamic-slice_convert_fusion), channel_id=1, source_target_pairs={{0,2},{1,3},{2,0},{3,1},{4,6},{5,7},{6,4},{7,5},{8,10},{9,11},{10,... | collective-permute-start | bytes 98312 | tf_op jit(solution)/shard_map/ppermute | solution.py:164
  11.6 6.6 %collective-permute-start.8 = (bf16[128,512]{1,0:T(8,128)(2,1)S(1)}, bf16[128,512]{1,0:T(8,128)(2,1)S(1)}, u32[]{:S(2)}, u32[]{:S(2)}) collective-permute-start(bf16[128,512]{1,0:T(8,128)(2,1)S(1)} %add_convert_fusion.refs_1_.refs_3_.reduced_ref), channel_id=1, source_target_pairs={{0,2},{1,3},{2,0},{3,1},{4,6},{5,7},{6,4},{7,5},{8,10},{9,11},{10,... | collective-permute-start | bytes 393224 | tf_op jit(solution)/shard_map/ppermute | solution.py:164
  13.4 5.3 %collective-permute-start.6 = (bf16[128,512]{1,0:T(8,128)(2,1)S(1)}, bf16[128,512]{1,0:T(8,128)(2,1)S(1)}, u32[]{:S(2)}, u32[]{:S(2)}) collective-permute-start(bf16[128,512]{1,0:T(8,128)(2,1)S(1)} %add_convert_fusion.refs_1_.refs_3_.reduced_ref), channel_id=1, source_target_pairs={{0,16},{1,17},{2,18},{3,19},{4,20},{5,21},{6,22},{7,23},{8,9},{9,8... | collective-permute-start | bytes 393224 | tf_op jit(solution)/shard_map/ppermute | solution.py:164
  16.0 7.1 %collective-permute-start.12 = (bf16[128,512]{1,0:T(8,128)(2,1)S(1)}, bf16[128,512]{1,0:T(8,128)(2,1)S(1)}, u32[]{:S(2)}, u32[]{:S(2)}) collective-permute-start(bf16[128,512]{1,0:T(8,128)(2,1)S(1)} %add_convert_fusion.refs_1_.refs_3_.reduced_ref), channel_id=1, source_target_pairs={{0,6},{1,7},{2,4},{3,5},{4,2},{5,3},{6,0},{7,1},{8,14},{9,15},{10,... | collective-permute-start | bytes 393224 | tf_op jit(solution)/shard_map/ppermute | solution.py:164
  18.1 10.1 %collective-permute-start.16 = (bf16[128,512]{1,0:T(8,128)(2,1)S(1)}, bf16[128,512]{1,0:T(8,128)(2,1)S(1)}, u32[]{:S(2)}, u32[]{:S(2)}) collective-permute-start(bf16[128,512]{1,0:T(8,128)(2,1)S(1)} %add_convert_fusion.refs_1_.refs_3_.reduced_ref), channel_id=1, source_target_pairs={{0,4},{1,5},{2,6},{3,7},{4,0},{5,1},{6,2},{7,3},{8,12},{9,13},{10,... | collective-permute-start | bytes 393224 | tf_op jit(solution)/shard_map/ppermute | solution.py:164
  18.2 10.0 %collective-permute-start.9 = (bf16[128,512]{1,0:T(8,128)(2,1)S(1)}, bf16[128,512]{1,0:T(8,128)(2,1)S(1)}, u32[]{:S(2)}, u32[]{:S(2)}) collective-permute-start(bf16[128,512]{1,0:T(8,128)(2,1)S(1)} %collective-permute-done.8.refs_7_.refs_12_), channel_id=1, source_target_pairs={{0,16},{1,17},{2,18},{3,19},{4,20},{5,21},{6,22},{7,23},{8,9},{9,8... | collective-permute-start | bytes 393224 | tf_op jit(solution)/shard_map/ppermute | solution.py:164
  18.7 10.8 %collective-permute-start.7 = (bf16[4,32,512]{2,1,0:T(8,128)(2,1)S(1)}, bf16[4,32,512]{2,1,0:T(8,128)(2,1)S(1)}, u32[]{:S(2)}, u32[]{:S(2)}) collective-permute-start(bf16[4,32,512]{2,1,0:T(8,128)(2,1)S(1)} %get-tuple-element.18), channel_id=1, source_target_pairs={{0,1},{1,0},{2,3},{3,2},{4,5},{5,4},{6,7},{7,6},{8,9},{9,8},{10,11... | collective-permute-start | bytes 393224 | tf_op jit(solution)/shard_map/ppermute | solution.py:164
  23.1 7.5 %collective-permute-start.13 = (bf16[128,512]{1,0:T(8,128)(2,1)S(1)}, bf16[128,512]{1,0:T(8,128)(2,1)S(1)}, u32[]{:S(2)}, u32[]{:S(2)}) collective-permute-start(bf16[128,512]{1,0:T(8,128)(2,1)S(1)} %collective-permute-done.12.refs_4_.refs_6_), channel_id=1, source_target_pairs={{0,16},{1,17},{2,18},{3,19},{4,20},{5,21},{6,22},{7,23},{8,9},{9,8... | collective-permute-start | bytes 393224 | tf_op jit(solution)/shard_map/ppermute | solution.py:164
  24.2 13.4 %collective-permute-start.11 = (bf16[2,128,512]{2,1,0:T(8,128)(2,1)S(1)}, bf16[2,128,512]{2,1,0:T(8,128)(2,1)S(1)}, u32[]{:S(2)}, u32[]{:S(2)}) collective-permute-start(bf16[2,128,512]{2,1,0:T(8,128)(2,1)S(1)} %pad_maximum_fusion.1), channel_id=1, source_target_pairs={{0,1},{1,0},{2,3},{3,2},{4,5},{5,4},{6,7},{7,6},{8,24},{9,25},{10,... | collective-permute-start | bytes 786440 | tf_op jit(solution)/shard_map/ppermute | solution.py:164
  28.2 6.3 %collective-permute-start.17 = (bf16[128,512]{1,0:T(8,128)(2,1)S(1)}, bf16[128,512]{1,0:T(8,128)(2,1)S(1)}, u32[]{:S(2)}, u32[]{:S(2)}) collective-permute-start(bf16[128,512]{1,0:T(8,128)(2,1)S(1)} %collective-permute-done.16.refs_2_.refs_9_), channel_id=1, source_target_pairs={{0,16},{1,17},{2,18},{3,19},{4,20},{5,21},{6,22},{7,23},{8,9},{9,8... | collective-permute-start | bytes 393224 | tf_op jit(solution)/shard_map/ppermute | solution.py:164
  29.5 8.1 %collective-permute-start.15 = (bf16[2,128,512]{2,1,0:T(8,128)(2,1)S(1)}, bf16[2,128,512]{2,1,0:T(8,128)(2,1)S(1)}, u32[]{:S(2)}, u32[]{:S(2)}) collective-permute-start(bf16[2,128,512]{2,1,0:T(8,128)(2,1)S(1)} %pad_maximum_fusion.3), channel_id=1, source_target_pairs={{0,1},{1,0},{2,3},{3,2},{4,5},{5,4},{6,7},{7,6},{8,24},{9,25},{10,... | collective-permute-start | bytes 786440 | tf_op jit(solution)/shard_map/ppermute | solution.py:164
  30.6 8.2 %collective-permute-start.14 = (bf16[2,128,512]{2,1,0:T(8,128)(2,1)S(1)}, bf16[2,128,512]{2,1,0:T(8,128)(2,1)S(1)}, u32[]{:S(2)}, u32[]{:S(2)}) collective-permute-start(bf16[2,128,512]{2,1,0:T(8,128)(2,1)S(1)} %pad_maximum_fusion.2), channel_id=1, source_target_pairs={{0,1},{1,0},{2,3},{3,2},{4,5},{5,4},{6,7},{7,6},{8,24},{9,25},{10,... | collective-permute-start | bytes 786440 | tf_op jit(solution)/shard_map/ppermute | solution.py:164
  31.7 5.3 %collective-permute-start.10 = (bf16[2,4,32,512]{3,2,1,0:T(8,128)(2,1)S(1)}, bf16[2,4,32,512]{3,2,1,0:T(8,128)(2,1)S(1)}, u32[]{:S(2)}, u32[]{:S(2)}) collective-permute-start(bf16[2,4,32,512]{3,2,1,0:T(8,128)(2,1)S(1)} %pad_maximum_fusion.mine_ref), channel_id=1, source_target_pairs={{0,8},{1,9},{2,10},{3,11},{4,12},{5,13},{6,14},{7,15},{8,0},{9,1},... | collective-permute-start | bytes 786440 | tf_op jit(solution)/shard_map/ppermute | solution.py:164
  35.2 6.6 %collective-permute-start.18 = (bf16[2,128,512]{2,1,0:T(8,128)(2,1)}, bf16[2,128,512]{2,1,0:T(8,128)(2,1)S(1)}, u32[]{:S(2)}, u32[]{:S(2)}) collective-permute-start(bf16[2,128,512]{2,1,0:T(8,128)(2,1)} %pad_maximum_fusion.4), channel_id=1, source_target_pairs={{0,1},{1,0},{2,3},{3,2},{4,5},{5,4},{6,7},{7,6},{8,24},{9,25},{10,... | collective-permute-start | bytes 786440 | tf_op jit(solution)/shard_map/ppermute | solution.py:164
  42.7 2.0 %collective-permute-start.19 = (bf16[512,512]{1,0:T(8,128)(2,1)S(1)}, bf16[512,512]{1,0:T(8,128)(2,1)S(1)}, u32[]{:S(2)}, u32[]{:S(2)}) collective-permute-start(bf16[512,512]{1,0:T(8,128)(2,1)S(1)} %shard_map.53.refs_0_), channel_id=1, source_target_pairs={{0,8},{1,9},{2,10},{3,11},{4,12},{5,13},{6,14},{7,15},{8,0},{9,1},... | collective-permute-start | bytes 1572872 | tf_op jit(solution)/shard_map/ppermute | solution.py:164
  47.8 2.0 %collective-permute-start.20 = (bf16[512,512]{1,0:T(8,128)(2,1)S(1)}, bf16[512,512]{1,0:T(8,128)(2,1)S(1)}, u32[]{:S(2)}, u32[]{:S(2)}) collective-permute-start(bf16[512,512]{1,0:T(8,128)(2,1)S(1)} %get-tuple-element.24.own_ref), channel_id=1, source_target_pairs={{0,8},{1,9},{2,10},{3,11},{4,12},{5,13},{6,14},{7,15},{8,0},{9,1},... | collective-permute-start | bytes 1572872 | tf_op jit(solution)/shard_map/ppermute | solution.py:164

commit v3 on v2

--- a/solution.py
+++ b/solution.py
@@ -15,14 +15,8 @@
 SMEM = pl.BlockSpec(memory_space=pltpu.SMEM)
 ANY = pl.BlockSpec(memory_space=pl.ANY)
 
-AFTER = {
-    "z3": ("wz1",),
-    "z2": ("wz3",),
-    "p3": ("p0",),
-    "p2": ("p1",),
-    "wy": ("p0",),
-    "wc": ("p1",),
-}
+ORDER = ("cf", "cn", "x", "w2", "p0", "z3", "z2", "z1", "w1", "q0", "wy", "p3", "p1", "wc", "q1", "q3", "p2", "q2")
+AFTER = {"wy": ("p0",), "p2": ("q0", "p1"), "q2": ("q1", "wc")}
 
 
 def after(value, *earlier):
@@ -79,9 +73,10 @@
 
 
 def place_body(places_ref, mine_ref, other_ref, out_ref):
-    rows = mine_ref.shape[-2]
-    pieces = [ref[j, k] for ref in (mine_ref, other_ref) for j in range(ref.shape[0]) for k in range(ref.shape[1])]
-    for n, piece in enumerate(pieces):
+    rows, pieces = out_ref.shape[0] // places_ref.shape[0], places_ref.shape[0] // 2
+    for n in range(2 * pieces):
+        ref = mine_ref if n < pieces else other_ref
+        piece = ref[n % pieces * rows : (n % pieces + 1) * rows, :]
         out_ref[pl.ds(pl.multiple_of(places_ref[n] * rows, rows), rows), :] = piece
 
 
@@ -150,9 +145,11 @@
     comps, own_rows = reduction.shape[1], unmixing.shape[0]
     rows, half = series.shape[0] // narrow_count, own_rows // 2
     gray_total = series.shape[0] * wide_count
-    offsets = sorted(range(1, wide_count // 2), key=lambda k: (k < 2, -k))
+    line = wide_count // 2
+    offsets = sorted(range(1, line), key=lambda k: (k == 2, k < 2, -k))
+    bits = [line >> (n + 1) for n in range(line.bit_length() - 1)]
     riding = half % 16 == 0
-    done = {}
+    done, held = {}, {}
 
     def permute(name, value, partner):
         pairs = []
@@ -178,49 +175,52 @@
 
     order = jnp.stack([narrow ^ 3, narrow ^ 1, narrow ^ 2, narrow]).astype(jnp.int32)
     send_far, send_near, keep_far, keep_near = partial_sums(order, series, reduction, rows)
-    far = (keep_far + core_swap("cf", send_far)).astype(jnp.bfloat16)
-    near = keep_near + core_swap("cn", send_near)
-    arrived = permute("x", far, lambda n, w: (n ^ 2, w))
-    own = (near + arrived.astype(jnp.float32)).astype(jnp.bfloat16)
-
-    blocks = {0: own}
-
-    def over_line(k):
-        blocks[k] = line_swap(f"z{k}", own, k)
-
-    def over_plane(k):
-        first = plane_one(f"p{k}", blocks[k])
-        return lambda: (blocks[k], first, plane_two(f"q{k}", jnp.stack([blocks[k], first])))
-
-    mine = lax.dynamic_slice_in_dim(unmixing, core * half, half, 0).astype(jnp.bfloat16)
+    held["w"] = lax.dynamic_slice_in_dim(unmixing, core * half, half, 0).astype(jnp.bfloat16)
+
+    def do(name):
+        kind, k = name[0], int("0" + name[1:]) if name[1:].isdigit() else 0
+        if name == "cf":
+            held["far"] = (keep_far + core_swap(name, send_far)).astype(jnp.bfloat16)
+        elif name == "cn":
+            held["near"] = keep_near + core_swap(name, send_near)
+        elif name == "x":
+            arrived = permute(name, held["far"], lambda n, w: (n ^ 2, w))
+            held["z0"] = (held["near"] + arrived.astype(jnp.float32)).astype(jnp.bfloat16)
+        elif name == "wc":
+            held[name] = core_swap(name, held["w"])
+        elif name == "wy":
+            held["w"] = jnp.concatenate([held["w"], permute(name, held["w"], lambda n, w: (n, w ^ 1))], axis=0)
+        elif kind == "w":
+            held["w"] = jnp.concatenate([held["w"], line_swap(name, held["w"], k)], axis=0)
+        elif kind == "z":
+            held[name] = line_swap(name, held["z0"], k)
+        elif kind == "p":
+            held[name] = plane_one(name, held[f"z{k}"])
+        else:
+            held[name] = plane_two(name, jnp.stack([held[f"z{k}"], held[f"p{k}"]]))
+
+    if line == 4:
+        names = ORDER
+    else:
+        names = ["cf", "cn", "x", *(f"w{k}" for k in bits), "wy", "wc", *(f"z{k}" for k in offsets)]
+        names += [f"{kind}{k}" for k in [0] + offsets for kind in "pq"]
+    for name in names:
+        if riding or name[0] != "w":
+            do(name)
+    own = held["z0"]
+    gathered = {k: [held[f"z{k}"], held[f"p{k}"], held[f"q{k}"]] for k in [0] + offsets}
     if riding:
-        along = jnp.stack([mine] + [line_swap(f"wz{k}", mine, k) for k in offsets])
-    finish = {0: over_plane(0)}
-    for k in offsets:
-        over_line(k)
-    gathered = {0: finish[0]()}
-    if riding:
-        paired = jnp.stack([along, permute("wy", along, lambda n, w: (n, w ^ 1))])
-    early, late = [k for k in offsets if k != 2], [k for k in offsets if k == 2]
-    for k in early:
-        finish[k] = over_plane(k)
-    if riding:
-        swapped = core_swap("wc", paired)
-        places = [
-            (wide ^ (2 * k + j)) * 2 + by for by in (core, 1 - core) for j in range(2) for k in [0] + offsets
-        ]
+        origins = [0]
+        for bit in bits:
+            origins = origins + [k ^ bit for k in origins]
+        places = [(wide ^ (2 * k + j)) * 2 + by for by in (core, 1 - core) for j in range(2) for k in origins]
         weights = call(
             place_body,
             jax.ShapeDtypeStruct((comps, comps), jnp.bfloat16),
-            (jnp.stack(places).astype(jnp.int32), paired, swapped),
+            (jnp.stack(places).astype(jnp.int32), held["w"], held["wc"]),
         )
     else:
         weights = lax.all_gather(unmixing, "wide", axis=0, tiled=True)
-    for k in early:
-        gathered[k] = finish[k]()
-    for k in late:
-        gathered[k] = over_plane(k)()
-
     at_once = max(1, CHUNK_BYTES // (4 * own.size * own.dtype.itemsize))
 
     def cut(names):
@@ -230,7 +230,7 @@
     core = core[None].astype(jnp.int32)
     for _ in range(ITERS):
         total = None
-        chunks = cut([0] + offsets) if shared is not None else cut([0] + early) + cut(late)
+        chunks = cut([0] + offsets) if shared is not None else cut([0] + offsets[:-1]) + [offsets[-1:]]
         for number, chunk in enumerate(chunks):
             update, last = shared is not None and number == 0, number == len(chunks) - 1
             operands = [shared, core_swap("m", shared)] if update else []

time: 51.8 us -> 51.4 us (level)
  starting transfers between devices: 22.9 us -> 27 us
  waiting for transfers between devices: 16.6 us -> 13 us
  other arithmetic: 1.04 us -> 0.3 us
    ppermute x21 -> x20, starting transfers between devices: 22.9 us -> 27 us  [permute(): done[name] = lax.ppermute(value, AXES, pairs)]
    ppermute x21 -> x20, waiting for transfers between devices: 16.6 us -> 13 us  [permute(): done[name] = lax.ppermute(value, AXES, pairs)]
    another operation x6 -> x4, other arithmetic: 0.87 us -> 0.1 us  [do(): held[name] = plane_two(name, jnp.stack([held[f'z{k}'], held[f'p{k}']]))]
  transfers between devices with their start and end apart: 21 -> 20, of which waited for: 9 -> 8; matrix products, arithmetic and copies ran while one was open for 2% -> 1% of each run, Pallas kernels for 5% -> 5%
where the time goes in v3:
time: 51.4 us; the launch traced here: 51.2 us
  starting transfers between devices  27 us (53%)
  waiting for transfers between devices  13 us (25%)
  Pallas kernels  10.1 us (20%)
  between operations  0.77 us (1%)
    ppermute x20, starting transfers between devices, permute(): done[name] = lax.ppermute(value, AXES, pairs)  27 us
    ppermute x20, waiting for transfers between devices, permute(): done[name] = lax.ppermute(value, AXES, pairs)  13 us
    pallas_call x6, Pallas kernels, call(): pl.pallas_call(body, out_shape=shapes, in_specs=specs or [SMEM if item.dt...  10.1 us
  transfers between devices with their start and end apart: 20, of which 8 were waited for; matrix products, arithmetic and copies ran while one was open for 1% of the time, Pallas kernels for 5%

profile of v3, /device:TPU:0, one launch (start us, length us, event | category | flops | bytes accessed | tf_op | source)
XLA Modules:
  0.0 51.2 jit_solution(15344962027531571936)
XLA Ops:
  0.6 0.1 pad_add_fusion.order_ref
  0.7 1.9 %shard_map.50 = (f32[128,512]{1,0:T(8,128)S(1)}, f32[128,512]{1,0:T(8,128)S(1)}, f32[128,512]{1,0:T(8,128)S(1)}, f32[128,512]{1,0:T(8,128)S(1)}) custom-call(s32[4]{0:T(128)S(1)} %pad_add_fusion.order_ref, bf16[512,256]{1,0:T(8,128)(2,1)} %series_ref.1, bf16[256,512]{1,0:T(8,128)(2,1)} %reduction_ref.1), custom_call_target="tpu_custom_call" | custom-call | tf_op jit(solution)/shard_map/pallas_call | solution.py:33
  2.6 0.5 %collective-permute-start.3 = (f32[128,512]{1,0:T(8,128)S(1)}, f32[128,512]{1,0:T(8,128)S(1)}, u32[]{:S(2)}, u32[]{:S(2)}) collective-permute-start(f32[128,512]{1,0:T(8,128)S(1)} %get-tuple-element.14), channel_id=1, source_target_pairs={{0,8},{1,9},{2,10},{3,11},{4,12},{5,13},{6,14},{7,15},{8,0},{9,1},... | collective-permute-start | bytes 786440 | tf_op jit(solution)/shard_map/ppermute | solution.py:161
  3.1 0.1 collective-permute-start.2
  3.2 1.1 %collective-permute-done.3 = f32[128,512]{1,0:T(8,128)S(1)} collective-permute-done((f32[128,512]{1,0:T(8,128)S(1)}, f32[128,512]{1,0:T(8,128)S(1)}, u32[]{:S(2)}, u32[]{:S(2)}) %collective-permute-start.3) | collective-permute-done | bytes 262176 | tf_op jit(solution)/shard_map/ppermute | solution.py:161
  4.3 0.0 copy-start
  4.3 2.9 %collective-permute-start.4 = (bf16[128,512]{1,0:T(8,128)(2,1)S(1)}, bf16[128,512]{1,0:T(8,128)(2,1)S(1)}, u32[]{:S(2)}, u32[]{:S(2)}) collective-permute-start(bf16[128,512]{1,0:T(8,128)(2,1)S(1)} %add_convert_fusion.1), channel_id=1, source_target_pairs={{0,16},{1,17},{2,18},{3,19},{4,20},{5,21},{6,22},{7,23},{8,24},{9,... | collective-permute-start | bytes 393224 | tf_op jit(solution)/shard_map/ppermute | solution.py:161
  7.3 0.0 copy-done
  7.3 2.7 %collective-permute-start = (bf16[32,512]{1,0:T(8,128)(2,1)S(1)}, bf16[32,512]{1,0:T(8,128)(2,1)S(1)}, u32[]{:S(2)}, u32[]{:S(2)}) collective-permute-start(bf16[32,512]{1,0:T(8,128)(2,1)S(1)} %dynamic-slice_convert_fusion), channel_id=1, source_target_pairs={{0,4},{1,5},{2,6},{3,7},{4,0},{5,1},{6,2},{7,3},{8,12},{9,13},{10,... | collective-permute-start | bytes 98312 | tf_op jit(solution)/shard_map/ppermute | solution.py:161
  9.9 0.0 collective-permute-done.2
  9.9 1.1 %collective-permute-done.4 = bf16[128,512]{1,0:T(8,128)(2,1)S(1)} collective-permute-done((bf16[128,512]{1,0:T(8,128)(2,1)S(1)}, bf16[128,512]{1,0:T(8,128)(2,1)S(1)}, u32[]{:S(2)}, u32[]{:S(2)}) %collective-permute-start.4) | collective-permute-done | bytes 131104 | tf_op jit(solution)/shard_map/ppermute | solution.py:161
  11.1 0.1 add_convert_fusion.refs_1_.refs_3_.reduced_ref
  11.1 1.9 %collective-permute-start.12 = (bf16[128,512]{1,0:T(8,128)(2,1)S(1)}, bf16[128,512]{1,0:T(8,128)(2,1)S(1)}, u32[]{:S(2)}, u32[]{:S(2)}) collective-permute-start(bf16[128,512]{1,0:T(8,128)(2,1)S(1)} %add_convert_fusion.refs_1_.refs_3_.reduced_ref), channel_id=1, source_target_pairs={{0,2},{1,3},{2,0},{3,1},{4,6},{5,7},{6,4},{7,5},{8,10},{9,11},{10,... | collective-permute-start | bytes 393224 | tf_op jit(solution)/shard_map/ppermute | solution.py:161
  13.0 1.5 %collective-permute-start.5 = (bf16[128,512]{1,0:T(8,128)(2,1)S(1)}, bf16[128,512]{1,0:T(8,128)(2,1)S(1)}, u32[]{:S(2)}, u32[]{:S(2)}) collective-permute-start(bf16[128,512]{1,0:T(8,128)(2,1)S(1)} %add_convert_fusion.refs_1_.refs_3_.reduced_ref), channel_id=1, source_target_pairs={{0,16},{1,17},{2,18},{3,19},{4,20},{5,21},{6,22},{7,23},{8,9},{9,8... | collective-permute-start | bytes 393224 | tf_op jit(solution)/shard_map/ppermute | solution.py:161
  14.5 0.0 collective-permute-done
  14.5 0.5 %collective-permute-start.1 = (bf16[64,512]{1,0:T(8,128)(2,1)S(1)}, bf16[64,512]{1,0:T(8,128)(2,1)S(1)}, u32[]{:S(2)}, u32[]{:S(2)}) collective-permute-start(bf16[64,512]{1,0:T(8,128)(2,1)S(1)} %pad_maximum_fusion.6), channel_id=1, source_target_pairs={{0,2},{1,3},{2,0},{3,1},{4,6},{5,7},{6,4},{7,5},{8,10},{9,11},{10,... | collective-permute-start | bytes 196616 | tf_op jit(solution)/shard_map/ppermute | solution.py:161
  15.0 3.6 %collective-permute-start.9 = (bf16[128,512]{1,0:T(8,128)(2,1)S(1)}, bf16[128,512]{1,0:T(8,128)(2,1)S(1)}, u32[]{:S(2)}, u32[]{:S(2)}) collective-permute-start(bf16[128,512]{1,0:T(8,128)(2,1)S(1)} %add_convert_fusion.refs_1_.refs_3_.reduced_ref), channel_id=1, source_target_pairs={{0,6},{1,7},{2,4},{3,5},{4,2},{5,3},{6,0},{7,1},{8,14},{9,15},{10,... | collective-permute-start | bytes 393224 | tf_op jit(solution)/shard_map/ppermute | solution.py:161
  18.6 0.0 collective-permute-done.12.refs_7_.refs_9_
  18.6 0.5 %collective-permute-start.13 = (bf16[128,512]{1,0:T(8,128)(2,1)S(1)}, bf16[128,512]{1,0:T(8,128)(2,1)S(1)}, u32[]{:S(2)}, u32[]{:S(2)}) collective-permute-start(bf16[128,512]{1,0:T(8,128)(2,1)S(1)} %collective-permute-done.12.refs_7_.refs_9_), channel_id=1, source_target_pairs={{0,16},{1,17},{2,18},{3,19},{4,20},{5,21},{6,22},{7,23},{8,9},{9,8... | collective-permute-start | bytes 393224 | tf_op jit(solution)/shard_map/ppermute | solution.py:161
  19.2 0.0 collective-permute-done.5.refs_2_.refs_4_
  19.2 1.6 %collective-permute-start.8 = (bf16[2,128,512]{2,1,0:T(8,128)(2,1)S(1)}, bf16[2,128,512]{2,1,0:T(8,128)(2,1)S(1)}, u32[]{:S(2)}, u32[]{:S(2)}) collective-permute-start(bf16[2,128,512]{2,1,0:T(8,128)(2,1)S(1)} %pad_maximum_fusion.1), channel_id=1, source_target_pairs={{0,1},{1,0},{2,3},{3,2},{4,5},{5,4},{6,7},{7,6},{8,24},{9,25},{10,... | collective-permute-start | bytes 786440 | tf_op jit(solution)/shard_map/ppermute | solution.py:161
  20.8 0.0 collective-permute-done.1
  20.8 0.6 %collective-permute-start.6 = (bf16[128,512]{1,0:T(8,128)(2,1)S(1)}, bf16[128,512]{1,0:T(8,128)(2,1)S(1)}, u32[]{:S(2)}, u32[]{:S(2)}) collective-permute-start(bf16[128,512]{1,0:T(8,128)(2,1)S(1)} %pad_maximum_fusion.5), channel_id=1, source_target_pairs={{0,1},{1,0},{2,3},{3,2},{4,5},{5,4},{6,7},{7,6},{8,9},{9,8},{10,11... | collective-permute-start | bytes 393224 | tf_op jit(solution)/shard_map/ppermute | solution.py:161
  21.4 2.3 %collective-permute-start.15 = (bf16[128,512]{1,0:T(8,128)(2,1)S(1)}, bf16[128,512]{1,0:T(8,128)(2,1)S(1)}, u32[]{:S(2)}, u32[]{:S(2)}) collective-permute-start(bf16[128,512]{1,0:T(8,128)(2,1)S(1)} %add_convert_fusion.refs_1_.refs_3_.reduced_ref), channel_id=1, source_target_pairs={{0,4},{1,5},{2,6},{3,7},{4,0},{5,1},{6,2},{7,3},{8,12},{9,13},{10,... | collective-permute-start | bytes 393224 | tf_op jit(solution)/shard_map/ppermute | solution.py:161
  23.7 0.0 collective-permute-done.9.refs_4_.refs_6_
  23.7 1.3 %collective-permute-start.10 = (bf16[128,512]{1,0:T(8,128)(2,1)S(1)}, bf16[128,512]{1,0:T(8,128)(2,1)S(1)}, u32[]{:S(2)}, u32[]{:S(2)}) collective-permute-start(bf16[128,512]{1,0:T(8,128)(2,1)S(1)} %collective-permute-done.9.refs_4_.refs_6_), channel_id=1, source_target_pairs={{0,16},{1,17},{2,18},{3,19},{4,20},{5,21},{6,22},{7,23},{8,9},{9,8... | collective-permute-start | bytes 393224 | tf_op jit(solution)/shard_map/ppermute | solution.py:161
  25.0 0.0 collective-permute-done.13.refs_8_.refs_10_
  25.0 2.2 %collective-permute-start.14 = (bf16[2,128,512]{2,1,0:T(8,128)(2,1)S(1)}, bf16[2,128,512]{2,1,0:T(8,128)(2,1)S(1)}, u32[]{:S(2)}, u32[]{:S(2)}) collective-permute-start(bf16[2,128,512]{2,1,0:T(8,128)(2,1)S(1)} %pad_maximum_fusion.3), channel_id=1, source_target_pairs={{0,1},{1,0},{2,3},{3,2},{4,5},{5,4},{6,7},{7,6},{8,24},{9,25},{10,... | collective-permute-start | bytes 786440 | tf_op jit(solution)/shard_map/ppermute | solution.py:161
  27.2 1.3 %collective-permute-done.6 = bf16[128,512]{1,0:T(8,128)(2,1)S(1)} collective-permute-done((bf16[128,512]{1,0:T(8,128)(2,1)S(1)}, bf16[128,512]{1,0:T(8,128)(2,1)S(1)}, u32[]{:S(2)}, u32[]{:S(2)}) %collective-permute-start.6) | collective-permute-done | bytes 131104 | tf_op jit(solution)/shard_map/ppermute | solution.py:161
  28.5 0.1 collective-permute-start.7
  28.6 0.4 collective-permute-done.15.refs_2_.refs_12_
  29.0 0.0 collective-permute-done.8.refs_3_.refs_5_
  29.0 1.2 %collective-permute-start.16 = (bf16[128,512]{1,0:T(8,128)(2,1)S(1)}, bf16[128,512]{1,0:T(8,128)(2,1)S(1)}, u32[]{:S(2)}, u32[]{:S(2)}) collective-permute-start(bf16[128,512]{1,0:T(8,128)(2,1)S(1)} %collective-permute-done.15.refs_2_.refs_12_), channel_id=1, source_target_pairs={{0,16},{1,17},{2,18},{3,19},{4,20},{5,21},{6,22},{7,23},{8,9},{9,8... | collective-permute-start | bytes 393224 | tf_op jit(solution)/shard_map/ppermute | solution.py:161
  30.1 0.0 collective-permute-done.10.refs_5_.refs_7_
  30.2 1.6 %collective-permute-start.11 = (bf16[2,128,512]{2,1,0:T(8,128)(2,1)S(1)}, bf16[2,128,512]{2,1,0:T(8,128)(2,1)S(1)}, u32[]{:S(2)}, u32[]{:S(2)}) collective-permute-start(bf16[2,128,512]{2,1,0:T(8,128)(2,1)S(1)} %pad_maximum_fusion.2), channel_id=1, source_target_pairs={{0,1},{1,0},{2,3},{3,2},{4,5},{5,4},{6,7},{7,6},{8,24},{9,25},{10,... | collective-permute-start | bytes 786440 | tf_op jit(solution)/shard_map/ppermute | solution.py:161
  31.7 3.2 %collective-permute-done.16.refs_3_.refs_13_ = bf16[128,512]{1,0:T(8,128)(2,1)S(1)} collective-permute-done((bf16[128,512]{1,0:T(8,128)(2,1)S(1)}, bf16[128,512]{1,0:T(8,128)(2,1)S(1)}, u32[]{:S(2)}, u32[]{:S(2)}) %collective-permute-start.16) | collective-permute-done | bytes 131104 | tf_op jit(solution)/shard_map/ppermute | solution.py:161
  35.0 0.0 collective-permute-done.14.refs_9_.refs_11_
  35.0 0.0 collective-permute-done.7.other_ref
  35.0 1.7 %collective-permute-start.17 = (bf16[2,128,512]{2,1,0:T(8,128)(2,1)S(1)}, bf16[2,128,512]{2,1,0:T(8,128)(2,1)S(1)}, u32[]{:S(2)}, u32[]{:S(2)}) collective-permute-start(bf16[2,128,512]{2,1,0:T(8,128)(2,1)S(1)} %pad_maximum_fusion.4), channel_id=1, source_target_pairs={{0,1},{1,0},{2,3},{3,2},{4,5},{5,4},{6,7},{7,6},{8,24},{9,25},{10,... | collective-permute-start | bytes 786440 | tf_op jit(solution)/shard_map/ppermute | solution.py:161
  36.7 0.1 stack.118.places_ref
  36.8 0.6 %shard_map.51.refs_0_.refs_2_ = bf16[512,512]{1,0:T(8,128)(2,1)S(1)} custom-call(s32[16]{0:T(128)S(1)} %stack.118.places_ref, bf16[256,512]{1,0:T(8,128)(2,1)S(1)} %pad_maximum_fusion.mine_ref, bf16[256,512]{1,0:T(8,128)(2,1)S(1)} %collective-permute-done.7.other_ref), custom_call_target="tpu_custom_call" | custom-call | tf_op jit(solution)/shard_map/pallas_call | solution.py:33
  37.4 0.0 collective-permute-done.11.refs_6_.refs_8_
  37.4 1.8 %shard_map.52.refs_1_ = f32[512,512]{1,0:T(8,128)S(1)} custom-call(s32[1]{0:T(128)} %bitcast.1.core_ref, bf16[512,512]{1,0:T(8,128)(2,1)S(1)} %shard_map.51.refs_0_.refs_2_, bf16[128,512]{1,0:T(8,128)(2,1)S(1)} %add_convert_fusion.refs_1_.refs_3_.reduced_ref, bf16[128,512]{1,0:T(8,128)(2,1)S(1)} %collective-permute-done.5.refs_2_.refs_4_, ...), custom_call_target="tpu_custom_call" | custom-call | tf_op jit(solution)/shard_map/pallas_call | solution.py:33
  39.3 2.2 %collective-permute-done.17.refs_4_.refs_14_ = bf16[2,128,512]{2,1,0:T(8,128)(2,1)S(1)} collective-permute-done((bf16[2,128,512]{2,1,0:T(8,128)(2,1)S(1)}, bf16[2,128,512]{2,1,0:T(8,128)(2,1)S(1)}, u32[]{:S(2)}, u32[]{:S(2)}) %collective-permute-start.17) | collective-permute-done | bytes 262176 | tf_op jit(solution)/shard_map/ppermute | solution.py:161
  41.4 0.9 %shard_map.53.refs_0_ = bf16[512,512]{1,0:T(8,128)(2,1)S(1)} custom-call(s32[1]{0:T(128)} %bitcast.1.core_ref, bf16[512,512]{1,0:T(8,128)(2,1)S(1)} %shard_map.51.refs_0_.refs_2_, f32[512,512]{1,0:T(8,128)S(1)} %shard_map.52.refs_1_, bf16[128,512]{1,0:T(8,128)(2,1)S(1)} %collective-permute-done.15.refs_2_.refs_12_, ...), custom_call_target="tpu_custom_call" | custom-call | tf_op jit(solution)/shard_map/pallas_call | solution.py:33
  42.3 0.1 collective-permute-start.18
  42.4 1.9 %collective-permute-done.18.refs_1_ = bf16[512,512]{1,0:T(8,128)(2,1)S(1)} collective-permute-done((bf16[512,512]{1,0:T(8,128)(2,1)S(1)}, bf16[512,512]{1,0:T(8,128)(2,1)S(1)}, u32[]{:S(2)}, u32[]{:S(2)}) %collective-permute-start.18) | collective-permute-done | bytes 524320 | tf_op jit(solution)/shard_map/ppermute | solution.py:161
  44.3 3.2 %shard_map.54 = (f32[512,512]{1,0:T(8,128)S(1)}, bf16[512,512]{1,0:T(8,128)(2,1)S(1)}) custom-call(s32[1]{0:T(128)} %bitcast.1.core_ref, bf16[512,512]{1,0:T(8,128)(2,1)S(1)} %shard_map.53.refs_0_, bf16[512,512]{1,0:T(8,128)(2,1)S(1)} %collective-permute-done.18.refs_1_, bf16[512,512]{1,0:T(8,128)(2,1)S(1)} %shard_map.51.refs_0_.refs_2_, ...), custom_call_target="tpu_custom_call" | custom-call | tf_op jit(solution)/shard_map/pallas_call | solution.py:33
  47.5 0.2 collective-permute-start.19
  47.7 1.8 %collective-permute-done.19.other_ref = bf16[512,512]{1,0:T(8,128)(2,1)S(1)} collective-permute-done((bf16[512,512]{1,0:T(8,128)(2,1)S(1)}, bf16[512,512]{1,0:T(8,128)(2,1)S(1)}, u32[]{:S(2)}, u32[]{:S(2)}) %collective-permute-start.19) | collective-permute-done | bytes 524320 | tf_op jit(solution)/shard_map/ppermute | solution.py:161
  49.4 1.8 %shard_map.55 = (bf16[128,512]{1,0:T(8,128)(2,1)}, f32[64,512]{1,0:T(8,128)}) custom-call(s32[1]{0:T(128)} %bitcast.place_ref, bf16[512,512]{1,0:T(8,128)(2,1)S(1)} %get-tuple-element.18.own_ref, bf16[512,512]{1,0:T(8,128)(2,1)S(1)} %collective-permute-done.19.other_ref, f32[512,512]{1,0:T(8,128)S(1)} %get-tuple-element.19.weights_ref, ...), custom_call_target="tpu_custom_call" | custom-call | tf_op jit(solution)/shard_map/pallas_call | solution.py:33
  (9 shorter events, 0.2 us)
Async XLA Ops:
  2.6 1.7 %collective-permute-start.3 = (f32[128,512]{1,0:T(8,128)S(1)}, f32[128,512]{1,0:T(8,128)S(1)}, u32[]{:S(2)}, u32[]{:S(2)}) collective-permute-start(f32[128,512]{1,0:T(8,128)S(1)} %get-tuple-element.14), channel_id=1, source_target_pairs={{0,8},{1,9},{2,10},{3,11},{4,12},{5,13},{6,14},{7,15},{8,0},{9,1},... | collective-permute-start | bytes 786440 | tf_op jit(solution)/shard_map/ppermute | solution.py:161
  3.1 6.8 %collective-permute-start.2 = (f32[128,512]{1,0:T(8,128)S(1)}, f32[128,512]{1,0:T(8,128)S(1)}, u32[]{:S(2)}, u32[]{:S(2)}) collective-permute-start(f32[128,512]{1,0:T(8,128)S(1)} %get-tuple-element.12), channel_id=1, source_target_pairs={{0,8},{1,9},{2,10},{3,11},{4,12},{5,13},{6,14},{7,15},{8,0},{9,1},... | collective-permute-start | bytes 786440 | tf_op jit(solution)/shard_map/ppermute | solution.py:161
  4.3 3.0 %copy-start = (f32[64,512]{1,0:T(8,128)S(1)}, f32[64,512]{1,0:T(8,128)}, u32[]{:S(2)}) copy-start(f32[64,512]{1,0:T(8,128)} %start_ref.1) | copy-start | bytes 393220
  4.3 6.7 %collective-permute-start.4 = (bf16[128,512]{1,0:T(8,128)(2,1)S(1)}, bf16[128,512]{1,0:T(8,128)(2,1)S(1)}, u32[]{:S(2)}, u32[]{:S(2)}) collective-permute-start(bf16[128,512]{1,0:T(8,128)(2,1)S(1)} %add_convert_fusion.1), channel_id=1, source_target_pairs={{0,16},{1,17},{2,18},{3,19},{4,20},{5,21},{6,22},{7,23},{8,24},{9,... | collective-permute-start | bytes 393224 | tf_op jit(solution)/shard_map/ppermute | solution.py:161
  7.3 7.2 %collective-permute-start = (bf16[32,512]{1,0:T(8,128)(2,1)S(1)}, bf16[32,512]{1,0:T(8,128)(2,1)S(1)}, u32[]{:S(2)}, u32[]{:S(2)}) collective-permute-start(bf16[32,512]{1,0:T(8,128)(2,1)S(1)} %dynamic-slice_convert_fusion), channel_id=1, source_target_pairs={{0,4},{1,5},{2,6},{3,7},{4,0},{5,1},{6,2},{7,3},{8,12},{9,13},{10,... | collective-permute-start | bytes 98312 | tf_op jit(solution)/shard_map/ppermute | solution.py:161
  11.1 7.5 %collective-permute-start.12 = (bf16[128,512]{1,0:T(8,128)(2,1)S(1)}, bf16[128,512]{1,0:T(8,128)(2,1)S(1)}, u32[]{:S(2)}, u32[]{:S(2)}) collective-permute-start(bf16[128,512]{1,0:T(8,128)(2,1)S(1)} %add_convert_fusion.refs_1_.refs_3_.reduced_ref), channel_id=1, source_target_pairs={{0,2},{1,3},{2,0},{3,1},{4,6},{5,7},{6,4},{7,5},{8,10},{9,11},{10,... | collective-permute-start | bytes 393224 | tf_op jit(solution)/shard_map/ppermute | solution.py:161
  13.0 6.2 %collective-permute-start.5 = (bf16[128,512]{1,0:T(8,128)(2,1)S(1)}, bf16[128,512]{1,0:T(8,128)(2,1)S(1)}, u32[]{:S(2)}, u32[]{:S(2)}) collective-permute-start(bf16[128,512]{1,0:T(8,128)(2,1)S(1)} %add_convert_fusion.refs_1_.refs_3_.reduced_ref), channel_id=1, source_target_pairs={{0,16},{1,17},{2,18},{3,19},{4,20},{5,21},{6,22},{7,23},{8,9},{9,8... | collective-permute-start | bytes 393224 | tf_op jit(solution)/shard_map/ppermute | solution.py:161
  14.5 6.3 %collective-permute-start.1 = (bf16[64,512]{1,0:T(8,128)(2,1)S(1)}, bf16[64,512]{1,0:T(8,128)(2,1)S(1)}, u32[]{:S(2)}, u32[]{:S(2)}) collective-permute-start(bf16[64,512]{1,0:T(8,128)(2,1)S(1)} %pad_maximum_fusion.6), channel_id=1, source_target_pairs={{0,2},{1,3},{2,0},{3,1},{4,6},{5,7},{6,4},{7,5},{8,10},{9,11},{10,... | collective-permute-start | bytes 196616 | tf_op jit(solution)/shard_map/ppermute | solution.py:161
  15.0 8.6 %collective-permute-start.9 = (bf16[128,512]{1,0:T(8,128)(2,1)S(1)}, bf16[128,512]{1,0:T(8,128)(2,1)S(1)}, u32[]{:S(2)}, u32[]{:S(2)}) collective-permute-start(bf16[128,512]{1,0:T(8,128)(2,1)S(1)} %add_convert_fusion.refs_1_.refs_3_.reduced_ref), channel_id=1, source_target_pairs={{0,6},{1,7},{2,4},{3,5},{4,2},{5,3},{6,0},{7,1},{8,14},{9,15},{10,... | collective-permute-start | bytes 393224 | tf_op jit(solution)/shard_map/ppermute | solution.py:161
  18.6 6.4 %collective-permute-start.13 = (bf16[128,512]{1,0:T(8,128)(2,1)S(1)}, bf16[128,512]{1,0:T(8,128)(2,1)S(1)}, u32[]{:S(2)}, u32[]{:S(2)}) collective-permute-start(bf16[128,512]{1,0:T(8,128)(2,1)S(1)} %collective-permute-done.12.refs_7_.refs_9_), channel_id=1, source_target_pairs={{0,16},{1,17},{2,18},{3,19},{4,20},{5,21},{6,22},{7,23},{8,9},{9,8... | collective-permute-start | bytes 393224 | tf_op jit(solution)/shard_map/ppermute | solution.py:161
  19.2 9.8 %collective-permute-start.8 = (bf16[2,128,512]{2,1,0:T(8,128)(2,1)S(1)}, bf16[2,128,512]{2,1,0:T(8,128)(2,1)S(1)}, u32[]{:S(2)}, u32[]{:S(2)}) collective-permute-start(bf16[2,128,512]{2,1,0:T(8,128)(2,1)S(1)} %pad_maximum_fusion.1), channel_id=1, source_target_pairs={{0,1},{1,0},{2,3},{3,2},{4,5},{5,4},{6,7},{7,6},{8,24},{9,25},{10,... | collective-permute-start | bytes 786440 | tf_op jit(solution)/shard_map/ppermute | solution.py:161
  20.8 7.6 %collective-permute-start.6 = (bf16[128,512]{1,0:T(8,128)(2,1)S(1)}, bf16[128,512]{1,0:T(8,128)(2,1)S(1)}, u32[]{:S(2)}, u32[]{:S(2)}) collective-permute-start(bf16[128,512]{1,0:T(8,128)(2,1)S(1)} %pad_maximum_fusion.5), channel_id=1, source_target_pairs={{0,1},{1,0},{2,3},{3,2},{4,5},{5,4},{6,7},{7,6},{8,9},{9,8},{10,11... | collective-permute-start | bytes 393224 | tf_op jit(solution)/shard_map/ppermute | solution.py:161
  21.4 7.6 %collective-permute-start.15 = (bf16[128,512]{1,0:T(8,128)(2,1)S(1)}, bf16[128,512]{1,0:T(8,128)(2,1)S(1)}, u32[]{:S(2)}, u32[]{:S(2)}) collective-permute-start(bf16[128,512]{1,0:T(8,128)(2,1)S(1)} %add_convert_fusion.refs_1_.refs_3_.reduced_ref), channel_id=1, source_target_pairs={{0,4},{1,5},{2,6},{3,7},{4,0},{5,1},{6,2},{7,3},{8,12},{9,13},{10,... | collective-permute-start | bytes 393224 | tf_op jit(solution)/shard_map/ppermute | solution.py:161
  23.7 6.5 %collective-permute-start.10 = (bf16[128,512]{1,0:T(8,128)(2,1)S(1)}, bf16[128,512]{1,0:T(8,128)(2,1)S(1)}, u32[]{:S(2)}, u32[]{:S(2)}) collective-permute-start(bf16[128,512]{1,0:T(8,128)(2,1)S(1)} %collective-permute-done.9.refs_4_.refs_6_), channel_id=1, source_target_pairs={{0,16},{1,17},{2,18},{3,19},{4,20},{5,21},{6,22},{7,23},{8,9},{9,8... | collective-permute-start | bytes 393224 | tf_op jit(solution)/shard_map/ppermute | solution.py:161
  25.0 10.0 %collective-permute-start.14 = (bf16[2,128,512]{2,1,0:T(8,128)(2,1)S(1)}, bf16[2,128,512]{2,1,0:T(8,128)(2,1)S(1)}, u32[]{:S(2)}, u32[]{:S(2)}) collective-permute-start(bf16[2,128,512]{2,1,0:T(8,128)(2,1)S(1)} %pad_maximum_fusion.3), channel_id=1, source_target_pairs={{0,1},{1,0},{2,3},{3,2},{4,5},{5,4},{6,7},{7,6},{8,24},{9,25},{10,... | collective-permute-start | bytes 786440 | tf_op jit(solution)/shard_map/ppermute | solution.py:161
  28.5 6.5 %collective-permute-start.7 = (bf16[256,512]{1,0:T(8,128)(2,1)S(1)}, bf16[256,512]{1,0:T(8,128)(2,1)S(1)}, u32[]{:S(2)}, u32[]{:S(2)}) collective-permute-start(bf16[256,512]{1,0:T(8,128)(2,1)S(1)} %pad_maximum_fusion.mine_ref), channel_id=1, source_target_pairs={{0,8},{1,9},{2,10},{3,11},{4,12},{5,13},{6,14},{7,15},{8,0},{9,1},... | collective-permute-start | bytes 786440 | tf_op jit(solution)/shard_map/ppermute | solution.py:161
  29.0 6.0 %collective-permute-start.16 = (bf16[128,512]{1,0:T(8,128)(2,1)S(1)}, bf16[128,512]{1,0:T(8,128)(2,1)S(1)}, u32[]{:S(2)}, u32[]{:S(2)}) collective-permute-start(bf16[128,512]{1,0:T(8,128)(2,1)S(1)} %collective-permute-done.15.refs_2_.refs_12_), channel_id=1, source_target_pairs={{0,16},{1,17},{2,18},{3,19},{4,20},{5,21},{6,22},{7,23},{8,9},{9,8... | collective-permute-start | bytes 393224 | tf_op jit(solution)/shard_map/ppermute | solution.py:161
  30.2 7.2 %collective-permute-start.11 = (bf16[2,128,512]{2,1,0:T(8,128)(2,1)S(1)}, bf16[2,128,512]{2,1,0:T(8,128)(2,1)S(1)}, u32[]{:S(2)}, u32[]{:S(2)}) collective-permute-start(bf16[2,128,512]{2,1,0:T(8,128)(2,1)S(1)} %pad_maximum_fusion.2), channel_id=1, source_target_pairs={{0,1},{1,0},{2,3},{3,2},{4,5},{5,4},{6,7},{7,6},{8,24},{9,25},{10,... | collective-permute-start | bytes 786440 | tf_op jit(solution)/shard_map/ppermute | solution.py:161
  35.0 6.4 %collective-permute-start.17 = (bf16[2,128,512]{2,1,0:T(8,128)(2,1)S(1)}, bf16[2,128,512]{2,1,0:T(8,128)(2,1)S(1)}, u32[]{:S(2)}, u32[]{:S(2)}) collective-permute-start(bf16[2,128,512]{2,1,0:T(8,128)(2,1)S(1)} %pad_maximum_fusion.4), channel_id=1, source_target_pairs={{0,1},{1,0},{2,3},{3,2},{4,5},{5,4},{6,7},{7,6},{8,24},{9,25},{10,... | collective-permute-start | bytes 786440 | tf_op jit(solution)/shard_map/ppermute | solution.py:161
  42.3 2.0 %collective-permute-start.18 = (bf16[512,512]{1,0:T(8,128)(2,1)S(1)}, bf16[512,512]{1,0:T(8,128)(2,1)S(1)}, u32[]{:S(2)}, u32[]{:S(2)}) collective-permute-start(bf16[512,512]{1,0:T(8,128)(2,1)S(1)} %shard_map.53.refs_0_), channel_id=1, source_target_pairs={{0,8},{1,9},{2,10},{3,11},{4,12},{5,13},{6,14},{7,15},{8,0},{9,1},... | collective-permute-start | bytes 1572872 | tf_op jit(solution)/shard_map/ppermute | solution.py:161
  47.5 2.0 %collective-permute-start.19 = (bf16[512,512]{1,0:T(8,128)(2,1)S(1)}, bf16[512,512]{1,0:T(8,128)(2,1)S(1)}, u32[]{:S(2)}, u32[]{:S(2)}) collective-permute-start(bf16[512,512]{1,0:T(8,128)(2,1)S(1)} %get-tuple-element.18.own_ref), channel_id=1, source_target_pairs={{0,8},{1,9},{2,10},{3,11},{4,12},{5,13},{6,14},{7,15},{8,0},{9,1},... | collective-permute-start | bytes 1572872 | tf_op jit(solution)/shard_map/ppermute | solution.py:161

commit v4 on v3

--- a/solution.py
+++ b/solution.py
@@ -15,8 +15,8 @@
 SMEM = pl.BlockSpec(memory_space=pltpu.SMEM)
 ANY = pl.BlockSpec(memory_space=pl.ANY)
 
-ORDER = ("cf", "cn", "x", "w2", "p0", "z3", "z2", "z1", "w1", "q0", "wy", "p3", "p1", "wc", "q1", "q3", "p2", "q2")
-AFTER = {"wy": ("p0",), "p2": ("q0", "p1"), "q2": ("q1", "wc")}
+ORDER = ("cf", "cn", "x", "w2", "p0", "z3", "z2", "z1", "w1", "q0", "wy", "p3", "p1", "q3", "q1", "p2", "wc", "q2")
+AFTER = {"w1": ("z1",), "wy": ("z3",), "p2": ("q0", "p1"), "wc": ("p2",), "q2": ("q1",)}
 
 
 def after(value, *earlier):

time: 51.4 us -> 50.8 us (0.988)
  starting transfers between devices: 27 us -> 24.4 us
  waiting for transfers between devices: 13 us -> 15 us
    ppermute x20, starting transfers between devices: 27 us -> 24.4 us  [permute(): done[name] = lax.ppermute(value, AXES, pairs)]
    ppermute x20, waiting for transfers between devices: 13 us -> 15 us  [permute(): done[name] = lax.ppermute(value, AXES, pairs)]
  transfers between devices with their start and end apart: 20 -> 20, of which waited for: 8 -> 10; matrix products, arithmetic and copies ran while one was open for 1% -> 1% of each run, Pallas kernels for 5% -> 5%
where the time goes in v4:
time: 50.8 us; the launch traced here: 50.6 us
  starting transfers between devices  24.4 us (48%)
  waiting for transfers between devices  15 us (30%)
  Pallas kernels  10.1 us (20%)
  between operations  0.76 us (1%)
    ppermute x20, starting transfers between devices, permute(): done[name] = lax.ppermute(value, AXES, pairs)  24.4 us
    ppermute x20, waiting for transfers between devices, permute(): done[name] = lax.ppermute(value, AXES, pairs)  15 us
    pallas_call x6, Pallas kernels, call(): pl.pallas_call(body, out_shape=shapes, in_specs=specs or [SMEM if item.dt...  10.1 us
  transfers between devices with their start and end apart: 20, of which 10 were waited for; matrix products, arithmetic and copies ran while one was open for 1% of the time, Pallas kernels for 5%

profile of v4, /device:TPU:0, one launch (start us, length us, event | category | flops | bytes accessed | tf_op | source)
XLA Modules:
  0.0 50.6 jit_solution(5586190734311264531)
XLA Ops:
  0.6 0.1 pad_add_fusion.order_ref
  0.7 1.9 %shard_map.50 = (f32[128,512]{1,0:T(8,128)S(1)}, f32[128,512]{1,0:T(8,128)S(1)}, f32[128,512]{1,0:T(8,128)S(1)}, f32[128,512]{1,0:T(8,128)S(1)}) custom-call(s32[4]{0:T(128)S(1)} %pad_add_fusion.order_ref, bf16[512,256]{1,0:T(8,128)(2,1)} %series_ref.1, bf16[256,512]{1,0:T(8,128)(2,1)} %reduction_ref.1), custom_call_target="tpu_custom_call" | custom-call | tf_op jit(solution)/shard_map/pallas_call | solution.py:33
  2.6 0.5 %collective-permute-start.2 = (f32[128,512]{1,0:T(8,128)S(1)}, f32[128,512]{1,0:T(8,128)S(1)}, u32[]{:S(2)}, u32[]{:S(2)}) collective-permute-start(f32[128,512]{1,0:T(8,128)S(1)} %get-tuple-element.16), channel_id=1, source_target_pairs={{0,8},{1,9},{2,10},{3,11},{4,12},{5,13},{6,14},{7,15},{8,0},{9,1},... | collective-permute-start | bytes 786440 | tf_op jit(solution)/shard_map/ppermute | solution.py:161
  3.1 0.1 collective-permute-start.1
  3.2 1.1 %collective-permute-done.2 = f32[128,512]{1,0:T(8,128)S(1)} collective-permute-done((f32[128,512]{1,0:T(8,128)S(1)}, f32[128,512]{1,0:T(8,128)S(1)}, u32[]{:S(2)}, u32[]{:S(2)}) %collective-permute-start.2) | collective-permute-done | bytes 262176 | tf_op jit(solution)/shard_map/ppermute | solution.py:161
  4.3 0.0 copy-start
  4.3 2.9 %collective-permute-start.3 = (bf16[128,512]{1,0:T(8,128)(2,1)S(1)}, bf16[128,512]{1,0:T(8,128)(2,1)S(1)}, u32[]{:S(2)}, u32[]{:S(2)}) collective-permute-start(bf16[128,512]{1,0:T(8,128)(2,1)S(1)} %add_convert_fusion.1), channel_id=1, source_target_pairs={{0,16},{1,17},{2,18},{3,19},{4,20},{5,21},{6,22},{7,23},{8,24},{9,... | collective-permute-start | bytes 393224 | tf_op jit(solution)/shard_map/ppermute | solution.py:161
  7.3 0.0 copy-done
  7.3 2.7 %collective-permute-start = (bf16[32,512]{1,0:T(8,128)(2,1)S(1)}, bf16[32,512]{1,0:T(8,128)(2,1)S(1)}, u32[]{:S(2)}, u32[]{:S(2)}) collective-permute-start(bf16[32,512]{1,0:T(8,128)(2,1)S(1)} %dynamic-slice_convert_fusion), channel_id=1, source_target_pairs={{0,4},{1,5},{2,6},{3,7},{4,0},{5,1},{6,2},{7,3},{8,12},{9,13},{10,... | collective-permute-start | bytes 98312 | tf_op jit(solution)/shard_map/ppermute | solution.py:161
  9.9 0.0 collective-permute-done.1
  9.9 1.1 %collective-permute-done.3 = bf16[128,512]{1,0:T(8,128)(2,1)S(1)} collective-permute-done((bf16[128,512]{1,0:T(8,128)(2,1)S(1)}, bf16[128,512]{1,0:T(8,128)(2,1)S(1)}, u32[]{:S(2)}, u32[]{:S(2)}) %collective-permute-start.3) | collective-permute-done | bytes 131104 | tf_op jit(solution)/shard_map/ppermute | solution.py:161
  11.1 0.1 add_convert_fusion.refs_1_.refs_3_.reduced_ref
  11.1 1.9 %collective-permute-start.4 = (bf16[128,512]{1,0:T(8,128)(2,1)S(1)}, bf16[128,512]{1,0:T(8,128)(2,1)S(1)}, u32[]{:S(2)}, u32[]{:S(2)}) collective-permute-start(bf16[128,512]{1,0:T(8,128)(2,1)S(1)} %add_convert_fusion.refs_1_.refs_3_.reduced_ref), channel_id=1, source_target_pairs={{0,2},{1,3},{2,0},{3,1},{4,6},{5,7},{6,4},{7,5},{8,10},{9,11},{10,... | collective-permute-start | bytes 393224 | tf_op jit(solution)/shard_map/ppermute | solution.py:161
  13.0 1.5 %collective-permute-start.9 = (bf16[128,512]{1,0:T(8,128)(2,1)S(1)}, bf16[128,512]{1,0:T(8,128)(2,1)S(1)}, u32[]{:S(2)}, u32[]{:S(2)}) collective-permute-start(bf16[128,512]{1,0:T(8,128)(2,1)S(1)} %add_convert_fusion.refs_1_.refs_3_.reduced_ref), channel_id=1, source_target_pairs={{0,16},{1,17},{2,18},{3,19},{4,20},{5,21},{6,22},{7,23},{8,9},{9,8... | collective-permute-start | bytes 393224 | tf_op jit(solution)/shard_map/ppermute | solution.py:161
  14.5 0.0 collective-permute-done
  14.5 2.5 %collective-permute-start.6 = (bf16[128,512]{1,0:T(8,128)(2,1)S(1)}, bf16[128,512]{1,0:T(8,128)(2,1)S(1)}, u32[]{:S(2)}, u32[]{:S(2)}) collective-permute-start(bf16[128,512]{1,0:T(8,128)(2,1)S(1)} %add_convert_fusion.refs_1_.refs_3_.reduced_ref), channel_id=1, source_target_pairs={{0,6},{1,7},{2,4},{3,5},{4,2},{5,3},{6,0},{7,1},{8,14},{9,15},{10,... | collective-permute-start | bytes 393224 | tf_op jit(solution)/shard_map/ppermute | solution.py:161
  17.1 0.0 collective-permute-done.4.refs_7_.refs_9_
  17.1 0.9 %collective-permute-start.5 = (bf16[64,512]{1,0:T(8,128)(2,1)S(1)}, bf16[64,512]{1,0:T(8,128)(2,1)S(1)}, u32[]{:S(2)}, u32[]{:S(2)}) collective-permute-start(bf16[64,512]{1,0:T(8,128)(2,1)S(1)} %pad_maximum_fusion.6), channel_id=1, source_target_pairs={{0,2},{1,3},{2,0},{3,1},{4,6},{5,7},{6,4},{7,5},{8,10},{9,11},{10,... | collective-permute-start | bytes 196616 | tf_op jit(solution)/shard_map/ppermute | solution.py:161
  18.0 0.0 collective-permute-done.9.refs_2_.refs_4_
  18.0 2.2 %collective-permute-start.10 = (bf16[2,128,512]{2,1,0:T(8,128)(2,1)S(1)}, bf16[2,128,512]{2,1,0:T(8,128)(2,1)S(1)}, u32[]{:S(2)}, u32[]{:S(2)}) collective-permute-start(bf16[2,128,512]{2,1,0:T(8,128)(2,1)S(1)} %pad_maximum_fusion.1), channel_id=1, source_target_pairs={{0,1},{1,0},{2,3},{3,2},{4,5},{5,4},{6,7},{7,6},{8,24},{9,25},{10,... | collective-permute-start | bytes 786440 | tf_op jit(solution)/shard_map/ppermute | solution.py:161
  20.2 1.5 %collective-permute-start.11 = (bf16[128,512]{1,0:T(8,128)(2,1)S(1)}, bf16[128,512]{1,0:T(8,128)(2,1)S(1)}, u32[]{:S(2)}, u32[]{:S(2)}) collective-permute-start(bf16[128,512]{1,0:T(8,128)(2,1)S(1)} %collective-permute-done.4.refs_7_.refs_9_), channel_id=1, source_target_pairs={{0,16},{1,17},{2,18},{3,19},{4,20},{5,21},{6,22},{7,23},{8,9},{9,8... | collective-permute-start | bytes 393224 | tf_op jit(solution)/shard_map/ppermute | solution.py:161
  21.7 3.5 %collective-permute-start.8 = (bf16[128,512]{1,0:T(8,128)(2,1)S(1)}, bf16[128,512]{1,0:T(8,128)(2,1)S(1)}, u32[]{:S(2)}, u32[]{:S(2)}) collective-permute-start(bf16[128,512]{1,0:T(8,128)(2,1)S(1)} %add_convert_fusion.refs_1_.refs_3_.reduced_ref), channel_id=1, source_target_pairs={{0,4},{1,5},{2,6},{3,7},{4,0},{5,1},{6,2},{7,3},{8,12},{9,13},{10,... | collective-permute-start | bytes 393224 | tf_op jit(solution)/shard_map/ppermute | solution.py:161
  25.2 0.0 collective-permute-done.6.refs_4_.refs_6_
  25.2 0.5 %collective-permute-start.14 = (bf16[128,512]{1,0:T(8,128)(2,1)S(1)}, bf16[128,512]{1,0:T(8,128)(2,1)S(1)}, u32[]{:S(2)}, u32[]{:S(2)}) collective-permute-start(bf16[128,512]{1,0:T(8,128)(2,1)S(1)} %collective-permute-done.6.refs_4_.refs_6_), channel_id=1, source_target_pairs={{0,16},{1,17},{2,18},{3,19},{4,20},{5,21},{6,22},{7,23},{8,9},{9,8... | collective-permute-start | bytes 393224 | tf_op jit(solution)/shard_map/ppermute | solution.py:161
  25.7 0.0 collective-permute-done.5
  25.8 0.1 collective-permute-start.7
  25.9 0.0 collective-permute-done.11.refs_8_.refs_10_
  25.9 2.0 %collective-permute-start.16 = (bf16[2,128,512]{2,1,0:T(8,128)(2,1)S(1)}, bf16[2,128,512]{2,1,0:T(8,128)(2,1)S(1)}, u32[]{:S(2)}, u32[]{:S(2)}) collective-permute-start(bf16[2,128,512]{2,1,0:T(8,128)(2,1)S(1)} %pad_maximum_fusion.3), channel_id=1, source_target_pairs={{0,1},{1,0},{2,3},{3,2},{4,5},{5,4},{6,7},{7,6},{8,24},{9,25},{10,... | collective-permute-start | bytes 786440 | tf_op jit(solution)/shard_map/ppermute | solution.py:161
  27.9 1.4 %collective-permute-done.8.refs_2_.refs_12_ = bf16[128,512]{1,0:T(8,128)(2,1)S(1)} collective-permute-done((bf16[128,512]{1,0:T(8,128)(2,1)S(1)}, bf16[128,512]{1,0:T(8,128)(2,1)S(1)}, u32[]{:S(2)}, u32[]{:S(2)}) %collective-permute-start.8) | collective-permute-done | bytes 131104 | tf_op jit(solution)/shard_map/ppermute | solution.py:161
  29.4 0.0 collective-permute-done.10.refs_3_.refs_5_
  29.4 0.5 %collective-permute-start.12 = (bf16[128,512]{1,0:T(8,128)(2,1)S(1)}, bf16[128,512]{1,0:T(8,128)(2,1)S(1)}, u32[]{:S(2)}, u32[]{:S(2)}) collective-permute-start(bf16[128,512]{1,0:T(8,128)(2,1)S(1)} %collective-permute-done.8.refs_2_.refs_12_), channel_id=1, source_target_pairs={{0,16},{1,17},{2,18},{3,19},{4,20},{5,21},{6,22},{7,23},{8,9},{9,8... | collective-permute-start | bytes 393224 | tf_op jit(solution)/shard_map/ppermute | solution.py:161
  29.9 1.7 %collective-permute-done.14.refs_5_.refs_7_ = bf16[128,512]{1,0:T(8,128)(2,1)S(1)} collective-permute-done((bf16[128,512]{1,0:T(8,128)(2,1)S(1)}, bf16[128,512]{1,0:T(8,128)(2,1)S(1)}, u32[]{:S(2)}, u32[]{:S(2)}) %collective-permute-start.14) | collective-permute-done | bytes 131104 | tf_op jit(solution)/shard_map/ppermute | solution.py:161
  31.6 0.1 collective-permute-start.15
  31.7 0.0 collective-permute-done.7
  31.7 2.6 %collective-permute-done.12.refs_3_.refs_13_ = bf16[128,512]{1,0:T(8,128)(2,1)S(1)} collective-permute-done((bf16[128,512]{1,0:T(8,128)(2,1)S(1)}, bf16[128,512]{1,0:T(8,128)(2,1)S(1)}, u32[]{:S(2)}, u32[]{:S(2)}) %collective-permute-start.12) | collective-permute-done | bytes 131104 | tf_op jit(solution)/shard_map/ppermute | solution.py:161
  34.4 0.0 collective-permute-start.13
  34.4 0.0 collective-permute-done.16.refs_9_.refs_11_
  34.4 0.6 %collective-permute-start.17 = (bf16[2,128,512]{2,1,0:T(8,128)(2,1)S(1)}, bf16[2,128,512]{2,1,0:T(8,128)(2,1)S(1)}, u32[]{:S(2)}, u32[]{:S(2)}) collective-permute-start(bf16[2,128,512]{2,1,0:T(8,128)(2,1)S(1)} %pad_maximum_fusion.4), channel_id=1, source_target_pairs={{0,1},{1,0},{2,3},{3,2},{4,5},{5,4},{6,7},{7,6},{8,24},{9,25},{10,... | collective-permute-start | bytes 786440 | tf_op jit(solution)/shard_map/ppermute | solution.py:161
  35.0 0.1 stack.118.places_ref
  35.1 0.8 %collective-permute-done.13.other_ref = bf16[256,512]{1,0:T(8,128)(2,1)S(1)} collective-permute-done((bf16[256,512]{1,0:T(8,128)(2,1)S(1)}, bf16[256,512]{1,0:T(8,128)(2,1)S(1)}, u32[]{:S(2)}, u32[]{:S(2)}) %collective-permute-start.13) | collective-permute-done | bytes 262176 | tf_op jit(solution)/shard_map/ppermute | solution.py:161
  35.9 0.6 %shard_map.51.refs_0_.refs_2_ = bf16[512,512]{1,0:T(8,128)(2,1)S(1)} custom-call(s32[16]{0:T(128)S(1)} %stack.118.places_ref, bf16[256,512]{1,0:T(8,128)(2,1)S(1)} %pad_maximum_fusion.mine_ref, bf16[256,512]{1,0:T(8,128)(2,1)S(1)} %collective-permute-done.13.other_ref), custom_call_target="tpu_custom_call" | custom-call | tf_op jit(solution)/shard_map/pallas_call | solution.py:33
  36.5 1.6 %collective-permute-done.15.refs_6_.refs_8_ = bf16[2,128,512]{2,1,0:T(8,128)(2,1)S(1)} collective-permute-done((bf16[2,128,512]{2,1,0:T(8,128)(2,1)S(1)}, bf16[2,128,512]{2,1,0:T(8,128)(2,1)S(1)}, u32[]{:S(2)}, u32[]{:S(2)}) %collective-permute-start.15) | collective-permute-done | bytes 262176 | tf_op jit(solution)/shard_map/ppermute | solution.py:161
  38.0 1.8 %shard_map.52.refs_1_ = f32[512,512]{1,0:T(8,128)S(1)} custom-call(s32[1]{0:T(128)} %bitcast.1.core_ref, bf16[512,512]{1,0:T(8,128)(2,1)S(1)} %shard_map.51.refs_0_.refs_2_, bf16[128,512]{1,0:T(8,128)(2,1)S(1)} %add_convert_fusion.refs_1_.refs_3_.reduced_ref, bf16[128,512]{1,0:T(8,128)(2,1)S(1)} %collective-permute-done.9.refs_2_.refs_4_, ...), custom_call_target="tpu_custom_call" | custom-call | tf_op jit(solution)/shard_map/pallas_call | solution.py:33
  39.9 1.0 %collective-permute-done.17.refs_4_.refs_14_ = bf16[2,128,512]{2,1,0:T(8,128)(2,1)S(1)} collective-permute-done((bf16[2,128,512]{2,1,0:T(8,128)(2,1)S(1)}, bf16[2,128,512]{2,1,0:T(8,128)(2,1)S(1)}, u32[]{:S(2)}, u32[]{:S(2)}) %collective-permute-start.17) | collective-permute-done | bytes 262176 | tf_op jit(solution)/shard_map/ppermute | solution.py:161
  40.9 0.9 %shard_map.53.refs_0_ = bf16[512,512]{1,0:T(8,128)(2,1)S(1)} custom-call(s32[1]{0:T(128)} %bitcast.1.core_ref, bf16[512,512]{1,0:T(8,128)(2,1)S(1)} %shard_map.51.refs_0_.refs_2_, f32[512,512]{1,0:T(8,128)S(1)} %shard_map.52.refs_1_, bf16[128,512]{1,0:T(8,128)(2,1)S(1)} %collective-permute-done.8.refs_2_.refs_12_, ...), custom_call_target="tpu_custom_call" | custom-call | tf_op jit(solution)/shard_map/pallas_call | solution.py:33
  41.7 0.1 collective-permute-start.18
  41.8 1.9 %collective-permute-done.18.refs_1_ = bf16[512,512]{1,0:T(8,128)(2,1)S(1)} collective-permute-done((bf16[512,512]{1,0:T(8,128)(2,1)S(1)}, bf16[512,512]{1,0:T(8,128)(2,1)S(1)}, u32[]{:S(2)}, u32[]{:S(2)}) %collective-permute-start.18) | collective-permute-done | bytes 524320 | tf_op jit(solution)/shard_map/ppermute | solution.py:161
  43.7 3.2 %shard_map.54 = (f32[512,512]{1,0:T(8,128)S(1)}, bf16[512,512]{1,0:T(8,128)(2,1)S(1)}) custom-call(s32[1]{0:T(128)} %bitcast.1.core_ref, bf16[512,512]{1,0:T(8,128)(2,1)S(1)} %shard_map.53.refs_0_, bf16[512,512]{1,0:T(8,128)(2,1)S(1)} %collective-permute-done.18.refs_1_, bf16[512,512]{1,0:T(8,128)(2,1)S(1)} %shard_map.51.refs_0_.refs_2_, ...), custom_call_target="tpu_custom_call" | custom-call | tf_op jit(solution)/shard_map/pallas_call | solution.py:33
  46.9 0.2 collective-permute-start.19
  47.1 1.8 %collective-permute-done.19.other_ref = bf16[512,512]{1,0:T(8,128)(2,1)S(1)} collective-permute-done((bf16[512,512]{1,0:T(8,128)(2,1)S(1)}, bf16[512,512]{1,0:T(8,128)(2,1)S(1)}, u32[]{:S(2)}, u32[]{:S(2)}) %collective-permute-start.19) | collective-permute-done | bytes 524320 | tf_op jit(solution)/shard_map/ppermute | solution.py:161
  48.8 1.8 %shard_map.55 = (bf16[128,512]{1,0:T(8,128)(2,1)}, f32[64,512]{1,0:T(8,128)}) custom-call(s32[1]{0:T(128)} %bitcast.place_ref, bf16[512,512]{1,0:T(8,128)(2,1)S(1)} %get-tuple-element.22.own_ref, bf16[512,512]{1,0:T(8,128)(2,1)S(1)} %collective-permute-done.19.other_ref, f32[512,512]{1,0:T(8,128)S(1)} %get-tuple-element.23.weights_ref, ...), custom_call_target="tpu_custom_call" | custom-call | tf_op jit(solution)/shard_map/pallas_call | solution.py:33
  (9 shorter events, 0.2 us)
Async XLA Ops:
  2.6 1.7 %collective-permute-start.2 = (f32[128,512]{1,0:T(8,128)S(1)}, f32[128,512]{1,0:T(8,128)S(1)}, u32[]{:S(2)}, u32[]{:S(2)}) collective-permute-start(f32[128,512]{1,0:T(8,128)S(1)} %get-tuple-element.16), channel_id=1, source_target_pairs={{0,8},{1,9},{2,10},{3,11},{4,12},{5,13},{6,14},{7,15},{8,0},{9,1},... | collective-permute-start | bytes 786440 | tf_op jit(solution)/shard_map/ppermute | solution.py:161
  3.1 6.8 %collective-permute-start.1 = (f32[128,512]{1,0:T(8,128)S(1)}, f32[128,512]{1,0:T(8,128)S(1)}, u32[]{:S(2)}, u32[]{:S(2)}) collective-permute-start(f32[128,512]{1,0:T(8,128)S(1)} %get-tuple-element.14), channel_id=1, source_target_pairs={{0,8},{1,9},{2,10},{3,11},{4,12},{5,13},{6,14},{7,15},{8,0},{9,1},... | collective-permute-start | bytes 786440 | tf_op jit(solution)/shard_map/ppermute | solution.py:161
  4.3 3.0 %copy-start = (f32[64,512]{1,0:T(8,128)S(1)}, f32[64,512]{1,0:T(8,128)}, u32[]{:S(2)}) copy-start(f32[64,512]{1,0:T(8,128)} %start_ref.1) | copy-start | bytes 393220
  4.3 6.7 %collective-permute-start.3 = (bf16[128,512]{1,0:T(8,128)(2,1)S(1)}, bf16[128,512]{1,0:T(8,128)(2,1)S(1)}, u32[]{:S(2)}, u32[]{:S(2)}) collective-permute-start(bf16[128,512]{1,0:T(8,128)(2,1)S(1)} %add_convert_fusion.1), channel_id=1, source_target_pairs={{0,16},{1,17},{2,18},{3,19},{4,20},{5,21},{6,22},{7,23},{8,24},{9,... | collective-permute-start | bytes 393224 | tf_op jit(solution)/shard_map/ppermute | solution.py:161
  7.3 7.2 %collective-permute-start = (bf16[32,512]{1,0:T(8,128)(2,1)S(1)}, bf16[32,512]{1,0:T(8,128)(2,1)S(1)}, u32[]{:S(2)}, u32[]{:S(2)}) collective-permute-start(bf16[32,512]{1,0:T(8,128)(2,1)S(1)} %dynamic-slice_convert_fusion), channel_id=1, source_target_pairs={{0,4},{1,5},{2,6},{3,7},{4,0},{5,1},{6,2},{7,3},{8,12},{9,13},{10,... | collective-permute-start | bytes 98312 | tf_op jit(solution)/shard_map/ppermute | solution.py:161
  11.1 5.9 %collective-permute-start.4 = (bf16[128,512]{1,0:T(8,128)(2,1)S(1)}, bf16[128,512]{1,0:T(8,128)(2,1)S(1)}, u32[]{:S(2)}, u32[]{:S(2)}) collective-permute-start(bf16[128,512]{1,0:T(8,128)(2,1)S(1)} %add_convert_fusion.refs_1_.refs_3_.reduced_ref), channel_id=1, source_target_pairs={{0,2},{1,3},{2,0},{3,1},{4,6},{5,7},{6,4},{7,5},{8,10},{9,11},{10,... | collective-permute-start | bytes 393224 | tf_op jit(solution)/shard_map/ppermute | solution.py:161
  13.0 5.0 %collective-permute-start.9 = (bf16[128,512]{1,0:T(8,128)(2,1)S(1)}, bf16[128,512]{1,0:T(8,128)(2,1)S(1)}, u32[]{:S(2)}, u32[]{:S(2)}) collective-permute-start(bf16[128,512]{1,0:T(8,128)(2,1)S(1)} %add_convert_fusion.refs_1_.refs_3_.reduced_ref), channel_id=1, source_target_pairs={{0,16},{1,17},{2,18},{3,19},{4,20},{5,21},{6,22},{7,23},{8,9},{9,8... | collective-permute-start | bytes 393224 | tf_op jit(solution)/shard_map/ppermute | solution.py:161
  14.5 10.7 %collective-permute-start.6 = (bf16[128,512]{1,0:T(8,128)(2,1)S(1)}, bf16[128,512]{1,0:T(8,128)(2,1)S(1)}, u32[]{:S(2)}, u32[]{:S(2)}) collective-permute-start(bf16[128,512]{1,0:T(8,128)(2,1)S(1)} %add_convert_fusion.refs_1_.refs_3_.reduced_ref), channel_id=1, source_target_pairs={{0,6},{1,7},{2,4},{3,5},{4,2},{5,3},{6,0},{7,1},{8,14},{9,15},{10,... | collective-permute-start | bytes 393224 | tf_op jit(solution)/shard_map/ppermute | solution.py:161
  17.1 8.7 %collective-permute-start.5 = (bf16[64,512]{1,0:T(8,128)(2,1)S(1)}, bf16[64,512]{1,0:T(8,128)(2,1)S(1)}, u32[]{:S(2)}, u32[]{:S(2)}) collective-permute-start(bf16[64,512]{1,0:T(8,128)(2,1)S(1)} %pad_maximum_fusion.6), channel_id=1, source_target_pairs={{0,2},{1,3},{2,0},{3,1},{4,6},{5,7},{6,4},{7,5},{8,10},{9,11},{10,... | collective-permute-start | bytes 196616 | tf_op jit(solution)/shard_map/ppermute | solution.py:161
  18.0 11.4 %collective-permute-start.10 = (bf16[2,128,512]{2,1,0:T(8,128)(2,1)S(1)}, bf16[2,128,512]{2,1,0:T(8,128)(2,1)S(1)}, u32[]{:S(2)}, u32[]{:S(2)}) collective-permute-start(bf16[2,128,512]{2,1,0:T(8,128)(2,1)S(1)} %pad_maximum_fusion.1), channel_id=1, source_target_pairs={{0,1},{1,0},{2,3},{3,2},{4,5},{5,4},{6,7},{7,6},{8,24},{9,25},{10,... | collective-permute-start | bytes 786440 | tf_op jit(solution)/shard_map/ppermute | solution.py:161
  20.2 5.7 %collective-permute-start.11 = (bf16[128,512]{1,0:T(8,128)(2,1)S(1)}, bf16[128,512]{1,0:T(8,128)(2,1)S(1)}, u32[]{:S(2)}, u32[]{:S(2)}) collective-permute-start(bf16[128,512]{1,0:T(8,128)(2,1)S(1)} %collective-permute-done.4.refs_7_.refs_9_), channel_id=1, source_target_pairs={{0,16},{1,17},{2,18},{3,19},{4,20},{5,21},{6,22},{7,23},{8,9},{9,8... | collective-permute-start | bytes 393224 | tf_op jit(solution)/shard_map/ppermute | solution.py:161
  21.7 7.7 %collective-permute-start.8 = (bf16[128,512]{1,0:T(8,128)(2,1)S(1)}, bf16[128,512]{1,0:T(8,128)(2,1)S(1)}, u32[]{:S(2)}, u32[]{:S(2)}) collective-permute-start(bf16[128,512]{1,0:T(8,128)(2,1)S(1)} %add_convert_fusion.refs_1_.refs_3_.reduced_ref), channel_id=1, source_target_pairs={{0,4},{1,5},{2,6},{3,7},{4,0},{5,1},{6,2},{7,3},{8,12},{9,13},{10,... | collective-permute-start | bytes 393224 | tf_op jit(solution)/shard_map/ppermute | solution.py:161
  25.2 6.4 %collective-permute-start.14 = (bf16[128,512]{1,0:T(8,128)(2,1)S(1)}, bf16[128,512]{1,0:T(8,128)(2,1)S(1)}, u32[]{:S(2)}, u32[]{:S(2)}) collective-permute-start(bf16[128,512]{1,0:T(8,128)(2,1)S(1)} %collective-permute-done.6.refs_4_.refs_6_), channel_id=1, source_target_pairs={{0,16},{1,17},{2,18},{3,19},{4,20},{5,21},{6,22},{7,23},{8,9},{9,8... | collective-permute-start | bytes 393224 | tf_op jit(solution)/shard_map/ppermute | solution.py:161
  25.8 5.9 %collective-permute-start.7 = (bf16[128,512]{1,0:T(8,128)(2,1)S(1)}, bf16[128,512]{1,0:T(8,128)(2,1)S(1)}, u32[]{:S(2)}, u32[]{:S(2)}) collective-permute-start(bf16[128,512]{1,0:T(8,128)(2,1)S(1)} %pad_maximum_fusion.5), channel_id=1, source_target_pairs={{0,1},{1,0},{2,3},{3,2},{4,5},{5,4},{6,7},{7,6},{8,9},{9,8},{10,11... | collective-permute-start | bytes 393224 | tf_op jit(solution)/shard_map/ppermute | solution.py:161
  25.9 8.5 %collective-permute-start.16 = (bf16[2,128,512]{2,1,0:T(8,128)(2,1)S(1)}, bf16[2,128,512]{2,1,0:T(8,128)(2,1)S(1)}, u32[]{:S(2)}, u32[]{:S(2)}) collective-permute-start(bf16[2,128,512]{2,1,0:T(8,128)(2,1)S(1)} %pad_maximum_fusion.3), channel_id=1, source_target_pairs={{0,1},{1,0},{2,3},{3,2},{4,5},{5,4},{6,7},{7,6},{8,24},{9,25},{10,... | collective-permute-start | bytes 786440 | tf_op jit(solution)/shard_map/ppermute | solution.py:161
  29.4 5.0 %collective-permute-start.12 = (bf16[128,512]{1,0:T(8,128)(2,1)S(1)}, bf16[128,512]{1,0:T(8,128)(2,1)S(1)}, u32[]{:S(2)}, u32[]{:S(2)}) collective-permute-start(bf16[128,512]{1,0:T(8,128)(2,1)S(1)} %collective-permute-done.8.refs_2_.refs_12_), channel_id=1, source_target_pairs={{0,16},{1,17},{2,18},{3,19},{4,20},{5,21},{6,22},{7,23},{8,9},{9,8... | collective-permute-start | bytes 393224 | tf_op jit(solution)/shard_map/ppermute | solution.py:161
  31.6 6.4 %collective-permute-start.15 = (bf16[2,128,512]{2,1,0:T(8,128)(2,1)S(1)}, bf16[2,128,512]{2,1,0:T(8,128)(2,1)S(1)}, u32[]{:S(2)}, u32[]{:S(2)}) collective-permute-start(bf16[2,128,512]{2,1,0:T(8,128)(2,1)S(1)} %pad_maximum_fusion.2), channel_id=1, source_target_pairs={{0,1},{1,0},{2,3},{3,2},{4,5},{5,4},{6,7},{7,6},{8,24},{9,25},{10,... | collective-permute-start | bytes 786440 | tf_op jit(solution)/shard_map/ppermute | solution.py:161
  34.4 1.5 %collective-permute-start.13 = (bf16[256,512]{1,0:T(8,128)(2,1)S(1)}, bf16[256,512]{1,0:T(8,128)(2,1)S(1)}, u32[]{:S(2)}, u32[]{:S(2)}) collective-permute-start(bf16[256,512]{1,0:T(8,128)(2,1)S(1)} %pad_maximum_fusion.mine_ref), channel_id=1, source_target_pairs={{0,8},{1,9},{2,10},{3,11},{4,12},{5,13},{6,14},{7,15},{8,0},{9,1},... | collective-permute-start | bytes 786440 | tf_op jit(solution)/shard_map/ppermute | solution.py:161
  34.4 6.5 %collective-permute-start.17 = (bf16[2,128,512]{2,1,0:T(8,128)(2,1)S(1)}, bf16[2,128,512]{2,1,0:T(8,128)(2,1)S(1)}, u32[]{:S(2)}, u32[]{:S(2)}) collective-permute-start(bf16[2,128,512]{2,1,0:T(8,128)(2,1)S(1)} %pad_maximum_fusion.4), channel_id=1, source_target_pairs={{0,1},{1,0},{2,3},{3,2},{4,5},{5,4},{6,7},{7,6},{8,24},{9,25},{10,... | collective-permute-start | bytes 786440 | tf_op jit(solution)/shard_map/ppermute | solution.py:161
  41.7 2.0 %collective-permute-start.18 = (bf16[512,512]{1,0:T(8,128)(2,1)S(1)}, bf16[512,512]{1,0:T(8,128)(2,1)S(1)}, u32[]{:S(2)}, u32[]{:S(2)}) collective-permute-start(bf16[512,512]{1,0:T(8,128)(2,1)S(1)} %shard_map.53.refs_0_), channel_id=1, source_target_pairs={{0,8},{1,9},{2,10},{3,11},{4,12},{5,13},{6,14},{7,15},{8,0},{9,1},... | collective-permute-start | bytes 1572872 | tf_op jit(solution)/shard_map/ppermute | solution.py:161
  46.9 2.0 %collective-permute-start.19 = (bf16[512,512]{1,0:T(8,128)(2,1)S(1)}, bf16[512,512]{1,0:T(8,128)(2,1)S(1)}, u32[]{:S(2)}, u32[]{:S(2)}) collective-permute-start(bf16[512,512]{1,0:T(8,128)(2,1)S(1)} %get-tuple-element.22.own_ref), channel_id=1, source_target_pairs={{0,8},{1,9},{2,10},{3,11},{4,12},{5,13},{6,14},{7,15},{8,0},{9,1},... | collective-permute-start | bytes 1572872 | tf_op jit(solution)/shard_map/ppermute | solution.py:161

commit v5 on v4

--- a/solution.py
+++ b/solution.py
@@ -16,7 +16,7 @@
 ANY = pl.BlockSpec(memory_space=pl.ANY)
 
 ORDER = ("cf", "cn", "x", "w2", "p0", "z3", "z2", "z1", "w1", "q0", "wy", "p3", "p1", "q3", "q1", "p2", "wc", "q2")
-AFTER = {"w1": ("z1",), "wy": ("z3",), "p2": ("q0", "p1"), "wc": ("p2",), "q2": ("q1",)}
+AFTER = {"w1": ("z1",), "wy": ("z3",), "q3": ("z2",), "p2": ("q0", "p1"), "wc": ("p2",), "q2": ("q1",)}
 
 
 def after(value, *earlier):

time: 50.8 us -> 50.8 us (level)
  no operation moved by 1% of the time
where the time goes in v5:
time: 50.8 us; the launch traced here: 50.6 us
  starting transfers between devices  24.4 us (48%)
  waiting for transfers between devices  15 us (30%)
  Pallas kernels  10.1 us (20%)
  between operations  0.76 us (1%)
    ppermute x20, starting transfers between devices, permute(): done[name] = lax.ppermute(value, AXES, pairs)  24.4 us
    ppermute x20, waiting for transfers between devices, permute(): done[name] = lax.ppermute(value, AXES, pairs)  15 us
    pallas_call x6, Pallas kernels, call(): pl.pallas_call(body, out_shape=shapes, in_specs=specs or [SMEM if item.dt...  10.1 us
  transfers between devices with their start and end apart: 20, of which 10 were waited for; matrix products, arithmetic and copies ran while one was open for 1% of the time, Pallas kernels for 5%

profile of v5, /device:TPU:0, one launch (start us, length us, event | category | flops | bytes accessed | tf_op | source)
XLA Modules:
  0.0 50.6 jit_solution(5586190734311264531)
XLA Ops:
  0.6 0.1 pad_add_fusion.order_ref
  0.7 1.9 %shard_map.50 = (f32[128,512]{1,0:T(8,128)S(1)}, f32[128,512]{1,0:T(8,128)S(1)}, f32[128,512]{1,0:T(8,128)S(1)}, f32[128,512]{1,0:T(8,128)S(1)}) custom-call(s32[4]{0:T(128)S(1)} %pad_add_fusion.order_ref, bf16[512,256]{1,0:T(8,128)(2,1)} %series_ref.1, bf16[256,512]{1,0:T(8,128)(2,1)} %reduction_ref.1), custom_call_target="tpu_custom_call" | custom-call | tf_op jit(solution)/shard_map/pallas_call | solution.py:33
  2.6 0.5 %collective-permute-start.2 = (f32[128,512]{1,0:T(8,128)S(1)}, f32[128,512]{1,0:T(8,128)S(1)}, u32[]{:S(2)}, u32[]{:S(2)}) collective-permute-start(f32[128,512]{1,0:T(8,128)S(1)} %get-tuple-element.17), channel_id=1, source_target_pairs={{0,8},{1,9},{2,10},{3,11},{4,12},{5,13},{6,14},{7,15},{8,0},{9,1},... | collective-permute-start | bytes 786440 | tf_op jit(solution)/shard_map/ppermute | solution.py:161
  3.1 0.1 collective-permute-start.1
  3.2 1.1 %collective-permute-done.2 = f32[128,512]{1,0:T(8,128)S(1)} collective-permute-done((f32[128,512]{1,0:T(8,128)S(1)}, f32[128,512]{1,0:T(8,128)S(1)}, u32[]{:S(2)}, u32[]{:S(2)}) %collective-permute-start.2) | collective-permute-done | bytes 262176 | tf_op jit(solution)/shard_map/ppermute | solution.py:161
  4.3 0.0 copy-start
  4.3 2.9 %collective-permute-start.3 = (bf16[128,512]{1,0:T(8,128)(2,1)S(1)}, bf16[128,512]{1,0:T(8,128)(2,1)S(1)}, u32[]{:S(2)}, u32[]{:S(2)}) collective-permute-start(bf16[128,512]{1,0:T(8,128)(2,1)S(1)} %add_convert_fusion.1), channel_id=1, source_target_pairs={{0,16},{1,17},{2,18},{3,19},{4,20},{5,21},{6,22},{7,23},{8,24},{9,... | collective-permute-start | bytes 393224 | tf_op jit(solution)/shard_map/ppermute | solution.py:161
  7.3 0.0 copy-done
  7.3 2.7 %collective-permute-start = (bf16[32,512]{1,0:T(8,128)(2,1)S(1)}, bf16[32,512]{1,0:T(8,128)(2,1)S(1)}, u32[]{:S(2)}, u32[]{:S(2)}) collective-permute-start(bf16[32,512]{1,0:T(8,128)(2,1)S(1)} %dynamic-slice_convert_fusion), channel_id=1, source_target_pairs={{0,4},{1,5},{2,6},{3,7},{4,0},{5,1},{6,2},{7,3},{8,12},{9,13},{10,... | collective-permute-start | bytes 98312 | tf_op jit(solution)/shard_map/ppermute | solution.py:161
  9.9 0.0 collective-permute-done.1
  9.9 1.1 %collective-permute-done.3 = bf16[128,512]{1,0:T(8,128)(2,1)S(1)} collective-permute-done((bf16[128,512]{1,0:T(8,128)(2,1)S(1)}, bf16[128,512]{1,0:T(8,128)(2,1)S(1)}, u32[]{:S(2)}, u32[]{:S(2)}) %collective-permute-start.3) | collective-permute-done | bytes 131104 | tf_op jit(solution)/shard_map/ppermute | solution.py:161
  11.1 0.1 add_convert_fusion.refs_1_.refs_3_.reduced_ref
  11.1 1.9 %collective-permute-start.4 = (bf16[128,512]{1,0:T(8,128)(2,1)S(1)}, bf16[128,512]{1,0:T(8,128)(2,1)S(1)}, u32[]{:S(2)}, u32[]{:S(2)}) collective-permute-start(bf16[128,512]{1,0:T(8,128)(2,1)S(1)} %add_convert_fusion.refs_1_.refs_3_.reduced_ref), channel_id=1, source_target_pairs={{0,2},{1,3},{2,0},{3,1},{4,6},{5,7},{6,4},{7,5},{8,10},{9,11},{10,... | collective-permute-start | bytes 393224 | tf_op jit(solution)/shard_map/ppermute | solution.py:161
  13.0 1.5 %collective-permute-start.9 = (bf16[128,512]{1,0:T(8,128)(2,1)S(1)}, bf16[128,512]{1,0:T(8,128)(2,1)S(1)}, u32[]{:S(2)}, u32[]{:S(2)}) collective-permute-start(bf16[128,512]{1,0:T(8,128)(2,1)S(1)} %add_convert_fusion.refs_1_.refs_3_.reduced_ref), channel_id=1, source_target_pairs={{0,16},{1,17},{2,18},{3,19},{4,20},{5,21},{6,22},{7,23},{8,9},{9,8... | collective-permute-start | bytes 393224 | tf_op jit(solution)/shard_map/ppermute | solution.py:161
  14.5 0.0 collective-permute-done
  14.5 2.5 %collective-permute-start.6 = (bf16[128,512]{1,0:T(8,128)(2,1)S(1)}, bf16[128,512]{1,0:T(8,128)(2,1)S(1)}, u32[]{:S(2)}, u32[]{:S(2)}) collective-permute-start(bf16[128,512]{1,0:T(8,128)(2,1)S(1)} %add_convert_fusion.refs_1_.refs_3_.reduced_ref), channel_id=1, source_target_pairs={{0,6},{1,7},{2,4},{3,5},{4,2},{5,3},{6,0},{7,1},{8,14},{9,15},{10,... | collective-permute-start | bytes 393224 | tf_op jit(solution)/shard_map/ppermute | solution.py:161
  17.1 0.0 collective-permute-done.4.refs_7_.refs_9_
  17.1 0.9 %collective-permute-start.5 = (bf16[64,512]{1,0:T(8,128)(2,1)S(1)}, bf16[64,512]{1,0:T(8,128)(2,1)S(1)}, u32[]{:S(2)}, u32[]{:S(2)}) collective-permute-start(bf16[64,512]{1,0:T(8,128)(2,1)S(1)} %pad_maximum_fusion.6), channel_id=1, source_target_pairs={{0,2},{1,3},{2,0},{3,1},{4,6},{5,7},{6,4},{7,5},{8,10},{9,11},{10,... | collective-permute-start | bytes 196616 | tf_op jit(solution)/shard_map/ppermute | solution.py:161
  18.0 0.0 collective-permute-done.9.refs_2_.refs_4_
  18.0 2.2 %collective-permute-start.10 = (bf16[2,128,512]{2,1,0:T(8,128)(2,1)S(1)}, bf16[2,128,512]{2,1,0:T(8,128)(2,1)S(1)}, u32[]{:S(2)}, u32[]{:S(2)}) collective-permute-start(bf16[2,128,512]{2,1,0:T(8,128)(2,1)S(1)} %pad_maximum_fusion.1), channel_id=1, source_target_pairs={{0,1},{1,0},{2,3},{3,2},{4,5},{5,4},{6,7},{7,6},{8,24},{9,25},{10,... | collective-permute-start | bytes 786440 | tf_op jit(solution)/shard_map/ppermute | solution.py:161
  20.2 1.5 %collective-permute-start.11 = (bf16[128,512]{1,0:T(8,128)(2,1)S(1)}, bf16[128,512]{1,0:T(8,128)(2,1)S(1)}, u32[]{:S(2)}, u32[]{:S(2)}) collective-permute-start(bf16[128,512]{1,0:T(8,128)(2,1)S(1)} %collective-permute-done.4.refs_7_.refs_9_), channel_id=1, source_target_pairs={{0,16},{1,17},{2,18},{3,19},{4,20},{5,21},{6,22},{7,23},{8,9},{9,8... | collective-permute-start | bytes 393224 | tf_op jit(solution)/shard_map/ppermute | solution.py:161
  21.7 3.5 %collective-permute-start.8 = (bf16[128,512]{1,0:T(8,128)(2,1)S(1)}, bf16[128,512]{1,0:T(8,128)(2,1)S(1)}, u32[]{:S(2)}, u32[]{:S(2)}) collective-permute-start(bf16[128,512]{1,0:T(8,128)(2,1)S(1)} %add_convert_fusion.refs_1_.refs_3_.reduced_ref), channel_id=1, source_target_pairs={{0,4},{1,5},{2,6},{3,7},{4,0},{5,1},{6,2},{7,3},{8,12},{9,13},{10,... | collective-permute-start | bytes 393224 | tf_op jit(solution)/shard_map/ppermute | solution.py:161
  25.2 0.0 collective-permute-done.6.refs_4_.refs_6_
  25.2 0.5 %collective-permute-start.14 = (bf16[128,512]{1,0:T(8,128)(2,1)S(1)}, bf16[128,512]{1,0:T(8,128)(2,1)S(1)}, u32[]{:S(2)}, u32[]{:S(2)}) collective-permute-start(bf16[128,512]{1,0:T(8,128)(2,1)S(1)} %collective-permute-done.6.refs_4_.refs_6_), channel_id=1, source_target_pairs={{0,16},{1,17},{2,18},{3,19},{4,20},{5,21},{6,22},{7,23},{8,9},{9,8... | collective-permute-start | bytes 393224 | tf_op jit(solution)/shard_map/ppermute | solution.py:161
  25.7 0.0 collective-permute-done.5
  25.8 0.1 collective-permute-start.7
  25.9 0.0 collective-permute-done.11.refs_8_.refs_10_
  25.9 2.0 %collective-permute-start.16 = (bf16[2,128,512]{2,1,0:T(8,128)(2,1)S(1)}, bf16[2,128,512]{2,1,0:T(8,128)(2,1)S(1)}, u32[]{:S(2)}, u32[]{:S(2)}) collective-permute-start(bf16[2,128,512]{2,1,0:T(8,128)(2,1)S(1)} %pad_maximum_fusion.3), channel_id=1, source_target_pairs={{0,1},{1,0},{2,3},{3,2},{4,5},{5,4},{6,7},{7,6},{8,24},{9,25},{10,... | collective-permute-start | bytes 786440 | tf_op jit(solution)/shard_map/ppermute | solution.py:161
  27.9 1.4 %collective-permute-done.8.refs_2_.refs_12_ = bf16[128,512]{1,0:T(8,128)(2,1)S(1)} collective-permute-done((bf16[128,512]{1,0:T(8,128)(2,1)S(1)}, bf16[128,512]{1,0:T(8,128)(2,1)S(1)}, u32[]{:S(2)}, u32[]{:S(2)}) %collective-permute-start.8) | collective-permute-done | bytes 131104 | tf_op jit(solution)/shard_map/ppermute | solution.py:161
  29.4 0.0 collective-permute-done.10.refs_3_.refs_5_
  29.4 0.5 %collective-permute-start.12 = (bf16[128,512]{1,0:T(8,128)(2,1)S(1)}, bf16[128,512]{1,0:T(8,128)(2,1)S(1)}, u32[]{:S(2)}, u32[]{:S(2)}) collective-permute-start(bf16[128,512]{1,0:T(8,128)(2,1)S(1)} %collective-permute-done.8.refs_2_.refs_12_), channel_id=1, source_target_pairs={{0,16},{1,17},{2,18},{3,19},{4,20},{5,21},{6,22},{7,23},{8,9},{9,8... | collective-permute-start | bytes 393224 | tf_op jit(solution)/shard_map/ppermute | solution.py:161
  29.9 1.7 %collective-permute-done.14.refs_5_.refs_7_ = bf16[128,512]{1,0:T(8,128)(2,1)S(1)} collective-permute-done((bf16[128,512]{1,0:T(8,128)(2,1)S(1)}, bf16[128,512]{1,0:T(8,128)(2,1)S(1)}, u32[]{:S(2)}, u32[]{:S(2)}) %collective-permute-start.14) | collective-permute-done | bytes 131104 | tf_op jit(solution)/shard_map/ppermute | solution.py:161
  31.6 0.1 collective-permute-start.15
  31.7 0.0 collective-permute-done.7
  31.7 2.6 %collective-permute-done.12.refs_3_.refs_13_ = bf16[128,512]{1,0:T(8,128)(2,1)S(1)} collective-permute-done((bf16[128,512]{1,0:T(8,128)(2,1)S(1)}, bf16[128,512]{1,0:T(8,128)(2,1)S(1)}, u32[]{:S(2)}, u32[]{:S(2)}) %collective-permute-start.12) | collective-permute-done | bytes 131104 | tf_op jit(solution)/shard_map/ppermute | solution.py:161
  34.4 0.0 collective-permute-start.13
  34.4 0.0 collective-permute-done.16.refs_9_.refs_11_
  34.4 0.6 %collective-permute-start.17 = (bf16[2,128,512]{2,1,0:T(8,128)(2,1)S(1)}, bf16[2,128,512]{2,1,0:T(8,128)(2,1)S(1)}, u32[]{:S(2)}, u32[]{:S(2)}) collective-permute-start(bf16[2,128,512]{2,1,0:T(8,128)(2,1)S(1)} %pad_maximum_fusion.4), channel_id=1, source_target_pairs={{0,1},{1,0},{2,3},{3,2},{4,5},{5,4},{6,7},{7,6},{8,24},{9,25},{10,... | collective-permute-start | bytes 786440 | tf_op jit(solution)/shard_map/ppermute | solution.py:161
  35.0 0.1 stack.118.places_ref
  35.1 0.8 %collective-permute-done.13.other_ref = bf16[256,512]{1,0:T(8,128)(2,1)S(1)} collective-permute-done((bf16[256,512]{1,0:T(8,128)(2,1)S(1)}, bf16[256,512]{1,0:T(8,128)(2,1)S(1)}, u32[]{:S(2)}, u32[]{:S(2)}) %collective-permute-start.13) | collective-permute-done | bytes 262176 | tf_op jit(solution)/shard_map/ppermute | solution.py:161
  35.9 0.6 %shard_map.51.refs_0_.refs_2_ = bf16[512,512]{1,0:T(8,128)(2,1)S(1)} custom-call(s32[16]{0:T(128)S(1)} %stack.118.places_ref, bf16[256,512]{1,0:T(8,128)(2,1)S(1)} %pad_maximum_fusion.mine_ref, bf16[256,512]{1,0:T(8,128)(2,1)S(1)} %collective-permute-done.13.other_ref), custom_call_target="tpu_custom_call" | custom-call | tf_op jit(solution)/shard_map/pallas_call | solution.py:33
  36.5 1.6 %collective-permute-done.15.refs_6_.refs_8_ = bf16[2,128,512]{2,1,0:T(8,128)(2,1)S(1)} collective-permute-done((bf16[2,128,512]{2,1,0:T(8,128)(2,1)S(1)}, bf16[2,128,512]{2,1,0:T(8,128)(2,1)S(1)}, u32[]{:S(2)}, u32[]{:S(2)}) %collective-permute-start.15) | collective-permute-done | bytes 262176 | tf_op jit(solution)/shard_map/ppermute | solution.py:161
  38.0 1.8 %shard_map.52.refs_1_ = f32[512,512]{1,0:T(8,128)S(1)} custom-call(s32[1]{0:T(128)} %bitcast.1.core_ref, bf16[512,512]{1,0:T(8,128)(2,1)S(1)} %shard_map.51.refs_0_.refs_2_, bf16[128,512]{1,0:T(8,128)(2,1)S(1)} %add_convert_fusion.refs_1_.refs_3_.reduced_ref, bf16[128,512]{1,0:T(8,128)(2,1)S(1)} %collective-permute-done.9.refs_2_.refs_4_, ...), custom_call_target="tpu_custom_call" | custom-call | tf_op jit(solution)/shard_map/pallas_call | solution.py:33
  39.9 1.0 %collective-permute-done.17.refs_4_.refs_14_ = bf16[2,128,512]{2,1,0:T(8,128)(2,1)S(1)} collective-permute-done((bf16[2,128,512]{2,1,0:T(8,128)(2,1)S(1)}, bf16[2,128,512]{2,1,0:T(8,128)(2,1)S(1)}, u32[]{:S(2)}, u32[]{:S(2)}) %collective-permute-start.17) | collective-permute-done | bytes 262176 | tf_op jit(solution)/shard_map/ppermute | solution.py:161
  40.9 0.9 %shard_map.53.refs_0_ = bf16[512,512]{1,0:T(8,128)(2,1)S(1)} custom-call(s32[1]{0:T(128)} %bitcast.1.core_ref, bf16[512,512]{1,0:T(8,128)(2,1)S(1)} %shard_map.51.refs_0_.refs_2_, f32[512,512]{1,0:T(8,128)S(1)} %shard_map.52.refs_1_, bf16[128,512]{1,0:T(8,128)(2,1)S(1)} %collective-permute-done.8.refs_2_.refs_12_, ...), custom_call_target="tpu_custom_call" | custom-call | tf_op jit(solution)/shard_map/pallas_call | solution.py:33
  41.7 0.1 collective-permute-start.18
  41.8 1.9 %collective-permute-done.18.refs_1_ = bf16[512,512]{1,0:T(8,128)(2,1)S(1)} collective-permute-done((bf16[512,512]{1,0:T(8,128)(2,1)S(1)}, bf16[512,512]{1,0:T(8,128)(2,1)S(1)}, u32[]{:S(2)}, u32[]{:S(2)}) %collective-permute-start.18) | collective-permute-done | bytes 524320 | tf_op jit(solution)/shard_map/ppermute | solution.py:161
  43.7 3.2 %shard_map.54 = (f32[512,512]{1,0:T(8,128)S(1)}, bf16[512,512]{1,0:T(8,128)(2,1)S(1)}) custom-call(s32[1]{0:T(128)} %bitcast.1.core_ref, bf16[512,512]{1,0:T(8,128)(2,1)S(1)} %shard_map.53.refs_0_, bf16[512,512]{1,0:T(8,128)(2,1)S(1)} %collective-permute-done.18.refs_1_, bf16[512,512]{1,0:T(8,128)(2,1)S(1)} %shard_map.51.refs_0_.refs_2_, ...), custom_call_target="tpu_custom_call" | custom-call | tf_op jit(solution)/shard_map/pallas_call | solution.py:33
  46.9 0.2 collective-permute-start.19
  47.1 1.8 %collective-permute-done.19.other_ref = bf16[512,512]{1,0:T(8,128)(2,1)S(1)} collective-permute-done((bf16[512,512]{1,0:T(8,128)(2,1)S(1)}, bf16[512,512]{1,0:T(8,128)(2,1)S(1)}, u32[]{:S(2)}, u32[]{:S(2)}) %collective-permute-start.19) | collective-permute-done | bytes 524320 | tf_op jit(solution)/shard_map/ppermute | solution.py:161
  48.8 1.8 %shard_map.55 = (bf16[128,512]{1,0:T(8,128)(2,1)}, f32[64,512]{1,0:T(8,128)}) custom-call(s32[1]{0:T(128)} %bitcast.place_ref, bf16[512,512]{1,0:T(8,128)(2,1)S(1)} %get-tuple-element.24.own_ref, bf16[512,512]{1,0:T(8,128)(2,1)S(1)} %collective-permute-done.19.other_ref, f32[512,512]{1,0:T(8,128)S(1)} %get-tuple-element.25.weights_ref, ...), custom_call_target="tpu_custom_call" | custom-call | tf_op jit(solution)/shard_map/pallas_call | solution.py:33
  (9 shorter events, 0.2 us)
Async XLA Ops:
  2.6 1.7 %collective-permute-start.2 = (f32[128,512]{1,0:T(8,128)S(1)}, f32[128,512]{1,0:T(8,128)S(1)}, u32[]{:S(2)}, u32[]{:S(2)}) collective-permute-start(f32[128,512]{1,0:T(8,128)S(1)} %get-tuple-element.17), channel_id=1, source_target_pairs={{0,8},{1,9},{2,10},{3,11},{4,12},{5,13},{6,14},{7,15},{8,0},{9,1},... | collective-permute-start | bytes 786440 | tf_op jit(solution)/shard_map/ppermute | solution.py:161
  3.1 6.8 %collective-permute-start.1 = (f32[128,512]{1,0:T(8,128)S(1)}, f32[128,512]{1,0:T(8,128)S(1)}, u32[]{:S(2)}, u32[]{:S(2)}) collective-permute-start(f32[128,512]{1,0:T(8,128)S(1)} %get-tuple-element.15), channel_id=1, source_target_pairs={{0,8},{1,9},{2,10},{3,11},{4,12},{5,13},{6,14},{7,15},{8,0},{9,1},... | collective-permute-start | bytes 786440 | tf_op jit(solution)/shard_map/ppermute | solution.py:161
  4.3 3.0 %copy-start = (f32[64,512]{1,0:T(8,128)S(1)}, f32[64,512]{1,0:T(8,128)}, u32[]{:S(2)}) copy-start(f32[64,512]{1,0:T(8,128)} %start_ref.1) | copy-start | bytes 393220
  4.3 6.7 %collective-permute-start.3 = (bf16[128,512]{1,0:T(8,128)(2,1)S(1)}, bf16[128,512]{1,0:T(8,128)(2,1)S(1)}, u32[]{:S(2)}, u32[]{:S(2)}) collective-permute-start(bf16[128,512]{1,0:T(8,128)(2,1)S(1)} %add_convert_fusion.1), channel_id=1, source_target_pairs={{0,16},{1,17},{2,18},{3,19},{4,20},{5,21},{6,22},{7,23},{8,24},{9,... | collective-permute-start | bytes 393224 | tf_op jit(solution)/shard_map/ppermute | solution.py:161
  7.3 7.2 %collective-permute-start = (bf16[32,512]{1,0:T(8,128)(2,1)S(1)}, bf16[32,512]{1,0:T(8,128)(2,1)S(1)}, u32[]{:S(2)}, u32[]{:S(2)}) collective-permute-start(bf16[32,512]{1,0:T(8,128)(2,1)S(1)} %dynamic-slice_convert_fusion), channel_id=1, source_target_pairs={{0,4},{1,5},{2,6},{3,7},{4,0},{5,1},{6,2},{7,3},{8,12},{9,13},{10,... | collective-permute-start | bytes 98312 | tf_op jit(solution)/shard_map/ppermute | solution.py:161
  11.1 5.9 %collective-permute-start.4 = (bf16[128,512]{1,0:T(8,128)(2,1)S(1)}, bf16[128,512]{1,0:T(8,128)(2,1)S(1)}, u32[]{:S(2)}, u32[]{:S(2)}) collective-permute-start(bf16[128,512]{1,0:T(8,128)(2,1)S(1)} %add_convert_fusion.refs_1_.refs_3_.reduced_ref), channel_id=1, source_target_pairs={{0,2},{1,3},{2,0},{3,1},{4,6},{5,7},{6,4},{7,5},{8,10},{9,11},{10,... | collective-permute-start | bytes 393224 | tf_op jit(solution)/shard_map/ppermute | solution.py:161
  13.0 5.0 %collective-permute-start.9 = (bf16[128,512]{1,0:T(8,128)(2,1)S(1)}, bf16[128,512]{1,0:T(8,128)(2,1)S(1)}, u32[]{:S(2)}, u32[]{:S(2)}) collective-permute-start(bf16[128,512]{1,0:T(8,128)(2,1)S(1)} %add_convert_fusion.refs_1_.refs_3_.reduced_ref), channel_id=1, source_target_pairs={{0,16},{1,17},{2,18},{3,19},{4,20},{5,21},{6,22},{7,23},{8,9},{9,8... | collective-permute-start | bytes 393224 | tf_op jit(solution)/shard_map/ppermute | solution.py:161
  14.5 10.7 %collective-permute-start.6 = (bf16[128,512]{1,0:T(8,128)(2,1)S(1)}, bf16[128,512]{1,0:T(8,128)(2,1)S(1)}, u32[]{:S(2)}, u32[]{:S(2)}) collective-permute-start(bf16[128,512]{1,0:T(8,128)(2,1)S(1)} %add_convert_fusion.refs_1_.refs_3_.reduced_ref), channel_id=1, source_target_pairs={{0,6},{1,7},{2,4},{3,5},{4,2},{5,3},{6,0},{7,1},{8,14},{9,15},{10,... | collective-permute-start | bytes 393224 | tf_op jit(solution)/shard_map/ppermute | solution.py:161
  17.1 8.7 %collective-permute-start.5 = (bf16[64,512]{1,0:T(8,128)(2,1)S(1)}, bf16[64,512]{1,0:T(8,128)(2,1)S(1)}, u32[]{:S(2)}, u32[]{:S(2)}) collective-permute-start(bf16[64,512]{1,0:T(8,128)(2,1)S(1)} %pad_maximum_fusion.6), channel_id=1, source_target_pairs={{0,2},{1,3},{2,0},{3,1},{4,6},{5,7},{6,4},{7,5},{8,10},{9,11},{10,... | collective-permute-start | bytes 196616 | tf_op jit(solution)/shard_map/ppermute | solution.py:161
  18.0 11.4 %collective-permute-start.10 = (bf16[2,128,512]{2,1,0:T(8,128)(2,1)S(1)}, bf16[2,128,512]{2,1,0:T(8,128)(2,1)S(1)}, u32[]{:S(2)}, u32[]{:S(2)}) collective-permute-start(bf16[2,128,512]{2,1,0:T(8,128)(2,1)S(1)} %pad_maximum_fusion.1), channel_id=1, source_target_pairs={{0,1},{1,0},{2,3},{3,2},{4,5},{5,4},{6,7},{7,6},{8,24},{9,25},{10,... | collective-permute-start | bytes 786440 | tf_op jit(solution)/shard_map/ppermute | solution.py:161
  20.2 5.7 %collective-permute-start.11 = (bf16[128,512]{1,0:T(8,128)(2,1)S(1)}, bf16[128,512]{1,0:T(8,128)(2,1)S(1)}, u32[]{:S(2)}, u32[]{:S(2)}) collective-permute-start(bf16[128,512]{1,0:T(8,128)(2,1)S(1)} %collective-permute-done.4.refs_7_.refs_9_), channel_id=1, source_target_pairs={{0,16},{1,17},{2,18},{3,19},{4,20},{5,21},{6,22},{7,23},{8,9},{9,8... | collective-permute-start | bytes 393224 | tf_op jit(solution)/shard_map/ppermute | solution.py:161
  21.7 7.7 %collective-permute-start.8 = (bf16[128,512]{1,0:T(8,128)(2,1)S(1)}, bf16[128,512]{1,0:T(8,128)(2,1)S(1)}, u32[]{:S(2)}, u32[]{:S(2)}) collective-permute-start(bf16[128,512]{1,0:T(8,128)(2,1)S(1)} %add_convert_fusion.refs_1_.refs_3_.reduced_ref), channel_id=1, source_target_pairs={{0,4},{1,5},{2,6},{3,7},{4,0},{5,1},{6,2},{7,3},{8,12},{9,13},{10,... | collective-permute-start | bytes 393224 | tf_op jit(solution)/shard_map/ppermute | solution.py:161
  25.2 6.4 %collective-permute-start.14 = (bf16[128,512]{1,0:T(8,128)(2,1)S(1)}, bf16[128,512]{1,0:T(8,128)(2,1)S(1)}, u32[]{:S(2)}, u32[]{:S(2)}) collective-permute-start(bf16[128,512]{1,0:T(8,128)(2,1)S(1)} %collective-permute-done.6.refs_4_.refs_6_), channel_id=1, source_target_pairs={{0,16},{1,17},{2,18},{3,19},{4,20},{5,21},{6,22},{7,23},{8,9},{9,8... | collective-permute-start | bytes 393224 | tf_op jit(solution)/shard_map/ppermute | solution.py:161
  25.8 5.9 %collective-permute-start.7 = (bf16[128,512]{1,0:T(8,128)(2,1)S(1)}, bf16[128,512]{1,0:T(8,128)(2,1)S(1)}, u32[]{:S(2)}, u32[]{:S(2)}) collective-permute-start(bf16[128,512]{1,0:T(8,128)(2,1)S(1)} %pad_maximum_fusion.5), channel_id=1, source_target_pairs={{0,1},{1,0},{2,3},{3,2},{4,5},{5,4},{6,7},{7,6},{8,9},{9,8},{10,11... | collective-permute-start | bytes 393224 | tf_op jit(solution)/shard_map/ppermute | solution.py:161
  25.9 8.5 %collective-permute-start.16 = (bf16[2,128,512]{2,1,0:T(8,128)(2,1)S(1)}, bf16[2,128,512]{2,1,0:T(8,128)(2,1)S(1)}, u32[]{:S(2)}, u32[]{:S(2)}) collective-permute-start(bf16[2,128,512]{2,1,0:T(8,128)(2,1)S(1)} %pad_maximum_fusion.3), channel_id=1, source_target_pairs={{0,1},{1,0},{2,3},{3,2},{4,5},{5,4},{6,7},{7,6},{8,24},{9,25},{10,... | collective-permute-start | bytes 786440 | tf_op jit(solution)/shard_map/ppermute | solution.py:161
  29.4 5.0 %collective-permute-start.12 = (bf16[128,512]{1,0:T(8,128)(2,1)S(1)}, bf16[128,512]{1,0:T(8,128)(2,1)S(1)}, u32[]{:S(2)}, u32[]{:S(2)}) collective-permute-start(bf16[128,512]{1,0:T(8,128)(2,1)S(1)} %collective-permute-done.8.refs_2_.refs_12_), channel_id=1, source_target_pairs={{0,16},{1,17},{2,18},{3,19},{4,20},{5,21},{6,22},{7,23},{8,9},{9,8... | collective-permute-start | bytes 393224 | tf_op jit(solution)/shard_map/ppermute | solution.py:161
  31.6 6.4 %collective-permute-start.15 = (bf16[2,128,512]{2,1,0:T(8,128)(2,1)S(1)}, bf16[2,128,512]{2,1,0:T(8,128)(2,1)S(1)}, u32[]{:S(2)}, u32[]{:S(2)}) collective-permute-start(bf16[2,128,512]{2,1,0:T(8,128)(2,1)S(1)} %pad_maximum_fusion.2), channel_id=1, source_target_pairs={{0,1},{1,0},{2,3},{3,2},{4,5},{5,4},{6,7},{7,6},{8,24},{9,25},{10,... | collective-permute-start | bytes 786440 | tf_op jit(solution)/shard_map/ppermute | solution.py:161
  34.4 1.5 %collective-permute-start.13 = (bf16[256,512]{1,0:T(8,128)(2,1)S(1)}, bf16[256,512]{1,0:T(8,128)(2,1)S(1)}, u32[]{:S(2)}, u32[]{:S(2)}) collective-permute-start(bf16[256,512]{1,0:T(8,128)(2,1)S(1)} %pad_maximum_fusion.mine_ref), channel_id=1, source_target_pairs={{0,8},{1,9},{2,10},{3,11},{4,12},{5,13},{6,14},{7,15},{8,0},{9,1},... | collective-permute-start | bytes 786440 | tf_op jit(solution)/shard_map/ppermute | solution.py:161
  34.4 6.5 %collective-permute-start.17 = (bf16[2,128,512]{2,1,0:T(8,128)(2,1)S(1)}, bf16[2,128,512]{2,1,0:T(8,128)(2,1)S(1)}, u32[]{:S(2)}, u32[]{:S(2)}) collective-permute-start(bf16[2,128,512]{2,1,0:T(8,128)(2,1)S(1)} %pad_maximum_fusion.4), channel_id=1, source_target_pairs={{0,1},{1,0},{2,3},{3,2},{4,5},{5,4},{6,7},{7,6},{8,24},{9,25},{10,... | collective-permute-start | bytes 786440 | tf_op jit(solution)/shard_map/ppermute | solution.py:161
  41.7 2.0 %collective-permute-start.18 = (bf16[512,512]{1,0:T(8,128)(2,1)S(1)}, bf16[512,512]{1,0:T(8,128)(2,1)S(1)}, u32[]{:S(2)}, u32[]{:S(2)}) collective-permute-start(bf16[512,512]{1,0:T(8,128)(2,1)S(1)} %shard_map.53.refs_0_), channel_id=1, source_target_pairs={{0,8},{1,9},{2,10},{3,11},{4,12},{5,13},{6,14},{7,15},{8,0},{9,1},... | collective-permute-start | bytes 1572872 | tf_op jit(solution)/shard_map/ppermute | solution.py:161
  46.9 2.0 %collective-permute-start.19 = (bf16[512,512]{1,0:T(8,128)(2,1)S(1)}, bf16[512,512]{1,0:T(8,128)(2,1)S(1)}, u32[]{:S(2)}, u32[]{:S(2)}) collective-permute-start(bf16[512,512]{1,0:T(8,128)(2,1)S(1)} %get-tuple-element.24.own_ref), channel_id=1, source_target_pairs={{0,8},{1,9},{2,10},{3,11},{4,12},{5,13},{6,14},{7,15},{8,0},{9,1},... | collective-permute-start | bytes 1572872 | tf_op jit(solution)/shard_map/ppermute | solution.py:161
